TPU v7x, 256 devices: a whole 4x4x8 slice. The times are simulated.
256 devices in a mesh: attn: 32 (over z, y_lo, core), sect: 8 (over y_hi, x).
Axes of the slice: x: 4, y: 4 (y_hi: 2, y_lo: 2; y = y_hi * 2 + y_lo), z: 8, core: 2. Of those that a mesh axis runs over, the one named last changes fastest.
Arguments:
- queries: bfloat16 [512, 6144], P('attn', 'sect'), may hold values from -405 to 405
- stream: bfloat16 [512, 6144], P('attn', 'sect'), may hold values from -41 to 41
- kv_pool: bfloat16 [10240, 8, 16, 256], P('attn', 'sect'), may hold values from -6 to 6
- fresh_kv: bfloat16 [1024, 8, 16, 256], P('attn', 'sect'), may hold values from -6 to 6
- fresh_owner: int32 [1024, 1], P('attn'), may hold values from 0 to 31; in each aligned block of 32 rows (0 to 31, 32 to 63, ...) at most 4 rows name the same one
- page_table: int32 [512, 16], P('attn'), may hold values from 0 to 319
- lengths: int32 [32, 16], P('attn'), may hold values from 1 to 256, 2560 in all within a row
- norm_gain: bfloat16 [6144], P('sect'), may hold values from 0.25 to 1.75
- router: bfloat16 [6144, 4], P('sect'), may hold values from -0.078125 to 0.078125
- expert_ids: int32 [512, 2], P('attn'), may hold values from 0 to 3, all different within a row; in each aligned block of 16 rows (0 to 15, 16 to 31, ...) at most 10 rows name the same one
- w_gate: bfloat16 [6144, 32768], P(None, ('attn', 'sect')), may hold values from -0.078125 to 0.078125
- w_up: bfloat16 [6144, 32768], P(None, ('attn', 'sect')), may hold values from -0.078125 to 0.078125
- w_down: bfloat16 [32768, 6144], P(('attn', 'sect')), may hold values from -0.0625 to 0.0625
Outputs:
- mixed: bfloat16 [512, 6144], P('attn', 'sect')
- kv_out: bfloat16 [10240, 8, 16, 256], P('attn', 'sect')
Inputs may be any that keep to these rules, and one draw needn't show every extreme that they name: `fresh_owner`: within each aligned block of 32 pages no owner is named more than 4 times, a bound that some block reaches. Each row of lengths sums to 2560, and its largest entry is 256. `expert_ids`: the two experts of a row differ. Within each aligned block of 16 rows no expert is named more than 10 times, a bound that some block reaches.
All inputs are finite; a program needn't handle non-finite values.
Results may differ from a plain program's by a relative error of at most 0.0052.
Values may be sent and summed in bfloat16 or wider, within the bound.
No kernel may reach another device: no remote copies, remote signals or barrier semaphores. Data moves between devices by JAX's collectives and lax.ppermute only.
A program may use at most 128 MiB of HBM per device.

v0:
```python
import jax
import jax.numpy as jnp
from jax import lax
from jax.sharding import PartitionSpec as P

EXPERTS = 4
PAGES_ROW = 16
CAPP = 4
OLD_PAGES = 192
CAP = 10


def on_device(
    queries,
    stream,
    kv_pool,
    fresh_kv,
    fresh_owner,
    page_table,
    lengths,
    norm_gain,
    router,
    expert_ids,
    w_gate,
    w_up,
    w_down,
):
    n_attn = lax.axis_size("attn")
    n_sect = lax.axis_size("sect")
    rows = stream.shape[0]
    width_local = stream.shape[1]
    width = width_local * n_sect
    kv_local = kv_pool.shape[1]
    page_len = kv_pool.shape[2]
    head_dim = kv_pool.shape[3] // 2
    group_heads = queries.shape[1] // head_dim // kv_local
    new_pages = fresh_kv.shape[0]
    page_shape = fresh_kv.shape[1:]
    owners = fresh_owner[:, 0]
    owner_hot = (owners[:, None] == jnp.arange(n_attn, dtype=jnp.int32)[None, :]).astype(jnp.int32)
    earlier = jnp.cumsum(owner_hot, axis=0) - owner_hot
    place = jnp.sum(earlier * owner_hot, axis=1)
    target = owners * CAPP + place
    select = (target[None, :] == jnp.arange(n_attn * CAPP, dtype=jnp.int32)[:, None]).astype(
        jnp.bfloat16
    )
    outgoing = jnp.dot(select, fresh_kv.reshape(new_pages, -1), preferred_element_type=jnp.float32)
    outgoing = outgoing.astype(jnp.bfloat16).reshape((n_attn, CAPP) + page_shape)
    arrived = lax.all_to_all(outgoing, "attn", split_axis=0, concat_axis=0, tiled=True)
    pool = jnp.concatenate(
        [kv_pool[:OLD_PAGES], arrived.reshape((n_attn * CAPP,) + page_shape)], axis=0
    )
    fetched = pool[page_table]
    keys = fetched[..., :head_dim]
    values = fetched[..., head_dim:]
    grouped = queries.reshape(rows, kv_local, group_heads, head_dim)
    scores = jnp.einsum(
        "rkgd,rpksd->rkgps", grouped, keys, preferred_element_type=jnp.float32
    ) * float(head_dim) ** (-0.5)
    scores = scores.reshape(rows, kv_local, group_heads, -1)
    length_row = lengths.reshape(rows)
    valid = (jnp.arange(scores.shape[-1], dtype=jnp.int32)[None, :] < length_row[:, None])[
        :, None, None, :
    ]
    masked = jnp.where(valid, scores, -1e30)
    top = jnp.max(masked, axis=-1, keepdims=True)
    weights = jnp.where(valid, jnp.exp(masked - top), 0.0)
    total = jnp.sum(weights, axis=-1)
    rounded = weights.astype(jnp.bfloat16).reshape(rows, kv_local, group_heads, PAGES_ROW, page_len)
    summed = jnp.einsum("rkgps,rpksd->rkgd", rounded, values, preferred_element_type=jnp.float32)
    attended = (summed / total[..., None]).reshape(rows, width_local)
    hidden = (stream.astype(jnp.float32) + attended).astype(jnp.bfloat16)
    hidden_f = hidden.astype(jnp.float32)
    squares = lax.psum(jnp.sum(hidden_f * hidden_f, axis=1), "sect")
    inverse = lax.rsqrt(squares / width + 1e-05)
    normed = (hidden_f * inverse[:, None] * norm_gain.astype(jnp.float32)[None, :]).astype(
        jnp.bfloat16
    )
    logits = lax.psum(jnp.dot(normed, router, preferred_element_type=jnp.float32), "sect")
    chosen = expert_ids[:, :, None] == jnp.arange(EXPERTS, dtype=jnp.int32)[None, None, :]
    picked = jnp.sum(jnp.where(chosen, logits[:, None, :], 0.0), axis=2)
    first = jax.nn.sigmoid(picked[:, 0] - picked[:, 1])
    second = jax.nn.sigmoid(picked[:, 1] - picked[:, 0])
    gate_by_expert = jnp.sum(
        jnp.where(chosen, jnp.stack([first, second], axis=1)[:, :, None], 0.0), axis=1
    )
    routed = jnp.sum(chosen.astype(jnp.int32), axis=1)
    slot = jnp.cumsum(routed, axis=0) - routed
    assign = (routed[:, :, None] == 1) & (
        slot[:, :, None] == jnp.arange(CAP, dtype=jnp.int32)[None, None, :]
    )
    dispatch_mat = assign.reshape(rows, EXPERTS * CAP).T.astype(jnp.bfloat16)
    combine_mat = jnp.where(assign, gate_by_expert[:, :, None], 0.0).reshape(rows, EXPERTS * CAP)
    source = lax.all_gather(normed, "sect", axis=1, tiled=True)
    packed = jnp.dot(dispatch_mat, source, preferred_element_type=jnp.float32).astype(jnp.bfloat16)
    packed = packed.reshape(EXPERTS, CAP, source.shape[1])
    outgoing_rows = jnp.repeat(packed, n_attn // EXPERTS, axis=0)
    received = lax.all_to_all(outgoing_rows, "attn", split_axis=0, concat_axis=0, tiled=True)
    count = received.shape[1]
    flat_rows = received.reshape(-1, width)
    gate_part = jnp.dot(flat_rows, w_gate, preferred_element_type=jnp.float32)
    up_part = jnp.dot(flat_rows, w_up, preferred_element_type=jnp.float32)
    active = (jax.nn.silu(gate_part) * up_part).astype(jnp.bfloat16)
    produced = jnp.dot(active, w_down, preferred_element_type=jnp.float32).reshape(
        n_attn, count, width
    )
    answer = lax.all_to_all(produced, "attn", split_axis=0, concat_axis=0, tiled=True)
    summed_group = jnp.sum(answer.reshape(EXPERTS, n_attn // EXPERTS, CAP, width), axis=1)
    per_expert = lax.psum_scatter(summed_group, "sect", scatter_dimension=2, tiled=True)
    blended = jnp.dot(
        combine_mat,
        per_expert.reshape(EXPERTS * CAP, width_local),
        precision=lax.Precision.HIGHEST,
        preferred_element_type=jnp.float32,
    )
    mixed = (hidden_f + blended).astype(jnp.bfloat16)
    return (mixed, pool)


def solution(mesh):
    return jax.shard_map(
        on_device,
        mesh=mesh,
        in_specs=(
            P("attn", "sect"),
            P("attn", "sect"),
            P("attn", "sect", None, None),
            P("attn", "sect", None, None),
            P("attn", None),
            P("attn", None),
            P("attn", None),
            P("sect"),
            P("sect", None),
            P("attn", None),
            P(None, ("attn", "sect")),
            P(None, ("attn", "sect")),
            P(("attn", "sect"), None),
        ),
        out_specs=(P("attn", "sect"), P("attn", "sect", None, None)),
        check_vma=False,
    )
```

profile of v0, /device:TPU:6, one launch (start us, length us, event | category | flops | bytes accessed | tf_op | source)
XLA Modules:
  0.0 666.1 jit_solution(18313220666818686993)
XLA Ops:
  7.2 0.0 copy-start
  7.2 0.8 fusion.28
  8.0 0.1 reduce_window_sum.22
  8.1 0.8 select_reduce_fusion
  8.9 0.7 multiply_add_fusion.1
  9.6 1.0 copy.37
  10.6 0.4 convolution_convert_fusion.1
  11.0 0.0 copy-start.5
  11.1 0.0 copy-start.7
  11.1 0.0 copy-start.6
  11.1 0.0 copy-start.3
  11.1 1.2 copy.38
  12.3 10.0 %all-to-all-start = ((bf16[32,4,1,16,256]{4,3,1,2,0:T(8,128)(2,1)}), bf16[32,4,1,16,256]{4,3,1,2,0:T(8,128)(2,1)}, u32[]{:S(2)}, u32[]{:S(2)}) async-start(bf16[32,4,1,16,256]{4,3,1,2,0:T(8,128)(2,1)} %bitcast.2), calls=%async_computation | async-start | bytes 2097152 | tf_op jit(solution)/shard_map/all_to_all | solution.py:49
  22.3 0.0 copy-start.8
  22.3 0.0 reduce-scatter.2.cloned.1.call-start
  22.4 0.0 copy-done.5
  22.4 0.1 copy.31
  22.5 0.1 copy.30
  22.6 0.1 eq.90
  22.7 0.0 copy-done.7
  22.7 0.1 and.13
  22.8 0.1 and.15
  22.9 0.0 copy-done.6
  22.9 0.1 reshape.156
  23.0 0.1 eq.85
  23.1 0.1 eq.88
  23.2 0.0 copy-done.3
  23.2 0.1 reshape.165
  23.2 1.5 slice.17
  24.8 0.0 copy-done.8
  24.8 0.1 broadcast_compare_fusion
  24.9 26.5 %all-to-all-done = bf16[32,4,1,16,256]{4,3,1,2,0:T(8,128)(2,1)} async-done(((bf16[32,4,1,16,256]{4,3,1,2,0:T(8,128)(2,1)}), bf16[32,4,1,16,256]{4,3,1,2,0:T(8,128)(2,1)}, u32[]{:S(2)}, u32[]{:S(2)}) %all-to-all-start) | async-done | bytes 1048608 | tf_op jit(solution)/shard_map/all_to_all | solution.py:49
  51.4 2.9 fusion.48
  54.3 3.8 gather_fusion
  58.2 4.0 fusion.35
  62.2 0.5 fusion.7
  62.7 0.0 copy-done.2
  62.7 0.7 fusion.6
  63.3 0.0 copy-done.4
  63.4 0.1 fusion.19
  63.5 18.7 %psum.14 = f32[16]{0:T(128)S(1)} all-reduce(f32[16]{0:T(128)S(1)} %get-tuple-element.2), channel_id=1, replica_groups=mesh['attn'=32,'sect'=8] {'sect'}, use_global_device_ids=true, to_apply=%region_7.8 | all-reduce | flops 16 | bytes 128 | tf_op jit(solution)/shard_map/psum | solution.py:74
  82.2 0.1 fusion.21
  82.3 34.6 %all_gather.3 = bf16[16,6144]{1,0:T(8,128)(2,1)S(1)} all-gather(bf16[16,768]{1,0:T(8,128)(2,1)S(1)} %fusion.21), channel_id=1, replica_groups=mesh['attn'=32,'sect'=8] {'sect'}, dimensions={1}, use_global_device_ids=true | all-gather | bytes 221184 | tf_op jit(solution)/shard_map/all_gather | solution.py:94
  116.8 1.1 convolution_convert_fusion
  117.9 2.1 reshape.147
  120.0 1.9 broadcast_in_dim.87
  121.9 145.3 %all_to_all.15 = bf16[32,10,6144]{2,1,0:T(8,128)(2,1)} all-to-all(bf16[32,10,6144]{2,1,0:T(8,128)(2,1)S(1)} %bitcast.63), channel_id=1, replica_groups=mesh['attn'=32,'sect'=8] {'attn'}, dimensions={0} | all-to-all | bytes 7864320 | tf_op jit(solution)/shard_map/all_to_all | solution.py:98
  267.2 7.6 %reshape.149 = bf16[320,6144]{1,0:T(8,128)(2,1)} reshape(bf16[32,10,6144]{2,1,0:T(8,128)(2,1)} %all_to_all.15) | data formatting | bytes 7864320 | tf_op jit(solution)/shard_map/reshape | solution.py:100
  274.8 3.8 fusion.37
  278.6 0.0 copy-done
  278.6 9.9 %fusion.3 = f32[320,6144]{1,0:T(8,128)} fusion(bf16[128,6144]{1,0:T(8,128)(2,1)S(1)} %copy-done, bf16[320,6144]{1,0:T(8,128)(2,1)} %reshape.149, bf16[6144,128]{1,0:T(8,128)(2,1)} %param.24, f32[320,128]{1,0:T(8,128)S(1)} %fusion.37), kind=kOutput, calls=%fused_computation.10 | convolution fusion | flops 1006878720 | bytes 15106048 | tf_op jit(solution)/shard_map/dot_general | solution.py:104
  288.5 9.5 %reshape.150 = f32[32,10,6144]{2,1,0:T(8,128)} reshape(f32[320,6144]{1,0:T(8,128)} %fusion.3) | data formatting | bytes 15728640 | tf_op jit(solution)/shard_map/reshape | solution.py:104
  298.0 280.6 %all_to_all.16 = f32[32,10,6144]{2,1,0:T(8,128)S(1)} all-to-all(f32[32,10,6144]{2,1,0:T(8,128)} %reshape.150), channel_id=1, replica_groups=mesh['attn'=32,'sect'=8] {'attn'}, dimensions={0} | all-to-all | bytes 15728640 | tf_op jit(solution)/shard_map/all_to_all | solution.py:107
  578.6 1.9 bitcast_reduce_fusion
  580.5 0.0 reduce-scatter.2.cloned.1.call-update
  580.6 0.1 fusion.36
  580.7 21.0 %psum.15 = f32[16,4]{0,1:T(4,128)S(1)} all-reduce(f32[16,4]{0,1:T(4,128)S(1)} %fusion.36), channel_id=1, replica_groups=mesh['attn'=32,'sect'=8] {'sect'}, use_global_device_ids=true, to_apply=%region_8.9 | all-reduce | flops 64 | bytes 512 | tf_op jit(solution)/shard_map/psum | solution.py:79
  601.8 0.0 copy-start.1
  601.8 0.1 copy.33
  601.9 3.1 pad_maximum_fusion
  605.0 0.1 fusion.27
  605.1 52.3 %reduce-scatter.2.cloned.1.call-done = f32[4,10,768]{2,1,0:T(8,128)} async-done(((f32[4,10,6144]{2,1,0:T(8,128)}), f32[4,10,768]{2,1,0:T(8,128)}) %reduce-scatter.2.cloned.1.call-update) | async-done | bytes 122896 | tf_op jit(solution)/shard_map/reduce_scatter | solution.py:109
  657.4 1.9 fusion.5
  659.3 0.0 copy-done.1
  (18 shorter events, 0.2 us)
Async XLA Ops:
  7.2 271.4 %copy-start = (bf16[128,6144]{1,0:T(8,128)(2,1)S(1)}, bf16[128,6144]{1,0:T(8,128)(2,1)}, u32[]{:S(2)}) copy-start(bf16[128,6144]{1,0:T(8,128)(2,1)} %param.25) | copy-start | bytes 4718596
  11.0 11.3 %copy-start.5 = (s32[16,2]{0,1:T(2,128)S(1)}, s32[16,2]{0,1:T(2,128)}, u32[]{:S(2)}) copy-start(s32[16,2]{0,1:T(2,128)} %param.22) | copy-start | bytes 388
  11.1 11.6 %copy-start.7 = (bf16[768]{0:T(1024)(128)(2,1)S(1)}, bf16[768]{0:T(1024)(128)(2,1)}, u32[]{:S(2)}) copy-start(bf16[768]{0:T(1024)(128)(2,1)} %param.20) | copy-start | bytes 4612
  11.1 11.9 %copy-start.6 = (s32[16,16]{1,0:T(8,128)S(1)}, s32[16,16]{1,0:T(8,128)}, u32[]{:S(2)}) copy-start(s32[16,16]{1,0:T(8,128)} %param.18) | copy-start | bytes 3076
  11.1 12.1 %copy-start.3 = (bf16[16,768]{1,0:T(8,128)(2,1)S(1)}, bf16[16,768]{1,0:T(8,128)(2,1)}, u32[]{:S(2)}) copy-start(bf16[16,768]{1,0:T(8,128)(2,1)} %param.13) | copy-start | bytes 73732
  12.3 39.1 %all-to-all-start = ((bf16[32,4,1,16,256]{4,3,1,2,0:T(8,128)(2,1)}), bf16[32,4,1,16,256]{4,3,1,2,0:T(8,128)(2,1)}, u32[]{:S(2)}, u32[]{:S(2)}) async-start(bf16[32,4,1,16,256]{4,3,1,2,0:T(8,128)(2,1)} %bitcast.2), calls=%async_computation | async-start | bytes 2097152 | tf_op jit(solution)/shard_map/all_to_all | solution.py:49
  22.3 2.5 copy-start.8
  22.3 635.0 %reduce-scatter.2.cloned.1.call-start = ((), (), s32[]{:S(2)}) async-start(), calls=%async_computation.4 | async-start | bytes 1769472 | tf_op jit(solution)/shard_map/reduce_scatter | solution.py:109
  58.2 4.5 copy-start.2
  62.2 1.2 copy-start.4
  578.6 2.0 copy-start.9
  601.8 57.5 %copy-start.1 = (bf16[128,6144]{1,0:T(8,128)(2,1)S(1)}, bf16[128,6144]{1,0:T(8,128)(2,1)}, u32[]{:S(2)}) copy-start(bf16[128,6144]{1,0:T(8,128)(2,1)} %param.25) | copy-start | bytes 4718596
Sparse Core Ops, SparseCore 0:
  580.7 76.6 reduce-scatter.1
where the time goes:
time: 667 us; the launch traced here: 666 us
  blocking collectives  500 us (75%)
  waiting for transfers between devices  78.8 us (12%)
  local copies, waits for them, and re-layouts  29.6 us (4%)
  matrix products  21.9 us (3%)
  between operations  14.2 us (2%)
  other arithmetic  11.4 us (2%)
  starting transfers between devices  10 us (1%)
    all_to_all x1, blocking collectives, on_device(): lax.all_to_all(produced, 'attn', split_axis=0, concat_axis=0, tiled=True)  281 us
    all_to_all x1, blocking collectives, on_device(): lax.all_to_all(outgoing_rows, 'attn', split_axis=0, concat_axis=0, tiled=...  145 us
    reduce_scatter x1, waiting for transfers between devices, on_device(): lax.psum_scatter(summed_group, 'sect', scatter_dimension=2, tiled=True)  52.3 us
    all_gather x1, blocking collectives, on_device(): source = lax.all_gather(normed, 'sect', axis=1, tiled=True)  34.6 us
    all_to_all x1, waiting for transfers between devices, on_device(): lax.all_to_all(outgoing, 'attn', split_axis=0, concat_axis=0, tiled=True)  26.5 us
    psum x1, blocking collectives, on_device(): lax.psum(jnp.dot(normed, router, preferred_element_type=jnp.float32), 'se...  21 us
    psum x1, blocking collectives, on_device(): squares = lax.psum(jnp.sum(hidden_f * hidden_f, axis=1), 'sect')  18.7 us
  transfers between devices with their start and end apart: 2, of which 2 were waited for; matrix products, arithmetic and copies ran while one was open for 1% of the time, Pallas kernels for 0%

commit v1 on v0

v1 whole, which is shorter than its diff:
```python
import functools

import jax
import jax.numpy as jnp
from jax import lax
from jax.experimental import pallas as pl
from jax.experimental.pallas import tpu as pltpu
from jax.sharding import PartitionSpec as P

F32 = jnp.float32
BF16 = jnp.bfloat16
EXPERTS = 4
CAPP = 4
OLD_PAGES = 192
CAP = 10
LANES = 128
SLAB = 64
SCALAR_ROW = 30
NZ = 8
ROWS = NZ * CAP
PIECES = 3
AXES = ("attn", "sect")
VMEM_BYTES = 56 * 1024 * 1024


def place(z, y, x, c):
    return (z * 4 + (y % 2) * 2 + c) * 8 + (y // 2) * 4 + x


def pairs(move):
    return [
        (place(z, y, x, c), place(*move(z, y, x, c)))
        for z in range(NZ)
        for y in range(4)
        for x in range(4)
        for c in range(2)
    ]


def along_x(step):
    return pairs(lambda z, y, x, c: (z, y, x ^ step, c))


def along_y(step):
    return pairs(lambda z, y, x, c: (z, y ^ step, x, c))


OTHER_CORE = pairs(lambda z, y, x, c: (z, y, x, c ^ 1))
Z_GROUPS = [[z * 4 + r for z in range(NZ)] for r in range(4)]


def permute(value, perm):
    return lax.ppermute(value, AXES, perm)


def gather4(value, along):
    return [value] + [permute(value, along(step)) for step in (1, 2, 3)]


def in_vmem(count):
    return [pl.BlockSpec(memory_space=pltpu.VMEM)] * count


def in_smem(count):
    return [pl.BlockSpec(memory_space=pltpu.SMEM)] * count


def params():
    return pltpu.CompilerParams(vmem_limit_bytes=VMEM_BYTES)


def iota(shape, dim):
    return lax.broadcasted_iota(jnp.int32, shape, dim)


def slab_offset(chunk):
    return jnp.where(chunk < 3, chunk * CAP, chunk * CAP + 2)


def pack_pages_kernel(owner, fresh, out, used):
    out[...] = jnp.zeros_like(out)

    def clear(o, carry):
        used[o] = 0
        return carry

    lax.fori_loop(0, used.shape[0], clear, 0)

    def put(p, carry):
        o = owner[p]
        k = used[o]
        out[o * CAPP + k] = fresh[p]
        used[o] = k + 1
        return carry

    lax.fori_loop(0, fresh.shape[0], put, 0, unroll=4)


def pack_pages(owners, fresh, n_attn):
    return pl.pallas_call(
        pack_pages_kernel,
        out_shape=jax.ShapeDtypeStruct((n_attn * CAPP,) + fresh.shape[1:], fresh.dtype),
        in_specs=in_smem(1) + in_vmem(1),
        out_specs=in_vmem(1)[0],
        scratch_shapes=[pltpu.SMEM((n_attn,), jnp.int32)],
        compiler_params=params(),
        name="pack_pages",
    )(owners, fresh)


def split3(value):
    pieces = []
    for _ in range(PIECES):
        piece = value.astype(BF16).astype(F32)
        pieces.append(piece)
        value = value - piece
    return pieces


def attend_kernel(
    table,
    lengths,
    queries,
    stream,
    kv_pool,
    arrived,
    gain,
    router,
    ids,
    kv_out,
    hidden_out,
    payload,
    select_out,
    pool,
    q_scr,
    o_scr,
    sems,
):
    rows, width = queries.shape
    heads = width // LANES
    pages = table.shape[1]
    load_old = pltpu.make_async_copy(
        kv_pool.at[pl.ds(0, OLD_PAGES)], pool.at[pl.ds(0, OLD_PAGES)], sems.at[0]
    )
    fresh_slots = pl.ds(OLD_PAGES, arrived.shape[0])
    load_new = pltpu.make_async_copy(arrived, pool.at[fresh_slots], sems.at[1])
    load_old.start()
    load_new.start()
    q_scr[...] = jnp.zeros_like(q_scr)
    for h in range(heads):
        q_scr[pl.ds(h, rows, stride=16), :] = queries[:, h * LANES : (h + 1) * LANES].astype(F32)

    ids_f = ids[...].astype(F32)
    cols = EXPERTS * 32
    spread = (iota((rows, cols), 1) % rows == iota((rows, cols), 0)).astype(F32)
    ids_l = lax.dot_general(ids_f, spread, (((0,), (0,)), ((), ())), preferred_element_type=F32)
    ids_l = ids_l.astype(jnp.int32)
    e0, e1 = ids_l[0:1], ids_l[1:2]
    expert = iota((8, cols), 0)
    routed = ((expert == e0) | (expert == e1)).astype(F32)
    before = ((iota((cols, cols), 0) < rows) & (iota((cols, cols), 0) < iota((cols, cols), 1) % rows)).astype(F32)
    slot = jnp.dot(routed, before, preferred_element_type=F32).astype(jnp.int32)
    slot0 = jnp.sum(jnp.where(expert == e0, slot, 0), axis=0, keepdims=True)
    slot1 = jnp.sum(jnp.where(expert == e1, slot, 0), axis=0, keepdims=True)
    column = iota((1, cols), 1)
    offset = slab_offset(column // rows)
    features = column < heads * rows
    target0 = jnp.where(
        features,
        e0 * SLAB + slot0 + offset,
        jnp.where(column < (heads + 1) * rows, e0 * SLAB + SCALAR_ROW, -1),
    )
    target1 = jnp.where(
        features,
        e1 * SLAB + slot1 + offset,
        jnp.where(column < (heads + 1) * rows, -1, e1 * SLAB + SCALAR_ROW),
    )
    at = iota((EXPERTS * SLAB, cols), 0)
    select = ((at == target0) | (at == target1)).astype(F32).astype(BF16)
    select_out[...] = select
    ids_c = ids[...]
    c0, c1 = ids_c[:, 0:1], ids_c[:, 1:2]
    expert_c = iota((rows, LANES), 1)
    routed_c = ((expert_c == c0) | (expert_c == c1)).astype(F32)
    before_c = (iota((rows, rows), 1) < iota((rows, rows), 0)).astype(F32)
    slot_c = jnp.dot(before_c, routed_c, preferred_element_type=F32).astype(jnp.int32)
    slot_c0 = jnp.sum(jnp.where(expert_c == c0, slot_c, 0), axis=1, keepdims=True)
    slot_c1 = jnp.sum(jnp.where(expert_c == c1, slot_c, 0), axis=1, keepdims=True)

    load_old.wait()
    load_new.wait()
    store = pltpu.make_async_copy(pool, kv_out, sems.at[2])
    store.start()
    scale = float(LANES) ** (-0.5)
    for r in range(rows):
        page_list = [pool[table[r, p]] for p in range(pages)]
        keys = jnp.concatenate([page[:, :LANES] for page in page_list], axis=0)
        values = jnp.concatenate([page[:, LANES:] for page in page_list], axis=0)
        query = q_scr[r * 16 : (r + 1) * 16, :].astype(BF16)
        scores = lax.dot_general(query, keys, (((1,), (1,)), ((), ())), preferred_element_type=F32)
        scores = scores[:8] * scale
        valid = iota(scores.shape, 1) < lengths[0, r]
        masked = jnp.where(valid, scores, -1e30)
        top = jnp.max(masked, axis=1, keepdims=True)
        weights = jnp.where(valid, jnp.exp(masked - top), 0.0)
        total = jnp.sum(weights, axis=1, keepdims=True)
        summed = jnp.dot(weights.astype(BF16), values, preferred_element_type=F32)
        o_scr[r * 8 : (r + 1) * 8, :] = summed / total
    attended = jnp.concatenate([o_scr[pl.ds(h, rows, stride=8), :] for h in range(heads)], axis=1)
    hidden = (stream[...].astype(F32) + attended).astype(BF16)
    hidden_out[...] = hidden
    hidden_f = hidden.astype(F32)
    squares = jnp.sum(hidden_f * hidden_f, axis=1, keepdims=True)
    gained = (hidden_f * gain[...].astype(F32)).astype(BF16)
    logits = jnp.dot(gained, router[...], preferred_element_type=F32)
    expert_r = iota(logits.shape, 1)
    delta = jnp.sum(
        jnp.where(expert_r == c0, logits, 0.0) - jnp.where(expert_r == c1, logits, 0.0),
        axis=1,
        keepdims=True,
    )
    lane = iota((rows, LANES), 1)

    def scalars(slots, difference):
        total = jnp.zeros((rows, LANES), F32)
        for i, piece in enumerate(split3(squares) + split3(difference)):
            total = total + jnp.where(lane == i * CAP + slots, piece, 0.0)
        return total.astype(BF16)

    parts = [gained[:, h * LANES : (h + 1) * LANES] for h in range(heads)]
    parts += [scalars(slot_c0, delta), scalars(slot_c1, -delta)]
    stacked = jnp.concatenate(parts, axis=0)
    slabs = jnp.dot(select, stacked, preferred_element_type=F32).astype(BF16)
    for e in range(EXPERTS):
        slab = slabs[e * SLAB : (e + 1) * SLAB]
        payload[2 * e] = slab
        payload[2 * e + 1] = slab
    store.wait()


def attend(table, lengths, queries, stream, kv_pool, arrived, gain, router, ids):
    rows, width = queries.shape
    anywhere = pl.BlockSpec(memory_space=pl.ANY)
    return pl.pallas_call(
        attend_kernel,
        out_shape=(
            jax.ShapeDtypeStruct(kv_pool.shape, kv_pool.dtype),
            jax.ShapeDtypeStruct((rows, width), BF16),
            jax.ShapeDtypeStruct((NZ, SLAB, LANES), BF16),
            jax.ShapeDtypeStruct((EXPERTS * SLAB, LANES), BF16),
        ),
        in_specs=in_smem(2) + in_vmem(2) + [anywhere, anywhere] + in_vmem(3),
        out_specs=tuple([anywhere] + in_vmem(3)),
        scratch_shapes=[
            pltpu.VMEM(kv_pool.shape, kv_pool.dtype),
            pltpu.VMEM((rows * 16, LANES), F32),
            pltpu.VMEM((rows * 8, LANES), F32),
            pltpu.SemaphoreType.DMA((3,)),
        ],
        compiler_params=params(),
        name="attend",
    )(table, lengths, queries, stream, kv_pool, arrived, gain, router, ids)


def to_rows_kernel(slabs, half_a, half_b):
    count = NZ * SLAB
    to, at = iota((count, count), 0), iota((count, count), 1)
    select = ((to % NZ) * SLAB + to // NZ == at).astype(F32).astype(BF16)
    flat = slabs[...].reshape(count, LANES)
    moved = jnp.dot(select, flat, preferred_element_type=F32).astype(BF16)
    half_a[...] = moved[: half_a.shape[0]]
    half_b[...] = moved[half_a.shape[0] : half_a.shape[0] + half_b.shape[0]]


def to_rows(slabs):
    return pl.pallas_call(
        to_rows_kernel,
        out_shape=(
            jax.ShapeDtypeStruct((3 * ROWS + 16, LANES), BF16),
            jax.ShapeDtypeStruct((3 * ROWS, LANES), BF16),
        ),
        in_specs=in_vmem(1),
        out_specs=tuple(in_vmem(2)),
        compiler_params=params(),
        name="to_rows",
    )(slabs)


def expert_kernel(where, *refs):
    a_refs = (refs[0:4], refs[4:8])
    b_refs = (refs[8:12], refs[12:16])
    w_gate, w_up, w_down = refs[16:19]
    out_a, out_b = (refs[19], refs[21]), (refs[20], refs[22])
    high, x = where[0], where[1]
    blocks = [(c, g) for c in range(2) for g in range(2)]
    width = 6 * LANES

    def section(hm, n):
        return jnp.bitwise_xor(high, hm) * 4 + jnp.bitwise_xor(x, n)

    def tile(c, m, n, chunk):
        if chunk < 3:
            start = n * (3 * ROWS + 16) + chunk * ROWS
            return a_refs[c][m][start : start + ROWS, :]
        start = m * 3 * ROWS + (chunk - 3) * ROWS
        return b_refs[c][n][start : start + ROWS, :]

    total = jnp.zeros((4 * ROWS, 2 * LANES), F32)
    for hm in range(2):
        for n in range(4):
            s = section(hm, n)
            for pair in range(3):
                left = jnp.concatenate(
                    [
                        jnp.concatenate(
                            [tile(c, 2 * hm + g, n, 2 * pair + i) for c, g in blocks], axis=0
                        )
                        for i in range(2)
                    ],
                    axis=1,
                )
                at = pl.ds(pl.multiple_of(s * width + pair * 2 * LANES, 2 * LANES), 2 * LANES)
                right = jnp.concatenate([w_gate[at, :], w_up[at, :]], axis=1)
                total = total + jnp.dot(left, right, preferred_element_type=F32)

    active = []
    for i, (c, g) in enumerate(blocks):
        sums = jnp.zeros((NZ, LANES), F32)
        for hm in range(2):
            for n in range(4):
                start = n * (3 * ROWS + 16) + 3 * ROWS
                sums = sums + a_refs[c][2 * hm + g][start : start + 16, :].astype(F32)[:NZ]

        def scalar(first):
            return sum(
                sums[:, (first + p) * CAP : (first + p + 1) * CAP] for p in range(PIECES)
            )

        inverse = lax.rsqrt(scalar(0) / (width * 8) + 1e-05)
        gate = 1.0 / (1.0 + jnp.exp(-scalar(PIECES) * inverse))
        part = total[i * ROWS : (i + 1) * ROWS]
        for k in range(CAP):
            rows = part[k * NZ : (k + 1) * NZ] * inverse[:, k : k + 1]
            v, up = rows[:, :LANES], rows[:, LANES:]
            active.append(v / (1.0 + jnp.exp(-v)) * up * gate[:, k : k + 1])
    active = jnp.concatenate(active, axis=0).astype(BF16)

    for hm in range(2):
        for n in range(4):
            s = section(hm, n)
            at = pl.ds(pl.multiple_of(s * width, width), width)
            made = jnp.dot(active, w_down[:, at], preferred_element_type=F32).astype(BF16)
            for i, (c, g) in enumerate(blocks):
                m = 2 * hm + g
                for chunk in range(6):
                    piece = made[i * ROWS : (i + 1) * ROWS, chunk * LANES : (chunk + 1) * LANES]
                    if chunk < 3:
                        out_a[c][n, m, chunk * ROWS : (chunk + 1) * ROWS, :] = piece
                    else:
                        out_b[c][m, n, (chunk - 3) * ROWS : (chunk - 2) * ROWS, :] = piece


def run_expert(where, own_a, other_a, own_b, other_b, w_gate, w_up, w_down):
    out = jax.ShapeDtypeStruct((4, 4, 3 * ROWS, LANES), BF16)
    return pl.pallas_call(
        expert_kernel,
        out_shape=(out,) * 4,
        in_specs=in_smem(1) + in_vmem(19),
        out_specs=tuple(in_vmem(4)),
        compiler_params=params(),
        name="expert",
    )(where, *own_a, *other_a, *own_b, *other_b, w_gate, w_up, w_down)


def add_cores_kernel(own_a, own_b, other_a, other_b, *outs):
    for n in range(4):
        outs[n][...] = (own_a[n].astype(F32) + other_a[n].astype(F32)).astype(BF16)
        outs[4 + n][...] = (own_b[n].astype(F32) + other_b[n].astype(F32)).astype(BF16)


def add_cores(own_a, own_b, other_a, other_b):
    out = jax.ShapeDtypeStruct(own_a.shape[1:], BF16)
    return pl.pallas_call(
        add_cores_kernel,
        out_shape=(out,) * 8,
        in_specs=in_vmem(4),
        out_specs=tuple(in_vmem(8)),
        compiler_params=params(),
        name="add_cores",
    )(own_a, own_b, other_a, other_b)


def sum4(refs):
    return (refs[0][...].astype(F32) + refs[1][...].astype(F32)) + (
        refs[2][...].astype(F32) + refs[3][...].astype(F32)
    )


def add_first_kernel(*refs):
    for half in range(2):
        summed = sum4(refs[4 * half : 4 * half + 4]).astype(BF16)
        for m in range(4):
            refs[8 + 4 * half + m][...] = summed[m]


def add_first(a, b):
    out = jax.ShapeDtypeStruct(a[0].shape[1:], BF16)
    return pl.pallas_call(
        add_first_kernel,
        out_shape=(out,) * 8,
        in_specs=in_vmem(8),
        out_specs=tuple(in_vmem(8)),
        compiler_params=params(),
        name="add_first",
    )(*a, *b)


def to_slabs_kernel(*refs):
    count = NZ * SLAB
    half = 3 * ROWS
    summed = jnp.concatenate([sum4(refs[0:4]), sum4(refs[4:8])], axis=0).astype(BF16)
    to, at = iota((count, 2 * half), 0), iota((count, 2 * half), 1)
    row = jnp.where(at < half, at // NZ, at // NZ + 2)
    select = ((at % NZ) * SLAB + row == to).astype(F32).astype(BF16)
    moved = jnp.dot(select, summed, preferred_element_type=F32).astype(BF16)
    refs[8][...] = moved.reshape(NZ, SLAB, LANES)


def to_slabs(a, b):
    return pl.pallas_call(
        to_slabs_kernel,
        out_shape=jax.ShapeDtypeStruct((NZ, SLAB, LANES), BF16),
        in_specs=in_vmem(8),
        out_specs=in_vmem(1)[0],
        compiler_params=params(),
        name="to_slabs",
    )(*a, *b)


def combine_kernel(slabs, hidden, select, mixed):
    rows, width = hidden.shape
    total = jnp.zeros((LANES, LANES), F32)
    for half in range(2):
        flat = jnp.concatenate([slabs[2 * e + half] for e in range(EXPERTS)], axis=0)
        total = total + lax.dot_general(
            select[...], flat, (((0,), (0,)), ((), ())), preferred_element_type=F32
        )
    blended = jnp.concatenate(
        [total[h * rows : (h + 1) * rows] for h in range(width // LANES)], axis=1
    )
    mixed[...] = (hidden[...].astype(F32) + blended).astype(BF16)


def combine(slabs, hidden, select):
    return pl.pallas_call(
        combine_kernel,
        out_shape=jax.ShapeDtypeStruct(hidden.shape, BF16),
        in_specs=in_vmem(3),
        out_specs=in_vmem(1)[0],
        compiler_params=params(),
        name="combine",
    )(slabs, hidden, select)


def exchange_z(slabs):
    return lax.all_to_all(slabs, "attn", 0, 0, axis_index_groups=Z_GROUPS, tiled=True)


def on_device(
    queries,
    stream,
    kv_pool,
    fresh_kv,
    fresh_owner,
    page_table,
    lengths,
    norm_gain,
    router,
    expert_ids,
    w_gate,
    w_up,
    w_down,
):
    n_attn = lax.axis_size("attn")
    pages, kv_local, page_len, page_width = kv_pool.shape
    sect = lax.axis_index("sect")
    where = jnp.stack([sect // 4, sect % 4]).astype(jnp.int32)

    outgoing = pack_pages(fresh_owner[:, 0], fresh_kv.reshape(-1, page_len, page_width), n_attn)
    arrived = lax.all_to_all(outgoing, "attn", 0, 0, tiled=True)
    kv_out, hidden, payload, select = attend(
        page_table,
        lengths,
        queries,
        stream,
        kv_pool.reshape(pages, page_len, page_width),
        arrived,
        norm_gain.reshape(1, -1),
        router,
        expert_ids,
    )

    half_a, half_b = to_rows(exchange_z(payload))
    a = gather4(half_a, along_x)
    b = gather4(half_b, along_y)
    a, b = lax.optimization_barrier((a, b))
    a = gather4(jnp.concatenate(a, axis=0), along_y)
    b = gather4(jnp.concatenate(b, axis=0), along_x)
    other_a = [permute(v, OTHER_CORE) for v in a]
    other_b = [permute(v, OTHER_CORE) for v in b]
    own_a, own_b, for_a, for_b = run_expert(where, a, other_a, b, other_b, w_gate, w_up, w_down)

    sums = add_cores(own_a, own_b, permute(for_a, OTHER_CORE), permute(for_b, OTHER_CORE))
    a = [sums[0]] + [permute(sums[i], along_x(i)) for i in (1, 2, 3)]
    b = [sums[4]] + [permute(sums[4 + i], along_y(i)) for i in (1, 2, 3)]
    sums = add_first(a, b)
    a = [sums[0]] + [permute(sums[i], along_y(i)) for i in (1, 2, 3)]
    b = [sums[4]] + [permute(sums[4 + i], along_x(i)) for i in (1, 2, 3)]
    mixed = combine(exchange_z(to_slabs(a, b)), hidden, select)
    return (mixed, kv_out.reshape(kv_pool.shape))


def solution(mesh):
    return jax.shard_map(
        on_device,
        mesh=mesh,
        in_specs=(
            P("attn", "sect"),
            P("attn", "sect"),
            P("attn", "sect", None, None),
            P("attn", "sect", None, None),
            P("attn", None),
            P("attn", None),
            P("attn", None),
            P("sect"),
            P("sect", None),
            P("attn", None),
            P(None, ("attn", "sect")),
            P(None, ("attn", "sect")),
            P(("attn", "sect"), None),
        ),
        out_specs=(P("attn", "sect"), P("attn", "sect", None, None)),
        check_vma=False,
    )
```

time: 667 us -> 181 us (0.27)
  blocking collectives: 500 us -> 26.1 us
  starting transfers between devices: 10 us -> 44.4 us
  Pallas kernels: 0 us -> 31 us
  matrix products: 21.9 us -> 0 us
  local copies, waits for them, and re-layouts: 29.6 us -> 9.27 us
  between operations: 14.2 us -> 1 us
  waiting for transfers between devices: 78.8 us -> 67.4 us
  other arithmetic: 11.4 us -> 0.62 us
    all_to_all x2, blocking collectives: 426 us -> 26.1 us  [exchange_z(): lax.all_to_all(slabs, 'attn', 0, 0, axis_index_groups=Z_GROUPS, tiled=True)]
    reduce_scatter x1 -> x0, waiting for transfers between devices: 52.3 us -> none  [on_device(): lax.psum_scatter(summed_group, 'sect', scatter_dimension=2, tiled=True)]
    ppermute x0 -> x34, waiting for transfers between devices: none -> 40.4 us  [permute(): return lax.ppermute(value, AXES, perm)]
    psum x2 -> x0, blocking collectives: 39.7 us -> none  [the longest x1 21 us: on_device(): lax.psum(jnp.dot(normed, router, preferred_element_type=jnp.float32), 'se...]
    all_gather x1 -> x0, blocking collectives: 34.6 us -> none  [on_device(): source = lax.all_gather(normed, 'sect', axis=1, tiled=True)]
    ppermute x0 -> x34, starting transfers between devices: none -> 34.5 us  [permute(): return lax.ppermute(value, AXES, perm)]
    pallas_call x0 -> x8, Pallas kernels: none -> 31 us  [the longest x1 9.64 us: run_expert(): pl.pallas_call(expert_kernel, out_shape=(out,) * 4, in_specs=in_smem(1) +...]
    dot_general x8 -> x0, matrix products: 21.9 us -> none  [the longest x1 9.89 us: on_device(): jnp.dot(active, w_down, preferred_element_type=jnp.float32)]
  transfers between devices with their start and end apart: 2 -> 35, of which waited for: 2 -> 16; matrix products, arithmetic and copies ran while one was open for 1% -> 2% of each run, Pallas kernels for 0% -> 0%
where the time goes in v1:
time: 181 us; the launch traced here: 180 us
  waiting for transfers between devices  67.4 us (37%)
  starting transfers between devices  44.4 us (25%)
  Pallas kernels  31 us (17%)
  blocking collectives  26.1 us (14%)
  local copies, waits for them, and re-layouts  9.27 us (5%)
    ppermute x34, waiting for transfers between devices, permute(): return lax.ppermute(value, AXES, perm)  40.4 us
    ppermute x34, starting transfers between devices, permute(): return lax.ppermute(value, AXES, perm)  34.5 us
    all_to_all x1, waiting for transfers between devices, on_device(): arrived = lax.all_to_all(outgoing, 'attn', 0, 0, tiled=True)  27 us
    all_to_all x2, blocking collectives, exchange_z(): lax.all_to_all(slabs, 'attn', 0, 0, axis_index_groups=Z_GROUPS, tiled=True)  26.1 us
    all_to_all x1, starting transfers between devices, on_device(): arrived = lax.all_to_all(outgoing, 'attn', 0, 0, tiled=True)  9.87 us
    pallas_call x1, Pallas kernels, run_expert(): pl.pallas_call(expert_kernel, out_shape=(out,) * 4, in_specs=in_smem(1) +...  9.64 us
    unnamed x72, local copies, waits for them, and re-layouts  8.65 us
    pallas_call x1, Pallas kernels, attend(): pl.pallas_call(attend_kernel, out_shape=(jax.ShapeDtypeStruct(kv_pool.sha...  7.43 us
  transfers between devices with their start and end apart: 35, of which 16 were waited for; matrix products, arithmetic and copies ran while one was open for 2% of the time, Pallas kernels for 0%

profile of v1, /device:TPU:6, one launch (start us, length us, event | category | flops | bytes accessed | tf_op | source)
XLA Modules:
  0.0 179.8 jit_solution(15586868806051914273)
XLA Ops:
  0.7 2.4 %pack_pages.1 = bf16[128,16,256]{2,1,0:T(8,128)(2,1)} custom-call(s32[32]{0:T(128)} %bitcast.10, bf16[32,16,256]{2,1,0:T(8,128)(2,1)} %bitcast.9), custom_call_target="tpu_custom_call" | custom-call | tf_op jit(solution)/shard_map/pack_pages/pallas_call | solution.py:100
  3.0 9.9 %all-to-all-start = ((bf16[128,16,256]{2,1,0:T(8,128)(2,1)}), bf16[128,16,256]{2,1,0:T(8,128)(2,1)S(1)}, u32[]{:S(2)}, u32[]{:S(2)}) async-start(bf16[128,16,256]{2,1,0:T(8,128)(2,1)} %pack_pages.1), calls=%async_computation | async-start | bytes 2097152 | tf_op jit(solution)/shard_map/all_to_all | solution.py:490
  12.9 0.6 reshape.18.gain
  13.5 0.7 copy.16.ids
  14.2 0.8 copy.15.router
  15.0 27.0 %all-to-all-done.arrived = bf16[128,16,256]{2,1,0:T(8,128)(2,1)S(1)} async-done(((bf16[128,16,256]{2,1,0:T(8,128)(2,1)}), bf16[128,16,256]{2,1,0:T(8,128)(2,1)S(1)}, u32[]{:S(2)}, u32[]{:S(2)}) %all-to-all-start) | async-done | bytes 1048608 | tf_op jit(solution)/shard_map/all_to_all | solution.py:490
  42.0 1.0 copy-done
  43.1 7.4 %attend.1 = (bf16[320,16,256]{2,1,0:T(8,128)(2,1)}, bf16[16,768]{1,0:T(8,128)(2,1)}, bf16[8,64,128]{2,1,0:T(8,128)(2,1)}, bf16[256,128]{1,0:T(8,128)(2,1)}) custom-call(s32[16,16]{1,0:T(8,128)} %table.1, s32[1,16]{1,0:T(1,128)} %lengths.1, bf16[16,768]{1,0:T(8,128)(2,1)} %queries.1, bf16[16,768]{1,0:T(8,128)(2,1)} %stream.1, bf16[320,16,256]{2,1,0:T(8,128)(2,1)} %bitcast.8, ...), custom_call_target="tpu_custom_call" | custom-call | tf_op jit(solution)/shard_map/attend/pallas_call | solution.py:244
  50.5 13.1 %all_to_all.15.slabs = bf16[8,64,128]{2,1,0:T(8,128)(2,1)} all-to-all(bf16[8,64,128]{2,1,0:T(8,128)(2,1)} %get-tuple-element.36), channel_id=1, replica_groups={{0,32,64,96,128,160,192,224},{8,40,72,104,136,168,200,232},{16,48,80,11..., dimensions={0} | all-to-all | bytes 262144 | tf_op jit(solution)/shard_map/all_to_all | solution.py:466
  63.6 1.8 %to_rows.1 = (bf16[256,128]{1,0:T(8,128)(2,1)}, bf16[240,128]{1,0:T(8,128)(2,1)}) custom-call(bf16[8,64,128]{2,1,0:T(8,128)(2,1)} %all_to_all.15.slabs), custom_call_target="tpu_custom_call" | custom-call | tf_op jit(solution)/shard_map/to_rows/pallas_call | solution.py:276
  65.4 3.1 %collective-permute-start.5 = (bf16[240,128]{1,0:T(8,128)(2,1)}, bf16[240,128]{1,0:T(8,128)(2,1)S(1)}, u32[]{:S(2)}, u32[]{:S(2)}) collective-permute-start(bf16[240,128]{1,0:T(8,128)(2,1)} %get-tuple-element.43), channel_id=1, source_target_pairs={{0,20},{8,28},{1,21},{9,29},{2,22},{10,30},{3,23},{11,31},{16,4},{... | collective-permute-start | bytes 184328 | tf_op jit(solution)/shard_map/ppermute | solution.py:53
  68.4 0.5 collective-permute-start.2
  68.9 2.4 %collective-permute-start.1 = (bf16[256,128]{1,0:T(8,128)(2,1)}, bf16[256,128]{1,0:T(8,128)(2,1)S(1)}, u32[]{:S(2)}, u32[]{:S(2)}) collective-permute-start(bf16[256,128]{1,0:T(8,128)(2,1)} %get-tuple-element.39), channel_id=1, source_target_pairs={{0,2},{8,10},{1,3},{9,11},{2,0},{10,8},{3,1},{11,9},{16,18},{24,26... | collective-permute-start | bytes 196616 | tf_op jit(solution)/shard_map/ppermute | solution.py:53
  71.3 1.2 collective-permute-start
  72.5 0.6 collective-permute-start.4
  73.2 0.4 collective-permute-start.3
  73.6 4.9 %collective-permute-done.4 = bf16[240,128]{1,0:T(8,128)(2,1)S(1)} collective-permute-done((bf16[240,128]{1,0:T(8,128)(2,1)}, bf16[240,128]{1,0:T(8,128)(2,1)S(1)}, u32[]{:S(2)}, u32[]{:S(2)}) %collective-permute-start.4) | collective-permute-done | bytes 61472 | tf_op jit(solution)/shard_map/ppermute | solution.py:53
  78.5 0.8 constant_dynamic-update-slice_fusion.7
  79.5 0.6 collective-permute-start.15
  80.0 2.4 %collective-permute-start.14 = (bf16[960,128]{1,0:T(8,128)(2,1)S(1)}, bf16[960,128]{1,0:T(8,128)(2,1)S(1)}, u32[]{:S(2)}, u32[]{:S(2)}) collective-permute-start(bf16[960,128]{1,0:T(8,128)(2,1)S(1)} %constant_dynamic-update-slice_fusion.4.refs_8_), channel_id=1, source_target_pairs={{0,2},{8,10},{1,3},{9,11},{2,0},{10,8},{3,1},{11,9},{16,18},{24,26... | collective-permute-start | bytes 737288 | tf_op jit(solution)/shard_map/ppermute | solution.py:53
  82.5 1.2 collective-permute-start.13
  83.7 0.8 constant_dynamic-update-slice_fusion.3
  84.6 1.3 collective-permute-start.8
  85.9 0.9 collective-permute-start.7
  86.8 7.5 %collective-permute-done.15.refs_11_ = bf16[960,128]{1,0:T(8,128)(2,1)S(1)} collective-permute-done((bf16[960,128]{1,0:T(8,128)(2,1)S(1)}, bf16[960,128]{1,0:T(8,128)(2,1)S(1)}, u32[]{:S(2)}, u32[]{:S(2)}) %collective-permute-start.15) | collective-permute-done | bytes 245792 | tf_op jit(solution)/shard_map/ppermute | solution.py:53
  94.5 0.5 collective-permute-done.13.refs_9_
  95.0 4.3 %collective-permute-done.8.refs_3_ = bf16[1024,128]{1,0:T(8,128)(2,1)S(1)} collective-permute-done((bf16[1024,128]{1,0:T(8,128)(2,1)S(1)}, bf16[1024,128]{1,0:T(8,128)(2,1)S(1)}, u32[]{:S(2)}, u32[]{:S(2)}) %collective-permute-start.8) | collective-permute-done | bytes 262176 | tf_op jit(solution)/shard_map/ppermute | solution.py:53
  99.3 0.5 collective-permute-start.11
  99.8 2.4 %collective-permute-done.6.refs_1_ = bf16[1024,128]{1,0:T(8,128)(2,1)S(1)} collective-permute-done((bf16[1024,128]{1,0:T(8,128)(2,1)S(1)}, bf16[1024,128]{1,0:T(8,128)(2,1)S(1)}, u32[]{:S(2)}, u32[]{:S(2)}) %collective-permute-start.6) | collective-permute-done | bytes 262176 | tf_op jit(solution)/shard_map/ppermute | solution.py:53
  102.2 0.5 collective-permute-start.18
  102.7 0.7 copy-done.16
  103.4 0.3 collective-permute-start.17
  103.7 0.6 pad_add_fusion.where
  104.3 0.7 collective-permute-done.17.refs_13_
  105.2 0.6 copy-done.9
  105.9 0.7 copy-done.11
  106.6 9.6 %expert.1 = (bf16[4,4,240,128]{3,2,1,0:T(8,128)(2,1)}, bf16[4,4,240,128]{3,2,1,0:T(8,128)(2,1)}, bf16[4,4,240,128]{3,2,1,0:T(8,128)(2,1)}, bf16[4,4,240,128]{3,2,1,0:T(8,128)(2,1)}) custom-call(s32[2]{0:T(128)} %pad_add_fusion.where, bf16[1024,128]{1,0:T(8,128)(2,1)} %copy-done.3, bf16[1024,128]{1,0:T(8,128)(2,1)} %copy-done.7, bf16[1024,128]{1,0:T(8,128)(2,1)} %copy-done.6, ...), custom_call_target="tpu_custom_call" | custom-call | tf_op jit(solution)/shard_map/expert/pallas_call | solution.py:365
  116.2 0.3 collective-permute-start.20
  116.7 2.3 %collective-permute-done.20.other_a = bf16[4,4,240,128]{3,2,1,0:T(8,128)(2,1)S(1)} collective-permute-done((bf16[4,4,240,128]{3,2,1,0:T(8,128)(2,1)}, bf16[4,4,240,128]{3,2,1,0:T(8,128)(2,1)S(1)}, u32[]{:S(2)}, u32[]{:S(2)}) %collective-permute-start.20) | collective-permute-done | bytes 983072 | tf_op jit(solution)/shard_map/ppermute | solution.py:53
  119.0 1.4 collective-permute-done.21.other_b
  120.4 1.0 copy-done.2
  121.4 3.5 %add_cores.1 = (bf16[4,240,128]{2,1,0:T(8,128)(2,1)}, bf16[4,240,128]{2,1,0:T(8,128)(2,1)}, bf16[4,240,128]{2,1,0:T(8,128)(2,1)}, bf16[4,240,128]{2,1,0:T(8,128)...) custom-call(bf16[4,4,240,128]{3,2,1,0:T(8,128)(2,1)} %get-tuple-elem, ...), custom_call_target="tpu_custom_call" | custom-call | tf_op jit(solution)/shard_map/add_cores/pallas_call | solution.py:383
  124.8 1.9 %collective-permute-start.23 = (bf16[4,240,128]{2,1,0:T(8,128)(2,1)}, bf16[4,240,128]{2,1,0:T(8,128)(2,1)S(1)}, u32[]{:S(2)}, u32[]{:S(2)}) collective-permute-start(bf16[4,240,128]{2,1,0:T(8,128)(2,1)} %get-tuple-element.53), channel_id=1, source_target_pairs={{0,2},{8,10},{1,3},{9,11},{2,0},{10,8},{3,1},{11,9},{16,18},{24,26... | collective-permute-start | bytes 737288 | tf_op jit(solution)/shard_map/ppermute | solution.py:53
  126.7 2.8 %collective-permute-start.24 = (bf16[4,240,128]{2,1,0:T(8,128)(2,1)}, bf16[4,240,128]{2,1,0:T(8,128)(2,1)S(1)}, u32[]{:S(2)}, u32[]{:S(2)}) collective-permute-start(bf16[4,240,128]{2,1,0:T(8,128)(2,1)} %get-tuple-element.54), channel_id=1, source_target_pairs={{0,3},{8,11},{1,2},{9,10},{2,1},{10,9},{3,0},{11,8},{16,19},{24,27... | collective-permute-start | bytes 737288 | tf_op jit(solution)/shard_map/ppermute | solution.py:53
  129.5 0.3 collective-permute-start.25
  129.8 2.4 %collective-permute-start.26 = (bf16[4,240,128]{2,1,0:T(8,128)(2,1)}, bf16[4,240,128]{2,1,0:T(8,128)(2,1)S(1)}, u32[]{:S(2)}, u32[]{:S(2)}) collective-permute-start(bf16[4,240,128]{2,1,0:T(8,128)(2,1)} %get-tuple-element.57), channel_id=1, source_target_pairs={{0,4},{8,12},{1,5},{9,13},{2,6},{10,14},{3,7},{11,15},{16,20},{24,... | collective-permute-start | bytes 737288 | tf_op jit(solution)/shard_map/ppermute | solution.py:53
  132.2 1.6 collective-permute-done.22.refs_1_
  133.8 1.2 collective-permute-start.27
  135.0 3.4 %collective-permute-done.23.refs_2_ = bf16[4,240,128]{2,1,0:T(8,128)(2,1)S(1)} collective-permute-done((bf16[4,240,128]{2,1,0:T(8,128)(2,1)}, bf16[4,240,128]{2,1,0:T(8,128)(2,1)S(1)}, u32[]{:S(2)}, u32[]{:S(2)}) %collective-permute-start.23) | collective-permute-done | bytes 245792 | tf_op jit(solution)/shard_map/ppermute | solution.py:53
  138.4 2.6 %collective-permute-done.24.refs_3_ = bf16[4,240,128]{2,1,0:T(8,128)(2,1)S(1)} collective-permute-done((bf16[4,240,128]{2,1,0:T(8,128)(2,1)}, bf16[4,240,128]{2,1,0:T(8,128)(2,1)S(1)}, u32[]{:S(2)}, u32[]{:S(2)}) %collective-permute-start.24) | collective-permute-done | bytes 245792 | tf_op jit(solution)/shard_map/ppermute | solution.py:53
  141.0 2.0 %collective-permute-done.26.refs_6_ = bf16[4,240,128]{2,1,0:T(8,128)(2,1)S(1)} collective-permute-done((bf16[4,240,128]{2,1,0:T(8,128)(2,1)}, bf16[4,240,128]{2,1,0:T(8,128)(2,1)S(1)}, u32[]{:S(2)}, u32[]{:S(2)}) %collective-permute-start.26) | collective-permute-done | bytes 245792 | tf_op jit(solution)/shard_map/ppermute | solution.py:53
  143.0 3.8 %collective-permute-done.27.refs_7_ = bf16[4,240,128]{2,1,0:T(8,128)(2,1)S(1)} collective-permute-done((bf16[4,240,128]{2,1,0:T(8,128)(2,1)}, bf16[4,240,128]{2,1,0:T(8,128)(2,1)S(1)}, u32[]{:S(2)}, u32[]{:S(2)}) %collective-permute-start.27) | collective-permute-done | bytes 245792 | tf_op jit(solution)/shard_map/ppermute | solution.py:53
  146.9 0.7 copy-done.22
  147.6 2.5 %add_first.1 = (bf16[240,128]{1,0:T(8,128)(2,1)}, bf16[240,128]{1,0:T(8,128)(2,1)}, bf16[240,128]{1,0:T(8,128)(2,1)}, bf16[240,128]{1,0:T(8,128)(2,1)}, bf16[240...) custom-call(bf16[4,240,128]{2,1,0:T(8,128)(2,1)} %get-tuple-element.51.refs_0_, ...), custom_call_target="tpu_custom_call" | custom-call | tf_op jit(solution)/shard_map/add_first/pallas_call | solution.py:408
  150.1 2.9 %collective-permute-start.29 = (bf16[240,128]{1,0:T(8,128)(2,1)}, bf16[240,128]{1,0:T(8,128)(2,1)S(1)}, u32[]{:S(2)}, u32[]{:S(2)}) collective-permute-start(bf16[240,128]{1,0:T(8,128)(2,1)} %get-tuple-element.61), channel_id=1, source_target_pairs={{0,4},{8,12},{1,5},{9,13},{2,6},{10,14},{3,7},{11,15},{16,20},{24,... | collective-permute-start | bytes 184328 | tf_op jit(solution)/shard_map/ppermute | solution.py:53
  153.0 1.7 collective-permute-start.30
  154.8 1.9 %collective-permute-start.32 = (bf16[240,128]{1,0:T(8,128)(2,1)}, bf16[240,128]{1,0:T(8,128)(2,1)S(1)}, u32[]{:S(2)}, u32[]{:S(2)}) collective-permute-start(bf16[240,128]{1,0:T(8,128)(2,1)} %get-tuple-element.65), channel_id=1, source_target_pairs={{0,2},{8,10},{1,3},{9,11},{2,0},{10,8},{3,1},{11,9},{16,18},{24,26... | collective-permute-start | bytes 184328 | tf_op jit(solution)/shard_map/ppermute | solution.py:53
  156.7 2.8 %collective-permute-start.33 = (bf16[240,128]{1,0:T(8,128)(2,1)}, bf16[240,128]{1,0:T(8,128)(2,1)S(1)}, u32[]{:S(2)}, u32[]{:S(2)}) collective-permute-start(bf16[240,128]{1,0:T(8,128)(2,1)} %get-tuple-element.66), channel_id=1, source_target_pairs={{0,3},{8,11},{1,2},{9,10},{2,1},{10,9},{3,0},{11,8},{16,19},{24,27... | collective-permute-start | bytes 184328 | tf_op jit(solution)/shard_map/ppermute | solution.py:53
  159.5 1.2 collective-permute-done.32.refs_6_
  160.7 1.6 collective-permute-done.33.refs_7_
  162.4 0.6 copy-done.28
  163.0 2.0 %to_slabs.1 = bf16[8,64,128]{2,1,0:T(8,128)(2,1)} custom-call(bf16[240,128]{1,0:T(8,128)(2,1)} %get-tuple-element.59.refs_0_, bf16[240,128]{1,0:T(8,128)(2,1)} %copy-done.23, bf16[240,128]{1,0:T(8,128)(2,1)} %copy-done.24, bf16[240,128]{1,0:T(8,128)(2,1)} %copy-done.25, bf16[240,128]{1,0:T(8,128)(2,1)} %get-tuple-element.63.refs_4_, ...), custom_call_target="tpu_custom_call" | custom-call | tf_op jit(solution)/shard_map/to_slabs/pallas_call | solution.py:430
  165.0 13.1 %all_to_all.16.slabs = bf16[8,64,128]{2,1,0:T(8,128)(2,1)} all-to-all(bf16[8,64,128]{2,1,0:T(8,128)(2,1)} %to_slabs.1), channel_id=1, replica_groups={{0,32,64,96,128,160,192,224},{8,40,72,104,136,168,200,232},{16,48,80,11..., dimensions={0} | all-to-all | bytes 262144 | tf_op jit(solution)/shard_map/all_to_all | solution.py:466
  178.1 1.7 combine.1
  (92 shorter events, 0.8 us)
Async XLA Ops:
  0.6 12.3 %copy-start.30 = (bf16[768]{0:T(1024)(128)(2,1)S(1)}, bf16[768]{0:T(1024)(128)(2,1)}, u32[]{:S(2)}) copy-start(bf16[768]{0:T(1024)(128)(2,1)} %param.20) | copy-start | bytes 4612
  0.6 12.9 %copy-start.31 = (s32[16,2]{0,1:T(2,128)S(1)}, s32[16,2]{0,1:T(2,128)}, u32[]{:S(2)}) copy-start(s32[16,2]{0,1:T(2,128)} %param.22) | copy-start | bytes 388
  0.7 13.6 %copy-start.29 = (bf16[768,4]{0,1:T(4,128)(2,1)S(1)}, bf16[768,4]{0,1:T(4,128)(2,1)}, u32[]{:S(2)}) copy-start(bf16[768,4]{0,1:T(4,128)(2,1)} %param.21) | copy-start | bytes 18436
  3.0 39.0 %all-to-all-start = ((bf16[128,16,256]{2,1,0:T(8,128)(2,1)}), bf16[128,16,256]{2,1,0:T(8,128)(2,1)S(1)}, u32[]{:S(2)}, u32[]{:S(2)}) async-start(bf16[128,16,256]{2,1,0:T(8,128)(2,1)} %pack_pages.1), calls=%async_computation | async-start | bytes 2097152 | tf_op jit(solution)/shard_map/all_to_all | solution.py:490
  42.0 1.0 copy-start
  65.4 7.8 %collective-permute-start.5 = (bf16[240,128]{1,0:T(8,128)(2,1)}, bf16[240,128]{1,0:T(8,128)(2,1)S(1)}, u32[]{:S(2)}, u32[]{:S(2)}) collective-permute-start(bf16[240,128]{1,0:T(8,128)(2,1)} %get-tuple-element.43), channel_id=1, source_target_pairs={{0,20},{8,28},{1,21},{9,29},{2,22},{10,30},{3,23},{11,31},{16,4},{... | collective-permute-start | bytes 184328 | tf_op jit(solution)/shard_map/ppermute | solution.py:53
  68.4 10.0 %collective-permute-start.2 = (bf16[256,128]{1,0:T(8,128)(2,1)}, bf16[256,128]{1,0:T(8,128)(2,1)S(1)}, u32[]{:S(2)}, u32[]{:S(2)}) collective-permute-start(bf16[256,128]{1,0:T(8,128)(2,1)} %get-tuple-element.39), channel_id=1, source_target_pairs={{0,3},{8,11},{1,2},{9,10},{2,1},{10,9},{3,0},{11,8},{16,19},{24,27... | collective-permute-start | bytes 196616 | tf_op jit(solution)/shard_map/ppermute | solution.py:53
  68.9 9.6 %collective-permute-start.1 = (bf16[256,128]{1,0:T(8,128)(2,1)}, bf16[256,128]{1,0:T(8,128)(2,1)S(1)}, u32[]{:S(2)}, u32[]{:S(2)}) collective-permute-start(bf16[256,128]{1,0:T(8,128)(2,1)} %get-tuple-element.39), channel_id=1, source_target_pairs={{0,2},{8,10},{1,3},{9,11},{2,0},{10,8},{3,1},{11,9},{16,18},{24,26... | collective-permute-start | bytes 196616 | tf_op jit(solution)/shard_map/ppermute | solution.py:53
  71.3 7.2 %collective-permute-start = (bf16[256,128]{1,0:T(8,128)(2,1)}, bf16[256,128]{1,0:T(8,128)(2,1)S(1)}, u32[]{:S(2)}, u32[]{:S(2)}) collective-permute-start(bf16[256,128]{1,0:T(8,128)(2,1)} %get-tuple-element.39), channel_id=1, source_target_pairs={{0,1},{8,9},{1,0},{9,8},{2,3},{10,11},{3,2},{11,10},{16,17},{24,25... | collective-permute-start | bytes 196616 | tf_op jit(solution)/shard_map/ppermute | solution.py:53
  72.5 5.9 %collective-permute-start.4 = (bf16[240,128]{1,0:T(8,128)(2,1)}, bf16[240,128]{1,0:T(8,128)(2,1)S(1)}, u32[]{:S(2)}, u32[]{:S(2)}) collective-permute-start(bf16[240,128]{1,0:T(8,128)(2,1)} %get-tuple-element.43), channel_id=1, source_target_pairs={{0,4},{8,12},{1,5},{9,13},{2,6},{10,14},{3,7},{11,15},{16,20},{24,... | collective-permute-start | bytes 184328 | tf_op jit(solution)/shard_map/ppermute | solution.py:53
  73.2 5.3 %collective-permute-start.3 = (bf16[240,128]{1,0:T(8,128)(2,1)}, bf16[240,128]{1,0:T(8,128)(2,1)S(1)}, u32[]{:S(2)}, u32[]{:S(2)}) collective-permute-start(bf16[240,128]{1,0:T(8,128)(2,1)} %get-tuple-element.43), channel_id=1, source_target_pairs={{0,16},{8,24},{1,17},{9,25},{2,18},{10,26},{3,19},{11,27},{16,0},{... | collective-permute-start | bytes 184328 | tf_op jit(solution)/shard_map/ppermute | solution.py:53
  79.4 25.7 %copy-start.4 = (bf16[960,128]{1,0:T(8,128)(2,1)}, bf16[960,128]{1,0:T(8,128)(2,1)S(1)}, u32[]{:S(2)}) copy-start(bf16[960,128]{1,0:T(8,128)(2,1)S(1)} %constant_dynamic-update-slice_fusion.4.refs_8_) | copy-start | bytes 737284
  79.4 6.5 %collective-permute-start.16 = (bf16[960,128]{1,0:T(8,128)(2,1)S(1)}, bf16[960,128]{1,0:T(8,128)(2,1)S(1)}, u32[]{:S(2)}, u32[]{:S(2)}) collective-permute-start(bf16[960,128]{1,0:T(8,128)(2,1)S(1)} %constant_dynamic-update-slice_fusion.4.refs_8_), channel_id=1, source_target_pairs={{0,8},{8,0},{1,9},{9,1},{2,10},{10,2},{3,11},{11,3},{16,24},{24,16... | collective-permute-start | bytes 737288 | tf_op jit(solution)/shard_map/ppermute | solution.py:53
  79.5 14.9 %collective-permute-start.15 = (bf16[960,128]{1,0:T(8,128)(2,1)S(1)}, bf16[960,128]{1,0:T(8,128)(2,1)S(1)}, u32[]{:S(2)}, u32[]{:S(2)}) collective-permute-start(bf16[960,128]{1,0:T(8,128)(2,1)S(1)} %constant_dynamic-update-slice_fusion.4.refs_8_), channel_id=1, source_target_pairs={{0,3},{8,11},{1,2},{9,10},{2,1},{10,9},{3,0},{11,8},{16,19},{24,27... | collective-permute-start | bytes 737288 | tf_op jit(solution)/shard_map/ppermute | solution.py:53
  80.0 14.3 %collective-permute-start.14 = (bf16[960,128]{1,0:T(8,128)(2,1)S(1)}, bf16[960,128]{1,0:T(8,128)(2,1)S(1)}, u32[]{:S(2)}, u32[]{:S(2)}) collective-permute-start(bf16[960,128]{1,0:T(8,128)(2,1)S(1)} %constant_dynamic-update-slice_fusion.4.refs_8_), channel_id=1, source_target_pairs={{0,2},{8,10},{1,3},{9,11},{2,0},{10,8},{3,1},{11,9},{16,18},{24,26... | collective-permute-start | bytes 737288 | tf_op jit(solution)/shard_map/ppermute | solution.py:53
  82.5 12.5 %collective-permute-start.13 = (bf16[960,128]{1,0:T(8,128)(2,1)S(1)}, bf16[960,128]{1,0:T(8,128)(2,1)S(1)}, u32[]{:S(2)}, u32[]{:S(2)}) collective-permute-start(bf16[960,128]{1,0:T(8,128)(2,1)S(1)} %constant_dynamic-update-slice_fusion.4.refs_8_), channel_id=1, source_target_pairs={{0,1},{8,9},{1,0},{9,8},{2,3},{10,11},{3,2},{11,10},{16,17},{24,25... | collective-permute-start | bytes 737288 | tf_op jit(solution)/shard_map/ppermute | solution.py:53
  84.6 20.6 %copy-start.3 = (bf16[1024,128]{1,0:T(8,128)(2,1)}, bf16[1024,128]{1,0:T(8,128)(2,1)S(1)}, u32[]{:S(2)}) copy-start(bf16[1024,128]{1,0:T(8,128)(2,1)S(1)} %constant_dynamic-update-slice_fusion.refs_0_) | copy-start | bytes 786436
  84.6 14.7 %collective-permute-start.8 = (bf16[1024,128]{1,0:T(8,128)(2,1)S(1)}, bf16[1024,128]{1,0:T(8,128)(2,1)S(1)}, u32[]{:S(2)}, u32[]{:S(2)}) collective-permute-start(bf16[1024,128]{1,0:T(8,128)(2,1)S(1)} %constant_dynamic-update-slice_fusion.refs_0_), channel_id=1, source_target_pairs={{0,20},{8,28},{1,21},{9,29},{2,22},{10,30},{3,23},{11,31},{16,4},{... | collective-permute-start | bytes 786440 | tf_op jit(solution)/shard_map/ppermute | solution.py:53
  85.9 19.3 %copy-start.12 = (bf16[960,128]{1,0:T(8,128)(2,1)}, bf16[960,128]{1,0:T(8,128)(2,1)S(1)}, u32[]{:S(2)}) copy-start(bf16[960,128]{1,0:T(8,128)(2,1)S(1)} %collective-permute-done.16.refs_12_) | copy-start | bytes 737284
  85.9 13.4 %collective-permute-start.7 = (bf16[1024,128]{1,0:T(8,128)(2,1)S(1)}, bf16[1024,128]{1,0:T(8,128)(2,1)S(1)}, u32[]{:S(2)}, u32[]{:S(2)}) collective-permute-start(bf16[1024,128]{1,0:T(8,128)(2,1)S(1)} %constant_dynamic-update-slice_fusion.refs_0_), channel_id=1, source_target_pairs={{0,4},{8,12},{1,5},{9,13},{2,6},{10,14},{3,7},{11,15},{16,20},{24,... | collective-permute-start | bytes 786440 | tf_op jit(solution)/shard_map/ppermute | solution.py:53
  94.3 10.8 %copy-start.13 = (bf16[960,128]{1,0:T(8,128)(2,1)}, bf16[960,128]{1,0:T(8,128)(2,1)S(1)}, u32[]{:S(2)}) copy-start(bf16[960,128]{1,0:T(8,128)(2,1)S(1)} %collective-permute-done.15.refs_11_) | copy-start | bytes 737284
  94.3 7.9 %collective-permute-start.6 = (bf16[1024,128]{1,0:T(8,128)(2,1)S(1)}, bf16[1024,128]{1,0:T(8,128)(2,1)S(1)}, u32[]{:S(2)}, u32[]{:S(2)}) collective-permute-start(bf16[1024,128]{1,0:T(8,128)(2,1)S(1)} %constant_dynamic-update-slice_fusion.refs_0_), channel_id=1, source_target_pairs={{0,16},{8,24},{1,17},{9,25},{2,18},{10,26},{3,19},{11,27},{16,0},{... | collective-permute-start | bytes 786440 | tf_op jit(solution)/shard_map/ppermute | solution.py:53
  94.3 10.8 %copy-start.14 = (bf16[960,128]{1,0:T(8,128)(2,1)}, bf16[960,128]{1,0:T(8,128)(2,1)S(1)}, u32[]{:S(2)}) copy-start(bf16[960,128]{1,0:T(8,128)(2,1)S(1)} %collective-permute-done.14.refs_10_) | copy-start | bytes 737284
  94.4 7.8 %collective-permute-start.9 = (bf16[1024,128]{1,0:T(8,128)(2,1)S(1)}, bf16[1024,128]{1,0:T(8,128)(2,1)S(1)}, u32[]{:S(2)}, u32[]{:S(2)}) collective-permute-start(bf16[1024,128]{1,0:T(8,128)(2,1)S(1)} %constant_dynamic-update-slice_fusion.refs_0_), channel_id=1, source_target_pairs={{0,8},{8,0},{1,9},{9,1},{2,10},{10,2},{3,11},{11,3},{16,24},{24,16... | collective-permute-start | bytes 786440 | tf_op jit(solution)/shard_map/ppermute | solution.py:53
  95.0 10.2 %copy-start.15 = (bf16[960,128]{1,0:T(8,128)(2,1)}, bf16[960,128]{1,0:T(8,128)(2,1)S(1)}, u32[]{:S(2)}) copy-start(bf16[960,128]{1,0:T(8,128)(2,1)S(1)} %collective-permute-done.13.refs_9_) | copy-start | bytes 737284
  95.0 7.8 %collective-permute-start.19 = (bf16[960,128]{1,0:T(8,128)(2,1)S(1)}, bf16[960,128]{1,0:T(8,128)(2,1)S(1)}, u32[]{:S(2)}, u32[]{:S(2)}) collective-permute-start(bf16[960,128]{1,0:T(8,128)(2,1)S(1)} %collective-permute-done.15.refs_11_), channel_id=1, source_target_pairs={{0,8},{8,0},{1,9},{9,1},{2,10},{10,2},{3,11},{11,3},{16,24},{24,16... | collective-permute-start | bytes 737288 | tf_op jit(solution)/shard_map/ppermute | solution.py:53
  99.3 5.9 %copy-start.5 = (bf16[1024,128]{1,0:T(8,128)(2,1)}, bf16[1024,128]{1,0:T(8,128)(2,1)S(1)}, u32[]{:S(2)}) copy-start(bf16[1024,128]{1,0:T(8,128)(2,1)S(1)} %collective-permute-done.8.refs_3_) | copy-start | bytes 786436
  99.3 5.8 %collective-permute-start.12 = (bf16[1024,128]{1,0:T(8,128)(2,1)S(1)}, bf16[1024,128]{1,0:T(8,128)(2,1)S(1)}, u32[]{:S(2)}, u32[]{:S(2)}) collective-permute-start(bf16[1024,128]{1,0:T(8,128)(2,1)S(1)} %collective-permute-done.8.refs_3_), channel_id=1, source_target_pairs={{0,8},{8,0},{1,9},{9,1},{2,10},{10,2},{3,11},{11,3},{16,24},{24,16... | collective-permute-start | bytes 786440 | tf_op jit(solution)/shard_map/ppermute | solution.py:53
  99.3 5.9 %copy-start.6 = (bf16[1024,128]{1,0:T(8,128)(2,1)}, bf16[1024,128]{1,0:T(8,128)(2,1)S(1)}, u32[]{:S(2)}) copy-start(bf16[1024,128]{1,0:T(8,128)(2,1)S(1)} %collective-permute-done.7.refs_2_) | copy-start | bytes 786436
  99.3 5.8 %collective-permute-start.11 = (bf16[1024,128]{1,0:T(8,128)(2,1)S(1)}, bf16[1024,128]{1,0:T(8,128)(2,1)S(1)}, u32[]{:S(2)}, u32[]{:S(2)}) collective-permute-start(bf16[1024,128]{1,0:T(8,128)(2,1)S(1)} %collective-permute-done.7.refs_2_), channel_id=1, source_target_pairs={{0,8},{8,0},{1,9},{9,1},{2,10},{10,2},{3,11},{11,3},{16,24},{24,16... | collective-permute-start | bytes 786440 | tf_op jit(solution)/shard_map/ppermute | solution.py:53
  102.2 3.0 %copy-start.7 = (bf16[1024,128]{1,0:T(8,128)(2,1)}, bf16[1024,128]{1,0:T(8,128)(2,1)S(1)}, u32[]{:S(2)}) copy-start(bf16[1024,128]{1,0:T(8,128)(2,1)S(1)} %collective-permute-done.6.refs_1_) | copy-start | bytes 786436
  102.2 2.9 %collective-permute-start.10 = (bf16[1024,128]{1,0:T(8,128)(2,1)S(1)}, bf16[1024,128]{1,0:T(8,128)(2,1)S(1)}, u32[]{:S(2)}, u32[]{:S(2)}) collective-permute-start(bf16[1024,128]{1,0:T(8,128)(2,1)S(1)} %collective-permute-done.6.refs_1_), channel_id=1, source_target_pairs={{0,8},{8,0},{1,9},{9,1},{2,10},{10,2},{3,11},{11,3},{16,24},{24,16... | collective-permute-start | bytes 786440 | tf_op jit(solution)/shard_map/ppermute | solution.py:53
  102.2 3.0 %copy-start.8 = (bf16[1024,128]{1,0:T(8,128)(2,1)}, bf16[1024,128]{1,0:T(8,128)(2,1)S(1)}, u32[]{:S(2)}) copy-start(bf16[1024,128]{1,0:T(8,128)(2,1)S(1)} %collective-permute-done.9.refs_4_) | copy-start | bytes 786436
  102.2 2.1 %collective-permute-start.18 = (bf16[960,128]{1,0:T(8,128)(2,1)S(1)}, bf16[960,128]{1,0:T(8,128)(2,1)}, u32[]{:S(2)}, u32[]{:S(2)}) collective-permute-start(bf16[960,128]{1,0:T(8,128)(2,1)S(1)} %collective-permute-done.14.refs_10_), channel_id=1, source_target_pairs={{0,8},{8,0},{1,9},{9,1},{2,10},{10,2},{3,11},{11,3},{16,24},{24,16... | collective-permute-start | bytes 737288 | tf_op jit(solution)/shard_map/ppermute | solution.py:53
  102.7 0.7 copy-start.16
  103.4 1.6 collective-permute-start.17
  105.1 0.7 copy-start.9
  105.1 0.8 copy-start.10
  116.2 2.8 %collective-permute-start.20 = (bf16[4,4,240,128]{3,2,1,0:T(8,128)(2,1)}, bf16[4,4,240,128]{3,2,1,0:T(8,128)(2,1)S(1)}, u32[]{:S(2)}, u32[]{:S(2)}) collective-permute-start(bf16[4,4,240,128]{3,2,1,0:T(8,128)(2,1)} %get-tuple-element.49), channel_id=1, source_target_pairs={{0,8},{8,0},{1,9},{9,1},{2,10},{10,2},{3,11},{11,3},{16,24},{24,16... | collective-permute-start | bytes 2949128 | tf_op jit(solution)/shard_map/ppermute | solution.py:53
  116.5 3.9 %collective-permute-start.21 = (bf16[4,4,240,128]{3,2,1,0:T(8,128)(2,1)}, bf16[4,4,240,128]{3,2,1,0:T(8,128)(2,1)S(1)}, u32[]{:S(2)}, u32[]{:S(2)}) collective-permute-start(bf16[4,4,240,128]{3,2,1,0:T(8,128)(2,1)} %get-tuple-element.50), channel_id=1, source_target_pairs={{0,8},{8,0},{1,9},{9,1},{2,10},{10,2},{3,11},{11,3},{16,24},{24,16... | collective-permute-start | bytes 2949128 | tf_op jit(solution)/shard_map/ppermute | solution.py:53
  119.0 1.4 copy-start.1
  120.4 1.0 copy-start.2
  124.8 9.0 %collective-permute-start.22 = (bf16[4,240,128]{2,1,0:T(8,128)(2,1)}, bf16[4,240,128]{2,1,0:T(8,128)(2,1)S(1)}, u32[]{:S(2)}, u32[]{:S(2)}) collective-permute-start(bf16[4,240,128]{2,1,0:T(8,128)(2,1)} %get-tuple-element.52), channel_id=1, source_target_pairs={{0,1},{8,9},{1,0},{9,8},{2,3},{10,11},{3,2},{11,10},{16,17},{24,25... | collective-permute-start | bytes 737288 | tf_op jit(solution)/shard_map/ppermute | solution.py:53
  124.8 13.6 %collective-permute-start.23 = (bf16[4,240,128]{2,1,0:T(8,128)(2,1)}, bf16[4,240,128]{2,1,0:T(8,128)(2,1)S(1)}, u32[]{:S(2)}, u32[]{:S(2)}) collective-permute-start(bf16[4,240,128]{2,1,0:T(8,128)(2,1)} %get-tuple-element.53), channel_id=1, source_target_pairs={{0,2},{8,10},{1,3},{9,11},{2,0},{10,8},{3,1},{11,9},{16,18},{24,26... | collective-permute-start | bytes 737288 | tf_op jit(solution)/shard_map/ppermute | solution.py:53
  126.7 14.3 %collective-permute-start.24 = (bf16[4,240,128]{2,1,0:T(8,128)(2,1)}, bf16[4,240,128]{2,1,0:T(8,128)(2,1)S(1)}, u32[]{:S(2)}, u32[]{:S(2)}) collective-permute-start(bf16[4,240,128]{2,1,0:T(8,128)(2,1)} %get-tuple-element.54), channel_id=1, source_target_pairs={{0,3},{8,11},{1,2},{9,10},{2,1},{10,9},{3,0},{11,8},{16,19},{24,27... | collective-permute-start | bytes 737288 | tf_op jit(solution)/shard_map/ppermute | solution.py:53
  129.5 11.5 %collective-permute-start.25 = (bf16[4,240,128]{2,1,0:T(8,128)(2,1)}, bf16[4,240,128]{2,1,0:T(8,128)(2,1)S(1)}, u32[]{:S(2)}, u32[]{:S(2)}) collective-permute-start(bf16[4,240,128]{2,1,0:T(8,128)(2,1)} %get-tuple-element.56), channel_id=1, source_target_pairs={{0,16},{8,24},{1,17},{9,25},{2,18},{10,26},{3,19},{11,27},{16,0},{... | collective-permute-start | bytes 737288 | tf_op jit(solution)/shard_map/ppermute | solution.py:53
  129.8 13.2 %collective-permute-start.26 = (bf16[4,240,128]{2,1,0:T(8,128)(2,1)}, bf16[4,240,128]{2,1,0:T(8,128)(2,1)S(1)}, u32[]{:S(2)}, u32[]{:S(2)}) collective-permute-start(bf16[4,240,128]{2,1,0:T(8,128)(2,1)} %get-tuple-element.57), channel_id=1, source_target_pairs={{0,4},{8,12},{1,5},{9,13},{2,6},{10,14},{3,7},{11,15},{16,20},{24,... | collective-permute-start | bytes 737288 | tf_op jit(solution)/shard_map/ppermute | solution.py:53
  133.8 13.1 %copy-start.17 = (bf16[4,240,128]{2,1,0:T(8,128)(2,1)}, bf16[4,240,128]{2,1,0:T(8,128)(2,1)S(1)}, u32[]{:S(2)}) copy-start(bf16[4,240,128]{2,1,0:T(8,128)(2,1)S(1)} %collective-permute-done.22.refs_1_) | copy-start | bytes 737284
  133.8 13.1 %collective-permute-start.27 = (bf16[4,240,128]{2,1,0:T(8,128)(2,1)}, bf16[4,240,128]{2,1,0:T(8,128)(2,1)S(1)}, u32[]{:S(2)}, u32[]{:S(2)}) collective-permute-start(bf16[4,240,128]{2,1,0:T(8,128)(2,1)} %get-tuple-element.58), channel_id=1, source_target_pairs={{0,20},{8,28},{1,21},{9,29},{2,22},{10,30},{3,23},{11,31},{16,4},{... | collective-permute-start | bytes 737288 | tf_op jit(solution)/shard_map/ppermute | solution.py:53
  138.4 8.5 %copy-start.18 = (bf16[4,240,128]{2,1,0:T(8,128)(2,1)}, bf16[4,240,128]{2,1,0:T(8,128)(2,1)S(1)}, u32[]{:S(2)}) copy-start(bf16[4,240,128]{2,1,0:T(8,128)(2,1)S(1)} %collective-permute-done.23.refs_2_) | copy-start | bytes 737284
  141.0 5.9 %copy-start.19 = (bf16[4,240,128]{2,1,0:T(8,128)(2,1)}, bf16[4,240,128]{2,1,0:T(8,128)(2,1)S(1)}, u32[]{:S(2)}) copy-start(bf16[4,240,128]{2,1,0:T(8,128)(2,1)S(1)} %collective-permute-done.24.refs_3_) | copy-start | bytes 737284
  141.0 5.9 %copy-start.20 = (bf16[4,240,128]{2,1,0:T(8,128)(2,1)}, bf16[4,240,128]{2,1,0:T(8,128)(2,1)S(1)}, u32[]{:S(2)}) copy-start(bf16[4,240,128]{2,1,0:T(8,128)(2,1)S(1)} %collective-permute-done.25.refs_5_) | copy-start | bytes 737284
  143.0 3.9 %copy-start.21 = (bf16[4,240,128]{2,1,0:T(8,128)(2,1)}, bf16[4,240,128]{2,1,0:T(8,128)(2,1)S(1)}, u32[]{:S(2)}) copy-start(bf16[4,240,128]{2,1,0:T(8,128)(2,1)S(1)} %collective-permute-done.26.refs_6_) | copy-start | bytes 737284
  150.1 6.6 %collective-permute-start.28 = (bf16[240,128]{1,0:T(8,128)(2,1)}, bf16[240,128]{1,0:T(8,128)(2,1)S(1)}, u32[]{:S(2)}, u32[]{:S(2)}) collective-permute-start(bf16[240,128]{1,0:T(8,128)(2,1)} %get-tuple-element.60), channel_id=1, source_target_pairs={{0,16},{8,24},{1,17},{9,25},{2,18},{10,26},{3,19},{11,27},{16,0},{... | collective-permute-start | bytes 184328 | tf_op jit(solution)/shard_map/ppermute | solution.py:53
  150.1 9.4 %collective-permute-start.29 = (bf16[240,128]{1,0:T(8,128)(2,1)}, bf16[240,128]{1,0:T(8,128)(2,1)S(1)}, u32[]{:S(2)}, u32[]{:S(2)}) collective-permute-start(bf16[240,128]{1,0:T(8,128)(2,1)} %get-tuple-element.61), channel_id=1, source_target_pairs={{0,4},{8,12},{1,5},{9,13},{2,6},{10,14},{3,7},{11,15},{16,20},{24,... | collective-permute-start | bytes 184328 | tf_op jit(solution)/shard_map/ppermute | solution.py:53
  153.0 6.5 %collective-permute-start.30 = (bf16[240,128]{1,0:T(8,128)(2,1)}, bf16[240,128]{1,0:T(8,128)(2,1)S(1)}, u32[]{:S(2)}, u32[]{:S(2)}) collective-permute-start(bf16[240,128]{1,0:T(8,128)(2,1)} %get-tuple-element.62), channel_id=1, source_target_pairs={{0,20},{8,28},{1,21},{9,29},{2,22},{10,30},{3,23},{11,31},{16,4},{... | collective-permute-start | bytes 184328 | tf_op jit(solution)/shard_map/ppermute | solution.py:53
  154.8 4.7 %collective-permute-start.31 = (bf16[240,128]{1,0:T(8,128)(2,1)}, bf16[240,128]{1,0:T(8,128)(2,1)S(1)}, u32[]{:S(2)}, u32[]{:S(2)}) collective-permute-start(bf16[240,128]{1,0:T(8,128)(2,1)} %get-tuple-element.64), channel_id=1, source_target_pairs={{0,1},{8,9},{1,0},{9,8},{2,3},{10,11},{3,2},{11,10},{16,17},{24,25... | collective-permute-start | bytes 184328 | tf_op jit(solution)/shard_map/ppermute | solution.py:53
  154.8 5.9 %collective-permute-start.32 = (bf16[240,128]{1,0:T(8,128)(2,1)}, bf16[240,128]{1,0:T(8,128)(2,1)S(1)}, u32[]{:S(2)}, u32[]{:S(2)}) collective-permute-start(bf16[240,128]{1,0:T(8,128)(2,1)} %get-tuple-element.65), channel_id=1, source_target_pairs={{0,2},{8,10},{1,3},{9,11},{2,0},{10,8},{3,1},{11,9},{16,18},{24,26... | collective-permute-start | bytes 184328 | tf_op jit(solution)/shard_map/ppermute | solution.py:53
  156.7 5.7 %copy-start.23 = (bf16[240,128]{1,0:T(8,128)(2,1)}, bf16[240,128]{1,0:T(8,128)(2,1)S(1)}, u32[]{:S(2)}) copy-start(bf16[240,128]{1,0:T(8,128)(2,1)S(1)} %collective-permute-done.28.refs_1_) | copy-start | bytes 184324
  156.7 5.6 %collective-permute-start.33 = (bf16[240,128]{1,0:T(8,128)(2,1)}, bf16[240,128]{1,0:T(8,128)(2,1)S(1)}, u32[]{:S(2)}, u32[]{:S(2)}) collective-permute-start(bf16[240,128]{1,0:T(8,128)(2,1)} %get-tuple-element.66), channel_id=1, source_target_pairs={{0,3},{8,11},{1,2},{9,10},{2,1},{10,9},{3,0},{11,8},{16,19},{24,27... | collective-permute-start | bytes 184328 | tf_op jit(solution)/shard_map/ppermute | solution.py:53
  159.5 2.9 %copy-start.24 = (bf16[240,128]{1,0:T(8,128)(2,1)}, bf16[240,128]{1,0:T(8,128)(2,1)S(1)}, u32[]{:S(2)}) copy-start(bf16[240,128]{1,0:T(8,128)(2,1)S(1)} %collective-permute-done.29.refs_2_) | copy-start | bytes 184324
  159.5 2.9 %copy-start.25 = (bf16[240,128]{1,0:T(8,128)(2,1)}, bf16[240,128]{1,0:T(8,128)(2,1)S(1)}, u32[]{:S(2)}) copy-start(bf16[240,128]{1,0:T(8,128)(2,1)S(1)} %collective-permute-done.30.refs_3_) | copy-start | bytes 184324
  159.5 2.9 %copy-start.26 = (bf16[240,128]{1,0:T(8,128)(2,1)}, bf16[240,128]{1,0:T(8,128)(2,1)S(1)}, u32[]{:S(2)}) copy-start(bf16[240,128]{1,0:T(8,128)(2,1)S(1)} %collective-permute-done.31.refs_5_) | copy-start | bytes 184324
  160.7 1.7 copy-start.27
  (3 other events, 2.0 us)

commit v2 on v1

v2 whole, which is shorter than its diff:
```python
import functools

import jax
import jax.numpy as jnp
from jax import lax
from jax.experimental import pallas as pl
from jax.experimental.pallas import tpu as pltpu
from jax.sharding import PartitionSpec as P

F32 = jnp.float32
BF16 = jnp.bfloat16
EXPERTS = 4
CAPP = 4
OLD_PAGES = 192
CAP = 10
WIDTH = 768
LANES = 128
SLAB = 64
SCALAR_ROW = 30
NZ = 8
ROWS = NZ * CAP
PIECES = 3
AXES = ("attn", "sect")
MIB = 1024 * 1024


def place(z, y, x, c):
    return (z * 4 + (y % 2) * 2 + c) * 8 + (y // 2) * 4 + x


def pairs(move):
    return [
        (place(z, y, x, c), place(*move(z, y, x, c)))
        for z in range(NZ)
        for y in range(4)
        for x in range(4)
        for c in range(2)
    ]


def along_x(step):
    return pairs(lambda z, y, x, c: (z, y, x ^ step, c))


def along_y(step):
    return pairs(lambda z, y, x, c: (z, y ^ step, x, c))


OTHER_CORE = pairs(lambda z, y, x, c: (z, y, x, c ^ 1))
Z_GROUPS = [[z * 4 + r for z in range(NZ)] for r in range(4)]


def permute(value, perm):
    return lax.ppermute(value, AXES, perm)


def gather4(value, along):
    return [value] + [permute(value, along(step)) for step in (1, 2, 3)]


def in_vmem(count):
    return [pl.BlockSpec(memory_space=pltpu.VMEM)] * count


def in_hbm(count):
    return [pl.BlockSpec(memory_space=pltpu.HBM)] * count


def in_smem(count):
    return [pl.BlockSpec(memory_space=pltpu.SMEM)] * count


def params(mib):
    return pltpu.CompilerParams(vmem_limit_bytes=mib * MIB)


def iota(shape, dim):
    return lax.broadcasted_iota(jnp.int32, shape, dim)


def slab_offset(chunk):
    return jnp.where(chunk < 3, chunk * CAP, chunk * CAP + 2)


def pack_pages_kernel(owner, fresh, out, used):
    out[...] = jnp.zeros_like(out)

    def clear(o, carry):
        used[o] = 0
        return carry

    lax.fori_loop(0, used.shape[0], clear, 0)

    def put(p, carry):
        o = owner[0, p]
        k = used[o]
        out[o * CAPP + k] = fresh[p]
        used[o] = k + 1
        return carry

    lax.fori_loop(0, fresh.shape[0], put, 0, unroll=4)


def pack_pages(owners, fresh, n_attn):
    return pl.pallas_call(
        pack_pages_kernel,
        out_shape=jax.ShapeDtypeStruct((n_attn * CAPP,) + fresh.shape[1:], fresh.dtype),
        in_specs=in_smem(1) + in_vmem(1),
        out_specs=in_vmem(1)[0],
        scratch_shapes=[pltpu.SMEM((n_attn,), jnp.int32)],
        compiler_params=params(56),
        name="pack_pages",
    )(owners, fresh)


def split3(value):
    pieces = []
    for _ in range(PIECES):
        piece = value.astype(BF16).astype(F32)
        pieces.append(piece)
        value = value - piece
    return pieces


def find_places(ids, queries, select_out, places_out, heads_out):
    rows, width = queries.shape
    heads = width // LANES
    for h in range(heads):
        heads_out[pl.ds(h, rows, stride=8), :] = queries[:, h * LANES : (h + 1) * LANES].astype(F32)
    for h in range(heads, 8):
        heads_out[pl.ds(h, rows, stride=8), :] = jnp.zeros((rows, LANES), F32)
    ids_f = ids[...].astype(F32)
    cols = EXPERTS * 32
    spread = (iota((rows, cols), 1) % rows == iota((rows, cols), 0)).astype(F32)
    ids_l = jnp.dot(ids_f, spread, preferred_element_type=F32).astype(jnp.int32)
    e0, e1 = ids_l[0:1], ids_l[1:2]
    expert = iota((8, cols), 0)
    routed = ((expert == e0) | (expert == e1)).astype(F32)
    before = ((iota((cols, cols), 0) < rows) & (iota((cols, cols), 0) < iota((cols, cols), 1) % rows)).astype(F32)
    slot = jnp.dot(routed, before, preferred_element_type=F32).astype(jnp.int32)
    slot0 = jnp.sum(jnp.where(expert == e0, slot, 0), axis=0, keepdims=True)
    slot1 = jnp.sum(jnp.where(expert == e1, slot, 0), axis=0, keepdims=True)
    column = iota((1, cols), 1)
    offset = slab_offset(column // rows)
    features = column < heads * rows
    target0 = jnp.where(
        features,
        e0 * SLAB + slot0 + offset,
        jnp.where(column < (heads + 1) * rows, e0 * SLAB + SCALAR_ROW, -1),
    )
    target1 = jnp.where(
        features,
        e1 * SLAB + slot1 + offset,
        jnp.where(column < (heads + 1) * rows, -1, e1 * SLAB + SCALAR_ROW),
    )
    at = iota((EXPERTS * SLAB, cols), 0)
    select_out[...] = ((at == target0) | (at == target1)).astype(F32).astype(BF16)

    diagonal = (iota((rows, cols), 1) == iota((rows, cols), 0)).astype(F32)
    for i, value in enumerate((e0, e1, slot0, slot1)):
        column_of = jnp.sum(diagonal * value.astype(F32), axis=1, keepdims=True)
        places_out[i * rows : (i + 1) * rows, :] = jnp.broadcast_to(
            column_of.astype(jnp.int32), (rows, LANES)
        )


def attend_kernel(
    table,
    lengths,
    *refs,
):
    in_hbm_refs = refs[:8]
    kv_out, hidden_out, payload = refs[8:11]
    pool, heads_v, stream, gain, router, select, places, scores_v, o_scr, sems = refs[11:]
    kv_pool, arrived = in_hbm_refs[:2]
    rows, width = stream.shape
    heads = width // LANES
    pages = table.shape[1]
    fresh = pl.ds(OLD_PAGES, arrived.shape[0])
    kept = pl.ds(0, OLD_PAGES)
    loads = [
        pltpu.make_async_copy(source, target, sems.at[i])
        for i, (source, target) in enumerate(
            [
                (kv_pool.at[kept], pool.at[kept]),
                (arrived, pool.at[fresh]),
                (in_hbm_refs[2], heads_v),
                (in_hbm_refs[3], stream),
                (in_hbm_refs[4], gain),
                (in_hbm_refs[5], router),
                (in_hbm_refs[6], select),
                (in_hbm_refs[7], places),
            ]
        )
    ]
    for load in loads:
        load.start()
    for load in loads[:3]:
        load.wait()
    store = pltpu.make_async_copy(pool, kv_out, sems.at[8])
    store.start()
    scale = float(LANES) ** (-0.5)
    length = jnp.concatenate(
        [jnp.full((8, 1), lengths[0, r], jnp.int32) for r in range(rows)], axis=0
    )
    for r in range(rows):
        keys = jnp.concatenate([pool[table[r, p], :, :LANES] for p in range(pages)], axis=0)
        query = heads_v[r * 8 : (r + 1) * 8, :]
        query = jnp.concatenate([query, query], axis=0).astype(BF16)
        scores = lax.dot_general(query, keys, (((1,), (1,)), ((), ())), preferred_element_type=F32)
        scores_v[r * 8 : (r + 1) * 8, :] = scores[:8]
    scores = scores_v[...] * scale
    valid = iota(scores.shape, 1) < length
    masked = jnp.where(valid, scores, -1e30)
    top = jnp.max(masked, axis=1, keepdims=True)
    weights = jnp.where(valid, jnp.exp(masked - top), 0.0)
    total = jnp.sum(weights, axis=1, keepdims=True)
    scores_v[...] = weights
    for r in range(rows):
        values = jnp.concatenate([pool[table[r, p], :, LANES:] for p in range(pages)], axis=0)
        weight = scores_v[r * 8 : (r + 1) * 8, :]
        weight = jnp.concatenate([weight, weight], axis=0).astype(BF16)
        o_scr[r * 8 : (r + 1) * 8, :] = jnp.dot(weight, values, preferred_element_type=F32)[:8]
    o_scr[...] = o_scr[...] / total
    for load in loads[3:]:
        load.wait()
    attended = jnp.concatenate([o_scr[pl.ds(h, rows, stride=8), :] for h in range(heads)], axis=1)
    hidden = (stream[...].astype(F32) + attended).astype(BF16)
    hidden_out[...] = hidden
    hidden_f = hidden.astype(F32)
    squares = jnp.sum(hidden_f * hidden_f, axis=1, keepdims=True)
    gained = (hidden_f * gain[...].astype(F32)).astype(BF16)
    logits = lax.dot_general(gained, router[...], (((1,), (1,)), ((), ())), preferred_element_type=F32)
    expert_r = iota(logits.shape, 1)
    c0, c1, slot_c0, slot_c1 = [places[i * rows : (i + 1) * rows, :] for i in range(4)]
    delta = jnp.sum(
        jnp.where(expert_r == c0[:, :EXPERTS], logits, 0.0)
        - jnp.where(expert_r == c1[:, :EXPERTS], logits, 0.0),
        axis=1,
        keepdims=True,
    )
    lane = iota((rows, LANES), 1)

    def scalars(slots, difference):
        total = jnp.zeros((rows, LANES), F32)
        for i, piece in enumerate(split3(squares) + split3(difference)):
            total = total + jnp.where(lane == i * CAP + slots, piece, 0.0)
        return total.astype(BF16)

    parts = [gained[:, h * LANES : (h + 1) * LANES] for h in range(heads)]
    parts += [scalars(slot_c0, delta), scalars(slot_c1, -delta)]
    stacked = jnp.concatenate(parts, axis=0)
    slabs = jnp.dot(select[...], stacked, preferred_element_type=F32).astype(BF16)
    for e in range(EXPERTS):
        slab = slabs[e * SLAB : (e + 1) * SLAB]
        payload[2 * e] = slab
        payload[2 * e + 1] = slab
    store.wait()


def attend(table, lengths, kv_pool, arrived, heads, stream, gain, router, select, places):
    rows, width = stream.shape
    shape = jax.ShapeDtypeStruct
    return pl.pallas_call(
        attend_kernel,
        out_shape=(
            shape(kv_pool.shape, kv_pool.dtype),
            shape((rows, width), BF16),
            shape((NZ, SLAB, LANES), BF16),
        ),
        in_specs=in_smem(2) + in_hbm(1) + in_vmem(1) + in_hbm(6),
        out_specs=tuple(in_hbm(1) + in_vmem(2)),
        scratch_shapes=[
            pltpu.VMEM(kv_pool.shape, kv_pool.dtype),
            pltpu.VMEM(heads.shape, F32),
            pltpu.VMEM(stream.shape, BF16),
            pltpu.VMEM(gain.shape, BF16),
            pltpu.VMEM(router.shape, BF16),
            pltpu.VMEM(select.shape, BF16),
            pltpu.VMEM(places.shape, jnp.int32),
            pltpu.VMEM((rows * 8, table.shape[1] * kv_pool.shape[1]), F32),
            pltpu.VMEM((rows * 8, LANES), F32),
            pltpu.SemaphoreType.DMA((9,)),
        ],
        compiler_params=params(56),
        name="attend",
    )(table, lengths, kv_pool, arrived, heads, stream, gain, router, select, places)


def prepare_kernel(where, w_gate, w_up, w_down, ids, queries, *refs):
    made, places, blocks, sems = refs[:6], refs[6:9], refs[9:15], refs[15]
    pieces = []
    for n in range(4):
        x = jnp.bitwise_xor(where[1], n)
        for h in range(2):
            at = pl.ds(pl.multiple_of((h * 4 + x) * WIDTH, WIDTH), WIDTH)
            to = pl.ds(h * WIDTH, WIDTH)
            pieces.append((n, w_gate.at[at, :], blocks[n].at[to, pl.ds(0, LANES)]))
            pieces.append((n, w_up.at[at, :], blocks[n].at[to, pl.ds(LANES, LANES)]))
    for hm in range(2):
        h = jnp.bitwise_xor(where[0], hm)
        for pair in range(12):
            start = pl.multiple_of(h * 4 * WIDTH + pair * 2 * LANES, 2 * LANES)
            to = pl.ds(pair * LANES, LANES)
            pieces.append((4 + hm, w_down.at[:, pl.ds(start, 2 * LANES)], blocks[4 + hm].at[to, :]))
    loads = [
        (n, pltpu.make_async_copy(source, target, sems.at[i]))
        for i, (n, source, target) in enumerate(pieces)
    ]
    for _, load in loads:
        load.start()
    stores = []
    for n in range(6):
        for block, load in loads:
            if block == n:
                load.wait()
        stores.append(pltpu.make_async_copy(blocks[n], made[n], sems.at[40 + n]))
        stores[n].start()
    find_places(ids, queries, *places)
    for store in stores:
        store.wait()


def prepare(where, w_gate, w_up, w_down, ids, queries):
    rows = queries.shape[0]
    block = (2 * WIDTH, 2 * LANES)
    shape = jax.ShapeDtypeStruct
    return pl.pallas_call(
        prepare_kernel,
        out_shape=(shape(block, BF16),) * 6
        + (
            shape((EXPERTS * SLAB, LANES), BF16),
            shape((4 * rows, LANES), jnp.int32),
            shape((rows * 8, LANES), F32),
        ),
        in_specs=in_smem(1) + in_hbm(3) + in_vmem(2),
        out_specs=tuple(in_hbm(6) + in_vmem(3)),
        scratch_shapes=[pltpu.VMEM(block, BF16)] * 6 + [pltpu.SemaphoreType.DMA((46,))],
        compiler_params=params(56),
        name="prepare",
    )(where, w_gate, w_up, w_down, ids, queries)


def to_rows_kernel(slabs, out):
    count = NZ * SLAB
    to, at = iota((count, count), 0), iota((count, count), 1)
    row = to // NZ
    row = jnp.where(row < 3 * CAP, row, row + 2)
    row = jnp.where(row >= SLAB - 2, SCALAR_ROW, row)
    select = ((to % NZ) * SLAB + row == at).astype(F32).astype(BF16)
    flat = slabs[...].reshape(count, LANES)
    out[...] = jnp.dot(select, flat, preferred_element_type=F32).astype(BF16)[: out.shape[0]]


def to_rows(slabs):
    return pl.pallas_call(
        to_rows_kernel,
        out_shape=jax.ShapeDtypeStruct((6 * ROWS + 16, LANES), BF16),
        in_specs=in_vmem(1),
        out_specs=in_vmem(1)[0],
        compiler_params=params(16),
        name="to_rows",
    )(slabs)


BLOCKS = [(c, g) for c in range(2) for g in range(2)]
PART_ROWS = 4 * ROWS + 4 * NZ


def gate_up_kernel(where, *refs):
    rows = (refs[0:4], refs[4:8])
    weights = refs[8:12]
    outs = refs[14:18]
    left = []
    for hm in range(2):
        for chunk in range(6):
            at = slice(chunk * ROWS, (chunk + 1) * ROWS)
            left.append(jnp.concatenate([rows[c][2 * hm + g][at, :] for c, g in BLOCKS], axis=0))
    left = [jnp.concatenate(left[6 * hm : 6 * hm + 6], axis=1) for hm in range(2)]
    scalars = []
    for hm in range(2):
        at = slice(6 * ROWS, 6 * ROWS + 16)
        scalars.append(
            jnp.concatenate([rows[c][2 * hm + g][at, :].astype(F32)[:NZ] for c, g in BLOCKS], axis=0)
        )
    scalars = jnp.concatenate(scalars, axis=1)
    for n in range(4):
        parts = []
        for hm in range(2):
            h = jnp.bitwise_xor(where[0], hm)
            at = pl.ds(pl.multiple_of(h * WIDTH, WIDTH), WIDTH)
            parts.append(jnp.dot(left[hm], weights[n][at, :], preferred_element_type=F32))
        total = parts[0] + parts[1]
        outs[n][: 4 * ROWS, :] = total.astype(outs[n].dtype)
        outs[n][4 * ROWS :, :] = scalars.astype(outs[n].dtype)


def gate_up(where, own, other, weights, later):
    out = jax.ShapeDtypeStruct((PART_ROWS, 2 * LANES), BF16)
    return pl.pallas_call(
        gate_up_kernel,
        out_shape=(jax.ShapeDtypeStruct(out.shape, F32), out, out, out),
        in_specs=in_smem(1) + in_vmem(12) + in_hbm(2),
        out_specs=tuple(in_vmem(4)),
        compiler_params=params(24),
        name="gate_up",
    )(where, *own, *other, *weights, *later)


def activate_kernel(*refs):
    outs = refs[4:6]
    for i, (c, g) in enumerate(BLOCKS):
        sums = jnp.zeros((NZ, 2 * LANES), F32)
        for ref in refs[:4]:
            sums = sums + ref[4 * ROWS :, :].astype(F32)[i * NZ : (i + 1) * NZ]
        sums = sums[:, :LANES] + sums[:, LANES:]

        def scalar(first):
            return sum(
                sums[:, (first + p) * CAP : (first + p + 1) * CAP] for p in range(PIECES)
            )

        inverse = lax.rsqrt(scalar(0) / (WIDTH * 8) + 1e-05)
        gate = 1.0 / (1.0 + jnp.exp(-scalar(PIECES) * inverse))
        at = slice(i * ROWS, (i + 1) * ROWS)
        part = (refs[0][at, :] + refs[1][at, :].astype(F32)) + (
            refs[2][at, :].astype(F32) + refs[3][at, :].astype(F32)
        )
        active = []
        for k in range(CAP):
            rows = part[k * NZ : (k + 1) * NZ] * inverse[:, k : k + 1]
            v, up = rows[:, :LANES], rows[:, LANES:]
            active.append(v / (1.0 + jnp.exp(-v)) * up * gate[:, k : k + 1])
        outs[g][c * ROWS : (c + 1) * ROWS, :] = jnp.concatenate(active, axis=0).astype(BF16)


def activate(parts):
    out = jax.ShapeDtypeStruct((2 * ROWS, LANES), BF16)
    return pl.pallas_call(
        activate_kernel,
        out_shape=(out, out),
        in_specs=in_vmem(4),
        out_specs=tuple(in_vmem(2)),
        compiler_params=params(8),
        name="activate",
    )(*parts)


def down_kernel(where, *refs):
    active, weights, outs = refs[0:4], refs[4:8], refs[8:10]
    left = jnp.concatenate([ref[...] for ref in active], axis=1)
    for n in range(4):
        x = jnp.bitwise_xor(where[1], n)
        for pair in range(3):
            at = pl.ds(pl.multiple_of((x * 3 + pair) * LANES, LANES), LANES)
            right = jnp.concatenate([ref[at, :] for ref in weights], axis=0)
            made = jnp.dot(left, right, preferred_element_type=F32).astype(BF16)
            for c in range(2):
                for half in range(2):
                    chunk = 2 * pair + half
                    outs[c][n, chunk * ROWS : (chunk + 1) * ROWS, :] = made[
                        c * ROWS : (c + 1) * ROWS, half * LANES : (half + 1) * LANES
                    ]


def down(where, active, weights):
    out = jax.ShapeDtypeStruct((4, 6 * ROWS, LANES), BF16)
    return pl.pallas_call(
        down_kernel,
        out_shape=(out, out),
        in_specs=in_smem(1) + in_vmem(8),
        out_specs=tuple(in_vmem(2)),
        compiler_params=params(16),
        name="down",
    )(where, *active, *weights)


def add_cores_kernel(own, other, *outs):
    for m in range(4):
        outs[m][...] = (own[m].astype(F32) + other[m].astype(F32)).astype(BF16)


def add_cores(own, other):
    out = jax.ShapeDtypeStruct(own.shape[1:], BF16)
    return pl.pallas_call(
        add_cores_kernel,
        out_shape=(out,) * 4,
        in_specs=in_vmem(2),
        out_specs=tuple(in_vmem(4)),
        compiler_params=params(8),
        name="add_cores",
    )(own, other)


def to_slabs_kernel(*refs):
    count = NZ * SLAB
    summed = (refs[0][...].astype(F32) + refs[1][...].astype(F32)) + (
        refs[2][...].astype(F32) + refs[3][...].astype(F32)
    )
    to, at = iota((count, 6 * ROWS), 0), iota((count, 6 * ROWS), 1)
    row = jnp.where(at < 3 * ROWS, at // NZ, at // NZ + 2)
    select = ((at % NZ) * SLAB + row == to).astype(F32).astype(BF16)
    moved = jnp.dot(select, summed.astype(BF16), preferred_element_type=F32).astype(BF16)
    refs[4][...] = moved.reshape(NZ, SLAB, LANES)


def to_slabs(parts):
    return pl.pallas_call(
        to_slabs_kernel,
        out_shape=jax.ShapeDtypeStruct((NZ, SLAB, LANES), BF16),
        in_specs=in_vmem(4),
        out_specs=in_vmem(1)[0],
        compiler_params=params(8),
        name="to_slabs",
    )(*parts)


def combine_kernel(slabs, hidden, select, mixed):
    rows, width = hidden.shape
    total = jnp.zeros((LANES, LANES), F32)
    for half in range(2):
        flat = jnp.concatenate([slabs[2 * e + half] for e in range(EXPERTS)], axis=0)
        total = total + lax.dot_general(
            select[...], flat, (((0,), (0,)), ((), ())), preferred_element_type=F32
        )
    blended = jnp.concatenate(
        [total[h * rows : (h + 1) * rows] for h in range(width // LANES)], axis=1
    )
    mixed[...] = (hidden[...].astype(F32) + blended).astype(BF16)


def combine(slabs, hidden, select):
    return pl.pallas_call(
        combine_kernel,
        out_shape=jax.ShapeDtypeStruct(hidden.shape, BF16),
        in_specs=in_vmem(3),
        out_specs=in_vmem(1)[0],
        compiler_params=params(16),
        name="combine",
    )(slabs, hidden, select)


def exchange_z(slabs):
    return lax.all_to_all(slabs, "attn", 0, 0, axis_index_groups=Z_GROUPS, tiled=True)


def on_device(
    queries,
    stream,
    kv_pool,
    fresh_kv,
    fresh_owner,
    page_table,
    lengths,
    norm_gain,
    router,
    expert_ids,
    w_gate,
    w_up,
    w_down,
):
    n_attn = lax.axis_size("attn")
    pages, kv_local, page_len, page_width = kv_pool.shape
    sect = lax.axis_index("sect")
    where = jnp.stack([sect // 4, sect % 4]).astype(jnp.int32)

    *blocks, select, places, heads = prepare(
        where, w_gate, w_up, w_down, expert_ids.T, queries
    )
    first = [blocks[0]] + [permute(blocks[n], along_x(n)) for n in (1, 2, 3)]
    second = [permute(blocks[5], along_y(m)) for m in (2, 3)]
    outgoing = pack_pages(fresh_owner.T, fresh_kv.reshape(-1, page_len, page_width), n_attn)
    arrived = lax.all_to_all(outgoing, "attn", 0, 0, tiled=True)
    kv_out, hidden, payload = attend(
        page_table,
        lengths,
        kv_pool.reshape(pages, page_len, page_width),
        arrived,
        heads,
        stream,
        norm_gain.reshape(1, -1),
        router.T,
        select,
        places,
    )

    near, payload = lax.optimization_barrier((blocks[4], payload))
    second = [blocks[4], permute(near, along_y(1))] + second

    own = gather4(to_rows(exchange_z(payload)), along_y)
    other = [permute(v, OTHER_CORE) for v in own]
    parts = gate_up(where, own, other, first, second[2:])
    active = activate([parts[0]] + [permute(parts[n], along_x(n)) for n in (1, 2, 3)])
    active = [active[0]] + [permute(active[m % 2], along_y(m)) for m in (1, 2, 3)]
    made, for_other = down(where, active, second)
    sums = add_cores(made, permute(for_other, OTHER_CORE))
    slabs = to_slabs([sums[0]] + [permute(sums[n], along_x(n)) for n in (1, 2, 3)])
    mixed = combine(exchange_z(slabs), hidden, select)
    return (mixed, kv_out.reshape(kv_pool.shape))


def solution(mesh):
    return jax.shard_map(
        on_device,
        mesh=mesh,
        in_specs=(
            P("attn", "sect"),
            P("attn", "sect"),
            P("attn", "sect", None, None),
            P("attn", "sect", None, None),
            P("attn", None),
            P("attn", None),
            P("attn", None),
            P("sect"),
            P("sect", None),
            P("attn", None),
            P(None, ("attn", "sect")),
            P(None, ("attn", "sect")),
            P(("attn", "sect"), None),
        ),
        out_specs=(P("attn", "sect"), P("attn", "sect", None, None)),
        check_vma=False,
    )
```

time: 181 us -> 131 us (0.72)
  waiting for transfers between devices: 67.4 us -> 43.7 us
  Pallas kernels: 31 us -> 18.9 us
  local copies, waits for them, and re-layouts: 9.27 us -> 0.62 us
  starting transfers between devices: 44.4 us -> 38.4 us
    all_to_all x1, waiting for transfers between devices: 27 us -> 13.3 us  [on_device(): arrived = lax.all_to_all(outgoing, 'attn', 0, 0, tiled=True)]
    ppermute x34 -> x23, waiting for transfers between devices: 40.4 us -> 30.4 us  [permute(): return lax.ppermute(value, AXES, perm)]
    pallas_call x5 -> x7, Pallas kernels: 24.8 us -> 15.3 us  [the longest x1 5.91 us: prepare(): pl.pallas_call(prepare_kernel, out_shape=(shape(block, BF16),) * 6 + (sha...]
    unnamed x72 -> x12, local copies, waits for them, and re-layouts: 8.65 us -> 0.03 us
    ppermute x34 -> x23, starting transfers between devices: 34.5 us -> 28.4 us  [permute(): return lax.ppermute(value, AXES, perm)]
  transfers between devices with their start and end apart: 35 -> 24, of which waited for: 16 -> 14; matrix products, arithmetic and copies ran while one was open for 2% -> 1% of each run, Pallas kernels for 0% -> 11%
where the time goes in v2:
time: 131 us; the launch traced here: 130 us
  waiting for transfers between devices  43.7 us (33%)
  starting transfers between devices  38.4 us (29%)
  blocking collectives  27.2 us (21%)
  Pallas kernels  18.9 us (14%)
    ppermute x23, waiting for transfers between devices, permute(): return lax.ppermute(value, AXES, perm)  30.4 us
    ppermute x23, starting transfers between devices, permute(): return lax.ppermute(value, AXES, perm)  28.4 us
    all_to_all x2, blocking collectives, exchange_z(): lax.all_to_all(slabs, 'attn', 0, 0, axis_index_groups=Z_GROUPS, tiled=True)  27.2 us
    all_to_all x1, waiting for transfers between devices, on_device(): arrived = lax.all_to_all(outgoing, 'attn', 0, 0, tiled=True)  13.3 us
    all_to_all x1, starting transfers between devices, on_device(): arrived = lax.all_to_all(outgoing, 'attn', 0, 0, tiled=True)  9.99 us
    pallas_call x1, Pallas kernels, prepare(): pl.pallas_call(prepare_kernel, out_shape=(shape(block, BF16),) * 6 + (sha...  5.91 us
    pallas_call x1, Pallas kernels, attend(): pl.pallas_call(attend_kernel, out_shape=(shape(kv_pool.shape, kv_pool.dty...  5.12 us
  transfers between devices with their start and end apart: 24, of which 14 were waited for; matrix products, arithmetic and copies ran while one was open for 1% of the time, Pallas kernels for 11%

profile of v2, /device:TPU:6, one launch (start us, length us, event | category | flops | bytes accessed | tf_op | source)
XLA Modules:
  0.0 130.2 jit_solution(3129298018275876326)
XLA Ops:
  0.6 2.4 %pack_pages.1 = bf16[128,16,256]{2,1,0:T(8,128)(2,1)} custom-call(s32[1,32]{1,0:T(1,128)} %bitcast.14, bf16[32,16,256]{2,1,0:T(8,128)(2,1)} %bitcast.11), custom_call_target="tpu_custom_call" | custom-call | tf_op jit(solution)/shard_map/pack_pages/pallas_call | solution.py:105
  3.0 10.0 %all-to-all-start = ((bf16[128,16,256]{2,1,0:T(8,128)(2,1)}), bf16[128,16,256]{2,1,0:T(8,128)(2,1)}, u32[]{:S(2)}, u32[]{:S(2)}) async-start(bf16[128,16,256]{2,1,0:T(8,128)(2,1)} %pack_pages.1), calls=%async_computation | async-start | bytes 2097152 | tf_op jit(solution)/shard_map/all_to_all | solution.py:573
  13.0 0.7 pad_add_fusion.where
  13.7 5.9 %prepare.1 = (bf16[1536,256]{1,0:T(8,128)(2,1)}, bf16[1536,256]{1,0:T(8,128)(2,1)}, bf16[1536,256]{1,0:T(8,128)(2,1)}, bf16[1536,256]{1,0:T(8,128)(2,1)}, bf16[1...) custom-call(s32[2]{0:T(128)} %pad_add_fusion.where, ...), custom_call_target="tpu_custom_call" | custom-call | tf_op jit(solution)/shard_map/prepare/pallas_call | solution.py:328
  19.6 0.9 collective-permute-start.7
  20.5 1.1 collective-permute-start.8
  21.6 2.8 %collective-permute-start.9 = (bf16[1536,256]{1,0:T(8,128)(2,1)}, bf16[1536,256]{1,0:T(8,128)(2,1)}, u32[]{:S(2)}, u32[]{:S(2)}) collective-permute-start(bf16[1536,256]{1,0:T(8,128)(2,1)} %get-tuple-element.37), channel_id=1, source_target_pairs={{0,3},{8,11},{1,2},{9,10},{2,1},{10,9},{3,0},{11,8},{16,19},{24,27... | collective-permute-start | bytes 2359304 | tf_op jit(solution)/shard_map/ppermute | solution.py:54
  24.4 3.2 %collective-permute-start.11 = (bf16[1536,256]{1,0:T(8,128)(2,1)}, bf16[1536,256]{1,0:T(8,128)(2,1)S(1)}, u32[]{:S(2)}, u32[]{:S(2)}) collective-permute-start(bf16[1536,256]{1,0:T(8,128)(2,1)} %get-tuple-element.38), channel_id=1, source_target_pairs={{0,20},{8,28},{1,21},{9,29},{2,22},{10,30},{3,23},{11,31},{16,4},{... | collective-permute-start | bytes 2359304 | tf_op jit(solution)/shard_map/ppermute | solution.py:54
  27.5 0.6 collective-permute-start.10
  28.2 0.6 reshape.18.refs_4_
  28.8 13.3 %all-to-all-done.refs_1_ = bf16[128,16,256]{2,1,0:T(8,128)(2,1)} async-done(((bf16[128,16,256]{2,1,0:T(8,128)(2,1)}), bf16[128,16,256]{2,1,0:T(8,128)(2,1)}, u32[]{:S(2)}, u32[]{:S(2)}) %all-to-all-start) | async-done | bytes 1048608 | tf_op jit(solution)/shard_map/all_to_all | solution.py:573
  42.1 5.1 %attend.1 = (bf16[320,16,256]{2,1,0:T(8,128)(2,1)}, bf16[16,768]{1,0:T(8,128)(2,1)}, bf16[8,64,128]{2,1,0:T(8,128)(2,1)}) custom-call(s32[16,16]{1,0:T(8,128)} %table.1, s32[1,16]{1,0:T(1,128)} %lengths.1, bf16[320,16,256]{2,1,0:T(8,128)(2,1)} %bitcast.10, bf16[128,16,256]{2,1,0:T(8,128)(2,1)} %all-to-all-done.refs_1_, ...), custom_call_target="tpu_custom_call" | custom-call | tf_op jit(solution)/shard_map/attend/pallas_call | solution.py:264
  47.2 0.0 collective-permute-done.7.refs_9_
  47.2 1.7 %collective-permute-start.18 = (bf16[1536,256]{1,0:T(8,128)(2,1)S(1)}, bf16[1536,256]{1,0:T(8,128)(2,1)S(1)}, u32[]{:S(2)}, u32[]{:S(2)}) collective-permute-start(bf16[1536,256]{1,0:T(8,128)(2,1)S(1)} %copy-done), channel_id=1, source_target_pairs={{0,16},{8,24},{1,17},{9,25},{2,18},{10,26},{3,19},{11,27},{16,0},{... | collective-permute-start | bytes 2359304 | tf_op jit(solution)/shard_map/ppermute | solution.py:54
  48.9 12.3 %all_to_all.15.slabs = bf16[8,64,128]{2,1,0:T(8,128)(2,1)S(1)} all-to-all(bf16[8,64,128]{2,1,0:T(8,128)(2,1)} %get-tuple-element.33), channel_id=1, replica_groups={{0,32,64,96,128,160,192,224},{8,40,72,104,136,168,200,232},{16,48,80,11..., dimensions={0} | all-to-all | bytes 262144 | tf_op jit(solution)/shard_map/all_to_all | solution.py:544
  61.3 0.3 to_rows.1.refs_0_
  61.6 0.0 collective-permute-done.8.refs_10_
  61.6 1.9 %collective-permute-start.2 = (bf16[496,128]{1,0:T(8,128)(2,1)S(1)}, bf16[496,128]{1,0:T(8,128)(2,1)S(1)}, u32[]{:S(2)}, u32[]{:S(2)}) collective-permute-start(bf16[496,128]{1,0:T(8,128)(2,1)S(1)} %to_rows.1.refs_0_), channel_id=1, source_target_pairs={{0,20},{8,28},{1,21},{9,29},{2,22},{10,30},{3,23},{11,31},{16,4},{... | collective-permute-start | bytes 380936 | tf_op jit(solution)/shard_map/ppermute | solution.py:54
  63.5 0.0 collective-permute-done.9.refs_11_
  63.5 1.2 collective-permute-start.1
  64.7 0.0 collective-permute-done.11.refs_13_.refs_7_
  64.7 1.1 collective-permute-start
  65.8 0.0 collective-permute-done.10.refs_12_.refs_6_
  65.8 0.0 collective-permute-start.3
  65.8 2.3 %collective-permute-done.2.refs_3_ = bf16[496,128]{1,0:T(8,128)(2,1)S(1)} collective-permute-done((bf16[496,128]{1,0:T(8,128)(2,1)S(1)}, bf16[496,128]{1,0:T(8,128)(2,1)S(1)}, u32[]{:S(2)}, u32[]{:S(2)}) %collective-permute-start.2) | collective-permute-done | bytes 127008 | tf_op jit(solution)/shard_map/ppermute | solution.py:54
  68.1 0.0 collective-permute-start.6
  68.1 4.9 %collective-permute-done.1.refs_2_ = bf16[496,128]{1,0:T(8,128)(2,1)S(1)} collective-permute-done((bf16[496,128]{1,0:T(8,128)(2,1)S(1)}, bf16[496,128]{1,0:T(8,128)(2,1)S(1)}, u32[]{:S(2)}, u32[]{:S(2)}) %collective-permute-start.1) | collective-permute-done | bytes 127008 | tf_op jit(solution)/shard_map/ppermute | solution.py:54
  73.0 0.0 collective-permute-start.5
  73.0 0.0 collective-permute-done.refs_1_
  73.0 0.5 collective-permute-start.4
  73.5 0.0 collective-permute-done.3.refs_4_
  73.5 0.0 collective-permute-done.6.refs_7_
  73.5 0.8 collective-permute-done.5.refs_6_
  74.4 0.2 collective-permute-done.4.refs_5_
  74.5 0.0 copy-done.4
  74.5 2.3 %gate_up.1 = (f32[352,256]{1,0:T(8,128)S(1)}, bf16[352,256]{1,0:T(8,128)(2,1)S(1)}, bf16[352,256]{1,0:T(8,128)(2,1)S(1)}, bf16[352,256]{1,0:T(8,128)(2,1)S(1)}) custom-call(s32[2]{0:T(128)S(1)} %copy-done.4, bf16[496,128]{1,0:T(8,128)(2,1)S(1)} %to_rows.1.refs_0_, bf16[496,128]{1,0:T(8,128)(2,1)S(1)} %collective-permute-done.refs_1_, ...), custom_call_target="tpu_custom_call" | custom-call | tf_op jit(solution)/shard_map/gate_up/pallas_call | solution.py:400
  76.9 0.7 collective-permute-start.12
  77.6 1.3 %collective-permute-start.13 = (bf16[352,256]{1,0:T(8,128)(2,1)S(1)}, bf16[352,256]{1,0:T(8,128)(2,1)S(1)}, u32[]{:S(2)}, u32[]{:S(2)}) collective-permute-start(bf16[352,256]{1,0:T(8,128)(2,1)S(1)} %get-tuple-element.41), channel_id=1, source_target_pairs={{0,2},{8,10},{1,3},{9,11},{2,0},{10,8},{3,1},{11,9},{16,18},{24,26... | collective-permute-start | bytes 540680 | tf_op jit(solution)/shard_map/ppermute | solution.py:54
  78.9 2.8 %collective-permute-start.14 = (bf16[352,256]{1,0:T(8,128)(2,1)S(1)}, bf16[352,256]{1,0:T(8,128)(2,1)S(1)}, u32[]{:S(2)}, u32[]{:S(2)}) collective-permute-start(bf16[352,256]{1,0:T(8,128)(2,1)S(1)} %get-tuple-element.42), channel_id=1, source_target_pairs={{0,3},{8,11},{1,2},{9,10},{2,1},{10,9},{3,0},{11,8},{16,19},{24,27... | collective-permute-start | bytes 540680 | tf_op jit(solution)/shard_map/ppermute | solution.py:54
  81.7 2.7 %collective-permute-done.12.refs_1_ = bf16[352,256]{1,0:T(8,128)(2,1)S(1)} collective-permute-done((bf16[352,256]{1,0:T(8,128)(2,1)S(1)}, bf16[352,256]{1,0:T(8,128)(2,1)S(1)}, u32[]{:S(2)}, u32[]{:S(2)}) %collective-permute-start.12) | collective-permute-done | bytes 180256 | tf_op jit(solution)/shard_map/ppermute | solution.py:54
  84.3 3.3 %collective-permute-done.13.refs_2_ = bf16[352,256]{1,0:T(8,128)(2,1)S(1)} collective-permute-done((bf16[352,256]{1,0:T(8,128)(2,1)S(1)}, bf16[352,256]{1,0:T(8,128)(2,1)S(1)}, u32[]{:S(2)}, u32[]{:S(2)}) %collective-permute-start.13) | collective-permute-done | bytes 180256 | tf_op jit(solution)/shard_map/ppermute | solution.py:54
  87.6 2.6 %collective-permute-done.14.refs_3_ = bf16[352,256]{1,0:T(8,128)(2,1)S(1)} collective-permute-done((bf16[352,256]{1,0:T(8,128)(2,1)S(1)}, bf16[352,256]{1,0:T(8,128)(2,1)S(1)}, u32[]{:S(2)}, u32[]{:S(2)}) %collective-permute-start.14) | collective-permute-done | bytes 180256 | tf_op jit(solution)/shard_map/ppermute | solution.py:54
  90.2 0.3 activate.1
  90.5 2.6 %collective-permute-start.16 = (bf16[160,128]{1,0:T(8,128)(2,1)S(1)}, bf16[160,128]{1,0:T(8,128)(2,1)S(1)}, u32[]{:S(2)}, u32[]{:S(2)}) collective-permute-start(bf16[160,128]{1,0:T(8,128)(2,1)S(1)} %get-tuple-element.43.refs_0_), channel_id=1, source_target_pairs={{0,4},{8,12},{1,5},{9,13},{2,6},{10,14},{3,7},{11,15},{16,20},{24,... | collective-permute-start | bytes 122888 | tf_op jit(solution)/shard_map/ppermute | solution.py:54
  93.1 0.9 collective-permute-start.17
  94.0 0.2 collective-permute-start.15
  94.3 2.1 %collective-permute-done.16.refs_2_ = bf16[160,128]{1,0:T(8,128)(2,1)S(1)} collective-permute-done((bf16[160,128]{1,0:T(8,128)(2,1)S(1)}, bf16[160,128]{1,0:T(8,128)(2,1)S(1)}, u32[]{:S(2)}, u32[]{:S(2)}) %collective-permute-start.16) | collective-permute-done | bytes 40992 | tf_op jit(solution)/shard_map/ppermute | solution.py:54
  96.4 1.9 %collective-permute-done.17.refs_3_ = bf16[160,128]{1,0:T(8,128)(2,1)S(1)} collective-permute-done((bf16[160,128]{1,0:T(8,128)(2,1)S(1)}, bf16[160,128]{1,0:T(8,128)(2,1)S(1)}, u32[]{:S(2)}, u32[]{:S(2)}) %collective-permute-start.17) | collective-permute-done | bytes 40992 | tf_op jit(solution)/shard_map/ppermute | solution.py:54
  98.3 0.0 collective-permute-done.15.refs_1_
  98.3 0.0 collective-permute-done.18.refs_5_
  98.3 1.2 down.1
  99.6 0.0 copy-start.3
  99.6 0.1 collective-permute-start.19
  99.7 1.9 %collective-permute-done.19.other = bf16[4,480,128]{2,1,0:T(8,128)(2,1)S(1)} collective-permute-done((bf16[4,480,128]{2,1,0:T(8,128)(2,1)S(1)}, bf16[4,480,128]{2,1,0:T(8,128)(2,1)S(1)}, u32[]{:S(2)}, u32[]{:S(2)}) %collective-permute-start.19) | collective-permute-done | bytes 491552 | tf_op jit(solution)/shard_map/ppermute | solution.py:54
  101.6 0.1 add_cores.1
  101.7 0.1 collective-permute-start.20
  101.8 4.2 %collective-permute-start.21 = (bf16[480,128]{1,0:T(8,128)(2,1)S(1)}, bf16[480,128]{1,0:T(8,128)(2,1)S(1)}, u32[]{:S(2)}, u32[]{:S(2)}) collective-permute-start(bf16[480,128]{1,0:T(8,128)(2,1)S(1)} %get-tuple-element.50), channel_id=1, source_target_pairs={{0,2},{8,10},{1,3},{9,11},{2,0},{10,8},{3,1},{11,9},{16,18},{24,26... | collective-permute-start | bytes 368648 | tf_op jit(solution)/shard_map/ppermute | solution.py:54
  106.0 0.5 collective-permute-start.22
  106.5 1.5 %collective-permute-done.20.refs_1_ = bf16[480,128]{1,0:T(8,128)(2,1)S(1)} collective-permute-done((bf16[480,128]{1,0:T(8,128)(2,1)S(1)}, bf16[480,128]{1,0:T(8,128)(2,1)S(1)}, u32[]{:S(2)}, u32[]{:S(2)}) %collective-permute-start.20) | collective-permute-done | bytes 122912 | tf_op jit(solution)/shard_map/ppermute | solution.py:54
  107.9 4.1 %collective-permute-done.21.refs_2_ = bf16[480,128]{1,0:T(8,128)(2,1)S(1)} collective-permute-done((bf16[480,128]{1,0:T(8,128)(2,1)S(1)}, bf16[480,128]{1,0:T(8,128)(2,1)S(1)}, u32[]{:S(2)}, u32[]{:S(2)}) %collective-permute-start.21) | collective-permute-done | bytes 122912 | tf_op jit(solution)/shard_map/ppermute | solution.py:54
  112.1 2.1 %collective-permute-done.22.refs_3_ = bf16[480,128]{1,0:T(8,128)(2,1)S(1)} collective-permute-done((bf16[480,128]{1,0:T(8,128)(2,1)S(1)}, bf16[480,128]{1,0:T(8,128)(2,1)S(1)}, u32[]{:S(2)}, u32[]{:S(2)}) %collective-permute-start.22) | collective-permute-done | bytes 122912 | tf_op jit(solution)/shard_map/ppermute | solution.py:54
  114.2 0.3 to_slabs.1
  114.6 14.8 %all_to_all.16.slabs = bf16[8,64,128]{2,1,0:T(8,128)(2,1)S(1)} all-to-all(bf16[8,64,128]{2,1,0:T(8,128)(2,1)S(1)} %to_slabs.1), channel_id=1, replica_groups={{0,32,64,96,128,160,192,224},{8,40,72,104,136,168,200,232},{16,48,80,11..., dimensions={0} | all-to-all | bytes 262144 | tf_op jit(solution)/shard_map/all_to_all | solution.py:544
  129.4 0.8 combine.1
  (10 shorter events, 0.0 us)
Async XLA Ops:
  3.0 39.1 %all-to-all-start = ((bf16[128,16,256]{2,1,0:T(8,128)(2,1)}), bf16[128,16,256]{2,1,0:T(8,128)(2,1)}, u32[]{:S(2)}, u32[]{:S(2)}) async-start(bf16[128,16,256]{2,1,0:T(8,128)(2,1)} %pack_pages.1), calls=%async_computation | async-start | bytes 2097152 | tf_op jit(solution)/shard_map/all_to_all | solution.py:573
  13.7 14.5 %copy-start.5 = (bf16[768]{0:T(1024)(128)(2,1)S(1)}, bf16[768]{0:T(1024)(128)(2,1)}, u32[]{:S(2)}) copy-start(bf16[768]{0:T(1024)(128)(2,1)} %param.20) | copy-start | bytes 4612
  19.6 27.6 %collective-permute-start.7 = (bf16[1536,256]{1,0:T(8,128)(2,1)}, bf16[1536,256]{1,0:T(8,128)(2,1)S(1)}, u32[]{:S(2)}, u32[]{:S(2)}) collective-permute-start(bf16[1536,256]{1,0:T(8,128)(2,1)} %get-tuple-element.35), channel_id=1, source_target_pairs={{0,1},{8,9},{1,0},{9,8},{2,3},{10,11},{3,2},{11,10},{16,17},{24,25... | collective-permute-start | bytes 2359304 | tf_op jit(solution)/shard_map/ppermute | solution.py:54
  20.5 41.1 %collective-permute-start.8 = (bf16[1536,256]{1,0:T(8,128)(2,1)}, bf16[1536,256]{1,0:T(8,128)(2,1)S(1)}, u32[]{:S(2)}, u32[]{:S(2)}) collective-permute-start(bf16[1536,256]{1,0:T(8,128)(2,1)} %get-tuple-element.36), channel_id=1, source_target_pairs={{0,2},{8,10},{1,3},{9,11},{2,0},{10,8},{3,1},{11,9},{16,18},{24,26... | collective-permute-start | bytes 2359304 | tf_op jit(solution)/shard_map/ppermute | solution.py:54
  21.6 41.9 %collective-permute-start.9 = (bf16[1536,256]{1,0:T(8,128)(2,1)}, bf16[1536,256]{1,0:T(8,128)(2,1)}, u32[]{:S(2)}, u32[]{:S(2)}) collective-permute-start(bf16[1536,256]{1,0:T(8,128)(2,1)} %get-tuple-element.37), channel_id=1, source_target_pairs={{0,3},{8,11},{1,2},{9,10},{2,1},{10,9},{3,0},{11,8},{16,19},{24,27... | collective-permute-start | bytes 2359304 | tf_op jit(solution)/shard_map/ppermute | solution.py:54
  24.4 40.3 %collective-permute-start.11 = (bf16[1536,256]{1,0:T(8,128)(2,1)}, bf16[1536,256]{1,0:T(8,128)(2,1)S(1)}, u32[]{:S(2)}, u32[]{:S(2)}) collective-permute-start(bf16[1536,256]{1,0:T(8,128)(2,1)} %get-tuple-element.38), channel_id=1, source_target_pairs={{0,20},{8,28},{1,21},{9,29},{2,22},{10,30},{3,23},{11,31},{16,4},{... | collective-permute-start | bytes 2359304 | tf_op jit(solution)/shard_map/ppermute | solution.py:54
  27.5 38.3 %collective-permute-start.10 = (bf16[1536,256]{1,0:T(8,128)(2,1)}, bf16[1536,256]{1,0:T(8,128)(2,1)S(1)}, u32[]{:S(2)}, u32[]{:S(2)}) collective-permute-start(bf16[1536,256]{1,0:T(8,128)(2,1)} %get-tuple-element.38), channel_id=1, source_target_pairs={{0,4},{8,12},{1,5},{9,13},{2,6},{10,14},{3,7},{11,15},{16,20},{24,... | collective-permute-start | bytes 2359304 | tf_op jit(solution)/shard_map/ppermute | solution.py:54
  42.1 5.1 %copy-start = (bf16[1536,256]{1,0:T(8,128)(2,1)S(1)}, bf16[1536,256]{1,0:T(8,128)(2,1)}, u32[]{:S(2)}) copy-start(bf16[1536,256]{1,0:T(8,128)(2,1)} %get-tuple-element.45.refs_4_) | copy-start | bytes 2359300
  42.1 32.5 %copy-start.1 = (bf16[1536,256]{1,0:T(8,128)(2,1)S(1)}, bf16[1536,256]{1,0:T(8,128)(2,1)}, u32[]{:S(2)}) copy-start(bf16[1536,256]{1,0:T(8,128)(2,1)} %get-tuple-element.34.refs_8_) | copy-start | bytes 2359300
  42.1 32.5 %copy-start.4 = (s32[2]{0:T(128)S(1)}, s32[2]{0:T(128)}, u32[]{:S(2)}) copy-start(s32[2]{0:T(128)} %pad_add_fusion.where) | copy-start | bytes 28
  47.2 51.1 %collective-permute-start.18 = (bf16[1536,256]{1,0:T(8,128)(2,1)S(1)}, bf16[1536,256]{1,0:T(8,128)(2,1)S(1)}, u32[]{:S(2)}, u32[]{:S(2)}) collective-permute-start(bf16[1536,256]{1,0:T(8,128)(2,1)S(1)} %copy-done), channel_id=1, source_target_pairs={{0,16},{8,24},{1,17},{9,25},{2,18},{10,26},{3,19},{11,27},{16,0},{... | collective-permute-start | bytes 2359304 | tf_op jit(solution)/shard_map/ppermute | solution.py:54
  61.6 6.5 %collective-permute-start.2 = (bf16[496,128]{1,0:T(8,128)(2,1)S(1)}, bf16[496,128]{1,0:T(8,128)(2,1)S(1)}, u32[]{:S(2)}, u32[]{:S(2)}) collective-permute-start(bf16[496,128]{1,0:T(8,128)(2,1)S(1)} %to_rows.1.refs_0_), channel_id=1, source_target_pairs={{0,20},{8,28},{1,21},{9,29},{2,22},{10,30},{3,23},{11,31},{16,4},{... | collective-permute-start | bytes 380936 | tf_op jit(solution)/shard_map/ppermute | solution.py:54
  63.5 9.5 %collective-permute-start.1 = (bf16[496,128]{1,0:T(8,128)(2,1)S(1)}, bf16[496,128]{1,0:T(8,128)(2,1)S(1)}, u32[]{:S(2)}, u32[]{:S(2)}) collective-permute-start(bf16[496,128]{1,0:T(8,128)(2,1)S(1)} %to_rows.1.refs_0_), channel_id=1, source_target_pairs={{0,4},{8,12},{1,5},{9,13},{2,6},{10,14},{3,7},{11,15},{16,20},{24,... | collective-permute-start | bytes 380936 | tf_op jit(solution)/shard_map/ppermute | solution.py:54
  64.7 8.3 %collective-permute-start = (bf16[496,128]{1,0:T(8,128)(2,1)S(1)}, bf16[496,128]{1,0:T(8,128)(2,1)S(1)}, u32[]{:S(2)}, u32[]{:S(2)}) collective-permute-start(bf16[496,128]{1,0:T(8,128)(2,1)S(1)} %to_rows.1.refs_0_), channel_id=1, source_target_pairs={{0,16},{8,24},{1,17},{9,25},{2,18},{10,26},{3,19},{11,27},{16,0},{... | collective-permute-start | bytes 380936 | tf_op jit(solution)/shard_map/ppermute | solution.py:54
  65.8 7.7 %collective-permute-start.3 = (bf16[496,128]{1,0:T(8,128)(2,1)S(1)}, bf16[496,128]{1,0:T(8,128)(2,1)S(1)}, u32[]{:S(2)}, u32[]{:S(2)}) collective-permute-start(bf16[496,128]{1,0:T(8,128)(2,1)S(1)} %to_rows.1.refs_0_), channel_id=1, source_target_pairs={{0,8},{8,0},{1,9},{9,1},{2,10},{10,2},{3,11},{11,3},{16,24},{24,16... | collective-permute-start | bytes 380936 | tf_op jit(solution)/shard_map/ppermute | solution.py:54
  68.1 5.5 %collective-permute-start.6 = (bf16[496,128]{1,0:T(8,128)(2,1)S(1)}, bf16[496,128]{1,0:T(8,128)(2,1)S(1)}, u32[]{:S(2)}, u32[]{:S(2)}) collective-permute-start(bf16[496,128]{1,0:T(8,128)(2,1)S(1)} %collective-permute-done.2.refs_3_), channel_id=1, source_target_pairs={{0,8},{8,0},{1,9},{9,1},{2,10},{10,2},{3,11},{11,3},{16,24},{24,16... | collective-permute-start | bytes 380936 | tf_op jit(solution)/shard_map/ppermute | solution.py:54
  73.0 1.3 %collective-permute-start.5 = (bf16[496,128]{1,0:T(8,128)(2,1)S(1)}, bf16[496,128]{1,0:T(8,128)(2,1)S(1)}, u32[]{:S(2)}, u32[]{:S(2)}) collective-permute-start(bf16[496,128]{1,0:T(8,128)(2,1)S(1)} %collective-permute-done.1.refs_2_), channel_id=1, source_target_pairs={{0,8},{8,0},{1,9},{9,1},{2,10},{10,2},{3,11},{11,3},{16,24},{24,16... | collective-permute-start | bytes 380936 | tf_op jit(solution)/shard_map/ppermute | solution.py:54
  73.0 1.5 %collective-permute-start.4 = (bf16[496,128]{1,0:T(8,128)(2,1)S(1)}, bf16[496,128]{1,0:T(8,128)(2,1)S(1)}, u32[]{:S(2)}, u32[]{:S(2)}) collective-permute-start(bf16[496,128]{1,0:T(8,128)(2,1)S(1)} %collective-permute-done.refs_1_), channel_id=1, source_target_pairs={{0,8},{8,0},{1,9},{9,1},{2,10},{10,2},{3,11},{11,3},{16,24},{24,16... | collective-permute-start | bytes 380936 | tf_op jit(solution)/shard_map/ppermute | solution.py:54
  76.9 7.5 %collective-permute-start.12 = (bf16[352,256]{1,0:T(8,128)(2,1)S(1)}, bf16[352,256]{1,0:T(8,128)(2,1)S(1)}, u32[]{:S(2)}, u32[]{:S(2)}) collective-permute-start(bf16[352,256]{1,0:T(8,128)(2,1)S(1)} %get-tuple-element.40), channel_id=1, source_target_pairs={{0,1},{8,9},{1,0},{9,8},{2,3},{10,11},{3,2},{11,10},{16,17},{24,25... | collective-permute-start | bytes 540680 | tf_op jit(solution)/shard_map/ppermute | solution.py:54
  77.6 10.0 %collective-permute-start.13 = (bf16[352,256]{1,0:T(8,128)(2,1)S(1)}, bf16[352,256]{1,0:T(8,128)(2,1)S(1)}, u32[]{:S(2)}, u32[]{:S(2)}) collective-permute-start(bf16[352,256]{1,0:T(8,128)(2,1)S(1)} %get-tuple-element.41), channel_id=1, source_target_pairs={{0,2},{8,10},{1,3},{9,11},{2,0},{10,8},{3,1},{11,9},{16,18},{24,26... | collective-permute-start | bytes 540680 | tf_op jit(solution)/shard_map/ppermute | solution.py:54
  78.9 11.3 %collective-permute-start.14 = (bf16[352,256]{1,0:T(8,128)(2,1)S(1)}, bf16[352,256]{1,0:T(8,128)(2,1)S(1)}, u32[]{:S(2)}, u32[]{:S(2)}) collective-permute-start(bf16[352,256]{1,0:T(8,128)(2,1)S(1)} %get-tuple-element.42), channel_id=1, source_target_pairs={{0,3},{8,11},{1,2},{9,10},{2,1},{10,9},{3,0},{11,8},{16,19},{24,27... | collective-permute-start | bytes 540680 | tf_op jit(solution)/shard_map/ppermute | solution.py:54
  90.5 5.9 %collective-permute-start.16 = (bf16[160,128]{1,0:T(8,128)(2,1)S(1)}, bf16[160,128]{1,0:T(8,128)(2,1)S(1)}, u32[]{:S(2)}, u32[]{:S(2)}) collective-permute-start(bf16[160,128]{1,0:T(8,128)(2,1)S(1)} %get-tuple-element.43.refs_0_), channel_id=1, source_target_pairs={{0,4},{8,12},{1,5},{9,13},{2,6},{10,14},{3,7},{11,15},{16,20},{24,... | collective-permute-start | bytes 122888 | tf_op jit(solution)/shard_map/ppermute | solution.py:54
  93.1 5.2 %collective-permute-start.17 = (bf16[160,128]{1,0:T(8,128)(2,1)S(1)}, bf16[160,128]{1,0:T(8,128)(2,1)S(1)}, u32[]{:S(2)}, u32[]{:S(2)}) collective-permute-start(bf16[160,128]{1,0:T(8,128)(2,1)S(1)} %get-tuple-element.44), channel_id=1, source_target_pairs={{0,20},{8,28},{1,21},{9,29},{2,22},{10,30},{3,23},{11,31},{16,4},{... | collective-permute-start | bytes 122888 | tf_op jit(solution)/shard_map/ppermute | solution.py:54
  94.0 4.3 %collective-permute-start.15 = (bf16[160,128]{1,0:T(8,128)(2,1)S(1)}, bf16[160,128]{1,0:T(8,128)(2,1)S(1)}, u32[]{:S(2)}, u32[]{:S(2)}) collective-permute-start(bf16[160,128]{1,0:T(8,128)(2,1)S(1)} %get-tuple-element.44), channel_id=1, source_target_pairs={{0,16},{8,24},{1,17},{9,25},{2,18},{10,26},{3,19},{11,27},{16,0},{... | collective-permute-start | bytes 122888 | tf_op jit(solution)/shard_map/ppermute | solution.py:54
  99.6 29.8 %copy-start.2 = (bf16[256,128]{1,0:T(8,128)(2,1)S(1)}, bf16[256,128]{1,0:T(8,128)(2,1)}, u32[]{:S(2)}) copy-start(bf16[256,128]{1,0:T(8,128)(2,1)} %get-tuple-element.30.refs_6_.select) | copy-start | bytes 196612
  99.6 29.8 %copy-start.3 = (bf16[16,768]{1,0:T(8,128)(2,1)S(1)}, bf16[16,768]{1,0:T(8,128)(2,1)}, u32[]{:S(2)}) copy-start(bf16[16,768]{1,0:T(8,128)(2,1)} %get-tuple-element.52.hidden) | copy-start | bytes 73732
  99.6 2.0 %collective-permute-start.19 = (bf16[4,480,128]{2,1,0:T(8,128)(2,1)S(1)}, bf16[4,480,128]{2,1,0:T(8,128)(2,1)S(1)}, u32[]{:S(2)}, u32[]{:S(2)}) collective-permute-start(bf16[4,480,128]{2,1,0:T(8,128)(2,1)S(1)} %get-tuple-element.47), channel_id=1, source_target_pairs={{0,8},{8,0},{1,9},{9,1},{2,10},{10,2},{3,11},{11,3},{16,24},{24,16... | collective-permute-start | bytes 1474568 | tf_op jit(solution)/shard_map/ppermute | solution.py:54
  101.7 6.3 %collective-permute-start.20 = (bf16[480,128]{1,0:T(8,128)(2,1)S(1)}, bf16[480,128]{1,0:T(8,128)(2,1)S(1)}, u32[]{:S(2)}, u32[]{:S(2)}) collective-permute-start(bf16[480,128]{1,0:T(8,128)(2,1)S(1)} %get-tuple-element.49), channel_id=1, source_target_pairs={{0,1},{8,9},{1,0},{9,8},{2,3},{10,11},{3,2},{11,10},{16,17},{24,25... | collective-permute-start | bytes 368648 | tf_op jit(solution)/shard_map/ppermute | solution.py:54
  101.8 10.3 %collective-permute-start.21 = (bf16[480,128]{1,0:T(8,128)(2,1)S(1)}, bf16[480,128]{1,0:T(8,128)(2,1)S(1)}, u32[]{:S(2)}, u32[]{:S(2)}) collective-permute-start(bf16[480,128]{1,0:T(8,128)(2,1)S(1)} %get-tuple-element.50), channel_id=1, source_target_pairs={{0,2},{8,10},{1,3},{9,11},{2,0},{10,8},{3,1},{11,9},{16,18},{24,26... | collective-permute-start | bytes 368648 | tf_op jit(solution)/shard_map/ppermute | solution.py:54
  106.0 8.2 %collective-permute-start.22 = (bf16[480,128]{1,0:T(8,128)(2,1)S(1)}, bf16[480,128]{1,0:T(8,128)(2,1)S(1)}, u32[]{:S(2)}, u32[]{:S(2)}) collective-permute-start(bf16[480,128]{1,0:T(8,128)(2,1)S(1)} %get-tuple-element.51), channel_id=1, source_target_pairs={{0,3},{8,11},{1,2},{9,10},{2,1},{10,9},{3,0},{11,8},{16,19},{24,27... | collective-permute-start | bytes 368648 | tf_op jit(solution)/shard_map/ppermute | solution.py:54

commit v3 on v2

--- a/solution.py
+++ b/solution.py
@@ -39,7 +39,7 @@
 
 
 def along_x(step):
-    return pairs(lambda z, y, x, c: (z, y, x ^ step, c))
+    return pairs(lambda z, y, x, c: (z, y, (x + step) % 4, c))
 
 
 def along_y(step):
@@ -47,7 +47,9 @@
 
 
 OTHER_CORE = pairs(lambda z, y, x, c: (z, y, x, c ^ 1))
-Z_GROUPS = [[z * 4 + r for z in range(NZ)] for r in range(4)]
+Z_GROUPS = [[z * 4 + r for z in reversed(range(NZ))] for r in range(4)]
+PAGE_GROUPS = [[z * 4 + r for z in reversed(range(NZ)) for r in range(4)]]
+OWNERS_Z = 4
 
 
 def permute(value, perm):
@@ -94,7 +96,8 @@
     def put(p, carry):
         o = owner[0, p]
         k = used[o]
-        out[o * CAPP + k] = fresh[p]
+        at = (NZ - 1 - o // OWNERS_Z) * OWNERS_Z + o % OWNERS_Z
+        out[at * CAPP + k] = fresh[p]
         used[o] = k + 1
         return carry
 
@@ -176,14 +179,13 @@
     rows, width = stream.shape
     heads = width // LANES
     pages = table.shape[1]
-    fresh = pl.ds(OLD_PAGES, arrived.shape[0])
     kept = pl.ds(0, OLD_PAGES)
+    share = arrived.shape[0] // NZ
     loads = [
         pltpu.make_async_copy(source, target, sems.at[i])
         for i, (source, target) in enumerate(
             [
                 (kv_pool.at[kept], pool.at[kept]),
-                (arrived, pool.at[fresh]),
                 (in_hbm_refs[2], heads_v),
                 (in_hbm_refs[3], stream),
                 (in_hbm_refs[4], gain),
@@ -195,9 +197,12 @@
     ]
     for load in loads:
         load.start()
-    for load in loads[:3]:
+    for z in range(NZ):
+        to, at = OLD_PAGES + z * share, (NZ - 1 - z) * share
+        pool[to : to + share] = arrived[at : at + share]
+    for load in loads[:2]:
         load.wait()
-    store = pltpu.make_async_copy(pool, kv_out, sems.at[8])
+    store = pltpu.make_async_copy(pool, kv_out, sems.at[7])
     store.start()
     scale = float(LANES) ** (-0.5)
     length = jnp.concatenate(
@@ -222,7 +227,7 @@
         weight = jnp.concatenate([weight, weight], axis=0).astype(BF16)
         o_scr[r * 8 : (r + 1) * 8, :] = jnp.dot(weight, values, preferred_element_type=F32)[:8]
     o_scr[...] = o_scr[...] / total
-    for load in loads[3:]:
+    for load in loads[2:]:
         load.wait()
     attended = jnp.concatenate([o_scr[pl.ds(h, rows, stride=8), :] for h in range(heads)], axis=1)
     hidden = (stream[...].astype(F32) + attended).astype(BF16)
@@ -253,8 +258,8 @@
     slabs = jnp.dot(select[...], stacked, preferred_element_type=F32).astype(BF16)
     for e in range(EXPERTS):
         slab = slabs[e * SLAB : (e + 1) * SLAB]
-        payload[2 * e] = slab
-        payload[2 * e + 1] = slab
+        payload[NZ - 1 - 2 * e] = slab
+        payload[NZ - 2 - 2 * e] = slab
     store.wait()
 
 
@@ -280,7 +285,7 @@
             pltpu.VMEM(places.shape, jnp.int32),
             pltpu.VMEM((rows * 8, table.shape[1] * kv_pool.shape[1]), F32),
             pltpu.VMEM((rows * 8, LANES), F32),
-            pltpu.SemaphoreType.DMA((9,)),
+            pltpu.SemaphoreType.DMA((8,)),
         ],
         compiler_params=params(56),
         name="attend",
@@ -291,7 +296,7 @@
     made, places, blocks, sems = refs[:6], refs[6:9], refs[9:15], refs[15]
     pieces = []
     for n in range(4):
-        x = jnp.bitwise_xor(where[1], n)
+        x = jnp.bitwise_and(where[1] + n, 3)
         for h in range(2):
             at = pl.ds(pl.multiple_of((h * 4 + x) * WIDTH, WIDTH), WIDTH)
             to = pl.ds(h * WIDTH, WIDTH)
@@ -450,7 +455,7 @@
     active, weights, outs = refs[0:4], refs[4:8], refs[8:10]
     left = jnp.concatenate([ref[...] for ref in active], axis=1)
     for n in range(4):
-        x = jnp.bitwise_xor(where[1], n)
+        x = jnp.bitwise_and(where[1] + n, 3)
         for pair in range(3):
             at = pl.ds(pl.multiple_of((x * 3 + pair) * LANES, LANES), LANES)
             right = jnp.concatenate([ref[at, :] for ref in weights], axis=0)
@@ -519,7 +524,7 @@
     rows, width = hidden.shape
     total = jnp.zeros((LANES, LANES), F32)
     for half in range(2):
-        flat = jnp.concatenate([slabs[2 * e + half] for e in range(EXPERTS)], axis=0)
+        flat = jnp.concatenate([slabs[NZ - 1 - 2 * e - half] for e in range(EXPERTS)], axis=0)
         total = total + lax.dot_general(
             select[...], flat, (((0,), (0,)), ((), ())), preferred_element_type=F32
         )
@@ -570,7 +575,9 @@
     first = [blocks[0]] + [permute(blocks[n], along_x(n)) for n in (1, 2, 3)]
     second = [permute(blocks[5], along_y(m)) for m in (2, 3)]
     outgoing = pack_pages(fresh_owner.T, fresh_kv.reshape(-1, page_len, page_width), n_attn)
-    arrived = lax.all_to_all(outgoing, "attn", 0, 0, tiled=True)
+    arrived = lax.all_to_all(
+        outgoing, "attn", 0, 0, axis_index_groups=PAGE_GROUPS, tiled=True
+    )
     kv_out, hidden, payload = attend(
         page_table,
         lengths,
@@ -584,13 +591,12 @@
         places,
     )
 
-    near, payload = lax.optimization_barrier((blocks[4], payload))
-    second = [blocks[4], permute(near, along_y(1))] + second
-
     own = gather4(to_rows(exchange_z(payload)), along_y)
     other = [permute(v, OTHER_CORE) for v in own]
-    parts = gate_up(where, own, other, first, second[2:])
-    active = activate([parts[0]] + [permute(parts[n], along_x(n)) for n in (1, 2, 3)])
+    parts = gate_up(where, own, other, first, second)
+    near, *parts = lax.optimization_barrier((blocks[4], *parts))
+    second = [blocks[4], permute(near, along_y(1))] + second
+    active = activate([parts[0]] + [permute(parts[n], along_x(-n)) for n in (1, 2, 3)])
     active = [active[0]] + [permute(active[m % 2], along_y(m)) for m in (1, 2, 3)]
     made, for_other = down(where, active, second)
     sums = add_cores(made, permute(for_other, OTHER_CORE))

time: 131 us -> 123 us (0.939)
  waiting for transfers between devices: 43.7 us -> 39.9 us
  starting transfers between devices: 38.4 us -> 35.4 us
    ppermute x23, starting transfers between devices: 28.4 us -> 25 us  [permute(): return lax.ppermute(value, AXES, perm)]
    all_to_all x1, waiting for transfers between devices: 13.3 us -> 10.6 us  [on_device(): lax.all_to_all(outgoing, 'attn', 0, 0, axis_index_groups=PAGE_GROUPS, til...]
  transfers between devices with their start and end apart: 24 -> 24, of which waited for: 14 -> 13; matrix products, arithmetic and copies ran while one was open for 1% -> 1% of each run, Pallas kernels for 11% -> 9%
where the time goes in v3:
time: 123 us
  waiting for transfers between devices  39.9 us (32%)
  starting transfers between devices  35.4 us (29%)
  blocking collectives  26.7 us (22%)
  Pallas kernels  19 us (15%)
    ppermute x23, waiting for transfers between devices, permute(): return lax.ppermute(value, AXES, perm)  29.3 us
    all_to_all x2, blocking collectives, exchange_z(): lax.all_to_all(slabs, 'attn', 0, 0, axis_index_groups=Z_GROUPS, tiled=True)  26.7 us
    ppermute x23, starting transfers between devices, permute(): return lax.ppermute(value, AXES, perm)  25 us
    all_to_all x1, waiting for transfers between devices, on_device(): lax.all_to_all(outgoing, 'attn', 0, 0, axis_index_groups=PAGE_GROUPS, til...  10.6 us
    all_to_all x1, starting transfers between devices, on_device(): lax.all_to_all(outgoing, 'attn', 0, 0, axis_index_groups=PAGE_GROUPS, til...  10.3 us
    pallas_call x1, Pallas kernels, prepare(): pl.pallas_call(prepare_kernel, out_shape=(shape(block, BF16),) * 6 + (sha...  5.92 us
    pallas_call x1, Pallas kernels, attend(): pl.pallas_call(attend_kernel, out_shape=(shape(kv_pool.shape, kv_pool.dty...  5.07 us
    pallas_call x1, Pallas kernels, pack_pages(): pl.pallas_call(pack_pages_kernel, out_shape=jax.ShapeDtypeStruct((n_attn...  2.5 us
  transfers between devices with their start and end apart: 24, of which 13 were waited for; matrix products, arithmetic and copies ran while one was open for 1% of the time, Pallas kernels for 9%

profile of v3, /device:TPU:6, one launch (start us, length us, event | category | flops | bytes accessed | tf_op | source)
XLA Modules:
  0.0 123.0 jit_solution(17980131333980487791)
XLA Ops:
  0.6 2.5 %pack_pages.1 = bf16[128,16,256]{2,1,0:T(8,128)(2,1)} custom-call(s32[1,32]{1,0:T(1,128)} %bitcast.14, bf16[32,16,256]{2,1,0:T(8,128)(2,1)} %bitcast.11), custom_call_target="tpu_custom_call" | custom-call | tf_op jit(solution)/shard_map/pack_pages/pallas_call | solution.py:108
  3.1 10.3 %all-to-all-start = ((bf16[128,16,256]{2,1,0:T(8,128)(2,1)}), bf16[128,16,256]{2,1,0:T(8,128)(2,1)}, u32[]{:S(2)}, u32[]{:S(2)}) async-start(bf16[128,16,256]{2,1,0:T(8,128)(2,1)} %pack_pages.1), calls=%async_computation | async-start | bytes 2097152 | tf_op jit(solution)/shard_map/all_to_all | solution.py:578
  13.5 0.7 pad_add_fusion.where
  14.1 5.9 %prepare.1 = (bf16[1536,256]{1,0:T(8,128)(2,1)}, bf16[1536,256]{1,0:T(8,128)(2,1)}, bf16[1536,256]{1,0:T(8,128)(2,1)}, bf16[1536,256]{1,0:T(8,128)(2,1)}, bf16[1...) custom-call(s32[2]{0:T(128)} %pad_add_fusion.where, ...), custom_call_target="tpu_custom_call" | custom-call | tf_op jit(solution)/shard_map/prepare/pallas_call | solution.py:333
  20.1 0.6 collective-permute-start.7
  20.6 2.4 %collective-permute-start.8 = (bf16[1536,256]{1,0:T(8,128)(2,1)}, bf16[1536,256]{1,0:T(8,128)(2,1)S(1)}, u32[]{:S(2)}, u32[]{:S(2)}) collective-permute-start(bf16[1536,256]{1,0:T(8,128)(2,1)} %get-tuple-element.38), channel_id=1, source_target_pairs={{0,2},{8,10},{1,3},{9,11},{2,0},{10,8},{3,1},{11,9},{16,18},{24,26... | collective-permute-start | bytes 2359304 | tf_op jit(solution)/shard_map/ppermute | solution.py:56
  23.0 0.0 collective-permute-start.9
  23.0 3.2 %collective-permute-start.11 = (bf16[1536,256]{1,0:T(8,128)(2,1)}, bf16[1536,256]{1,0:T(8,128)(2,1)S(1)}, u32[]{:S(2)}, u32[]{:S(2)}) collective-permute-start(bf16[1536,256]{1,0:T(8,128)(2,1)} %get-tuple-element.40), channel_id=1, source_target_pairs={{0,20},{8,28},{1,21},{9,29},{2,22},{10,30},{3,23},{11,31},{16,4},{... | collective-permute-start | bytes 2359304 | tf_op jit(solution)/shard_map/ppermute | solution.py:56
  26.2 0.4 collective-permute-start.10
  26.6 0.6 reshape.18.refs_4_
  27.2 10.6 %all-to-all-done.refs_1_ = bf16[128,16,256]{2,1,0:T(8,128)(2,1)} async-done(((bf16[128,16,256]{2,1,0:T(8,128)(2,1)}), bf16[128,16,256]{2,1,0:T(8,128)(2,1)}, u32[]{:S(2)}, u32[]{:S(2)}) %all-to-all-start) | async-done | bytes 1048608 | tf_op jit(solution)/shard_map/all_to_all | solution.py:578
  37.8 5.1 %attend.1 = (bf16[320,16,256]{2,1,0:T(8,128)(2,1)}, bf16[16,768]{1,0:T(8,128)(2,1)}, bf16[8,64,128]{2,1,0:T(8,128)(2,1)}) custom-call(s32[16,16]{1,0:T(8,128)} %table.1, s32[1,16]{1,0:T(1,128)} %lengths.1, bf16[320,16,256]{2,1,0:T(8,128)(2,1)} %bitcast.10, bf16[128,16,256]{2,1,0:T(8,128)(2,1)} %all-to-all-done.refs_1_, ...), custom_call_target="tpu_custom_call" | custom-call | tf_op jit(solution)/shard_map/attend/pallas_call | solution.py:269
  42.8 14.0 %all_to_all.15.slabs = bf16[8,64,128]{2,1,0:T(8,128)(2,1)S(1)} all-to-all(bf16[8,64,128]{2,1,0:T(8,128)(2,1)} %get-tuple-element.35), channel_id=1, replica_groups={{224,192,160,128,96,64,32,0},{232,200,168,136,104,72,40,8},{240,208,176..., dimensions={0} | all-to-all | bytes 262144 | tf_op jit(solution)/shard_map/all_to_all | solution.py:549
  56.9 0.3 to_rows.1.refs_0_
  57.2 0.0 collective-permute-done.7.refs_9_
  57.2 3.4 %collective-permute-start.2 = (bf16[496,128]{1,0:T(8,128)(2,1)S(1)}, bf16[496,128]{1,0:T(8,128)(2,1)S(1)}, u32[]{:S(2)}, u32[]{:S(2)}) collective-permute-start(bf16[496,128]{1,0:T(8,128)(2,1)S(1)} %to_rows.1.refs_0_), channel_id=1, source_target_pairs={{0,20},{8,28},{1,21},{9,29},{2,22},{10,30},{3,23},{11,31},{16,4},{... | collective-permute-start | bytes 380936 | tf_op jit(solution)/shard_map/ppermute | solution.py:56
  60.5 0.0 collective-permute-done.8.refs_10_
  60.5 0.4 collective-permute-start.1
  60.9 0.0 collective-permute-done.9.refs_11_
  61.0 0.6 collective-permute-start
  61.5 0.0 collective-permute-done.11.refs_13_.refs_7_
  61.5 0.0 collective-permute-start.3
  61.5 3.8 %collective-permute-done.2.refs_3_ = bf16[496,128]{1,0:T(8,128)(2,1)S(1)} collective-permute-done((bf16[496,128]{1,0:T(8,128)(2,1)S(1)}, bf16[496,128]{1,0:T(8,128)(2,1)S(1)}, u32[]{:S(2)}, u32[]{:S(2)}) %collective-permute-start.2) | collective-permute-done | bytes 127008 | tf_op jit(solution)/shard_map/ppermute | solution.py:56
  65.3 0.0 collective-permute-start.6
  65.3 2.2 %collective-permute-done.1.refs_2_ = bf16[496,128]{1,0:T(8,128)(2,1)S(1)} collective-permute-done((bf16[496,128]{1,0:T(8,128)(2,1)S(1)}, bf16[496,128]{1,0:T(8,128)(2,1)S(1)}, u32[]{:S(2)}, u32[]{:S(2)}) %collective-permute-start.1) | collective-permute-done | bytes 127008 | tf_op jit(solution)/shard_map/ppermute | solution.py:56
  67.5 0.0 collective-permute-start.5
  67.5 0.0 collective-permute-done.refs_1_
  67.5 0.5 collective-permute-start.4
  68.0 0.0 collective-permute-done.10.refs_12_.refs_6_
  68.0 0.0 collective-permute-done.3.refs_4_
  68.0 0.0 collective-permute-done.6.refs_7_
  68.0 0.8 collective-permute-done.5.refs_6_
  68.8 0.2 collective-permute-done.4.refs_5_
  69.0 2.4 %gate_up.1 = (f32[352,256]{1,0:T(8,128)S(1)}, bf16[352,256]{1,0:T(8,128)(2,1)S(1)}, bf16[352,256]{1,0:T(8,128)(2,1)S(1)}, bf16[352,256]{1,0:T(8,128)(2,1)S(1)}) custom-call(s32[2]{0:T(128)S(1)} %copy-done.4, bf16[496,128]{1,0:T(8,128)(2,1)S(1)} %to_rows.1.refs_0_, bf16[496,128]{1,0:T(8,128)(2,1)S(1)} %collective-permute-done.refs_1_, ...), custom_call_target="tpu_custom_call" | custom-call | tf_op jit(solution)/shard_map/gate_up/pallas_call | solution.py:405
  71.4 0.1 collective-permute-start.18
  71.5 0.9 collective-permute-start.12
  72.4 2.9 %collective-permute-start.13 = (bf16[352,256]{1,0:T(8,128)(2,1)S(1)}, bf16[352,256]{1,0:T(8,128)(2,1)S(1)}, u32[]{:S(2)}, u32[]{:S(2)}) collective-permute-start(bf16[352,256]{1,0:T(8,128)(2,1)S(1)} %get-tuple-element.47), channel_id=1, source_target_pairs={{0,2},{8,10},{1,3},{9,11},{2,0},{10,8},{3,1},{11,9},{16,18},{24,26... | collective-permute-start | bytes 540680 | tf_op jit(solution)/shard_map/ppermute | solution.py:56
  75.4 0.7 collective-permute-start.14
  76.1 4.6 %collective-permute-done.12.refs_1_ = bf16[352,256]{1,0:T(8,128)(2,1)S(1)} collective-permute-done((bf16[352,256]{1,0:T(8,128)(2,1)S(1)}, bf16[352,256]{1,0:T(8,128)(2,1)S(1)}, u32[]{:S(2)}, u32[]{:S(2)}) %collective-permute-start.12) | collective-permute-done | bytes 180256 | tf_op jit(solution)/shard_map/ppermute | solution.py:56
  80.7 2.9 %collective-permute-done.13.refs_2_ = bf16[352,256]{1,0:T(8,128)(2,1)S(1)} collective-permute-done((bf16[352,256]{1,0:T(8,128)(2,1)S(1)}, bf16[352,256]{1,0:T(8,128)(2,1)S(1)}, u32[]{:S(2)}, u32[]{:S(2)}) %collective-permute-start.13) | collective-permute-done | bytes 180256 | tf_op jit(solution)/shard_map/ppermute | solution.py:56
  83.5 0.6 collective-permute-done.14.refs_3_
  84.1 0.3 activate.1
  84.4 3.4 %collective-permute-start.16 = (bf16[160,128]{1,0:T(8,128)(2,1)S(1)}, bf16[160,128]{1,0:T(8,128)(2,1)S(1)}, u32[]{:S(2)}, u32[]{:S(2)}) collective-permute-start(bf16[160,128]{1,0:T(8,128)(2,1)S(1)} %get-tuple-element.49.refs_0_), channel_id=1, source_target_pairs={{0,4},{8,12},{1,5},{9,13},{2,6},{10,14},{3,7},{11,15},{16,20},{24,... | collective-permute-start | bytes 122888 | tf_op jit(solution)/shard_map/ppermute | solution.py:56
  87.8 1.0 collective-permute-start.17
  88.8 0.0 collective-permute-start.15
  88.8 4.9 %collective-permute-done.16.refs_2_ = bf16[160,128]{1,0:T(8,128)(2,1)S(1)} collective-permute-done((bf16[160,128]{1,0:T(8,128)(2,1)S(1)}, bf16[160,128]{1,0:T(8,128)(2,1)S(1)}, u32[]{:S(2)}, u32[]{:S(2)}) %collective-permute-start.16) | collective-permute-done | bytes 40992 | tf_op jit(solution)/shard_map/ppermute | solution.py:56
  93.7 0.0 collective-permute-done.17.refs_3_
  93.7 0.0 collective-permute-done.15.refs_1_
  93.7 0.0 collective-permute-done.18.refs_5_
  93.8 1.3 %down.1 = (bf16[4,480,128]{2,1,0:T(8,128)(2,1)S(1)}, bf16[4,480,128]{2,1,0:T(8,128)(2,1)S(1)}) custom-call(s32[2]{0:T(128)S(1)} %copy-done.4, bf16[160,128]{1,0:T(8,128)(2,1)S(1)} %get-tuple-element.49.refs_0_, bf16[160,128]{1,0:T(8,128)(2,1)S(1)} %collective-permute-done.15.refs_1_, bf16[160,128]{1,0:T(8,128)(2,1)S(1)} %collective-permute-done.16.refs_2_, ...), custom_call_target="tpu_custom_call" | custom-call | tf_op jit(solution)/shard_map/down/pallas_call | solution.py:473
  95.0 0.0 copy-start.3
  95.0 0.1 collective-permute-start.19
  95.1 1.9 %collective-permute-done.19.other = bf16[4,480,128]{2,1,0:T(8,128)(2,1)S(1)} collective-permute-done((bf16[4,480,128]{2,1,0:T(8,128)(2,1)S(1)}, bf16[4,480,128]{2,1,0:T(8,128)(2,1)S(1)}, u32[]{:S(2)}, u32[]{:S(2)}) %collective-permute-start.19) | collective-permute-done | bytes 491552 | tf_op jit(solution)/shard_map/ppermute | solution.py:56
  97.0 0.1 add_cores.1
  97.1 3.0 %collective-permute-start.20 = (bf16[480,128]{1,0:T(8,128)(2,1)S(1)}, bf16[480,128]{1,0:T(8,128)(2,1)S(1)}, u32[]{:S(2)}, u32[]{:S(2)}) collective-permute-start(bf16[480,128]{1,0:T(8,128)(2,1)S(1)} %get-tuple-element.55), channel_id=1, source_target_pairs={{0,1},{8,9},{1,2},{9,10},{2,3},{10,11},{3,0},{11,8},{16,17},{24,25... | collective-permute-start | bytes 368648 | tf_op jit(solution)/shard_map/ppermute | solution.py:56
  100.1 0.1 collective-permute-start.21
  100.3 1.3 %collective-permute-start.22 = (bf16[480,128]{1,0:T(8,128)(2,1)S(1)}, bf16[480,128]{1,0:T(8,128)(2,1)S(1)}, u32[]{:S(2)}, u32[]{:S(2)}) collective-permute-start(bf16[480,128]{1,0:T(8,128)(2,1)S(1)} %get-tuple-element.57), channel_id=1, source_target_pairs={{0,3},{8,11},{1,0},{9,8},{2,1},{10,9},{3,2},{11,10},{16,19},{24,27... | collective-permute-start | bytes 368648 | tf_op jit(solution)/shard_map/ppermute | solution.py:56
  101.6 4.1 %collective-permute-done.20.refs_1_ = bf16[480,128]{1,0:T(8,128)(2,1)S(1)} collective-permute-done((bf16[480,128]{1,0:T(8,128)(2,1)S(1)}, bf16[480,128]{1,0:T(8,128)(2,1)S(1)}, u32[]{:S(2)}, u32[]{:S(2)}) %collective-permute-start.20) | collective-permute-done | bytes 122912 | tf_op jit(solution)/shard_map/ppermute | solution.py:56
  105.7 2.2 %collective-permute-done.21.refs_2_ = bf16[480,128]{1,0:T(8,128)(2,1)S(1)} collective-permute-done((bf16[480,128]{1,0:T(8,128)(2,1)S(1)}, bf16[480,128]{1,0:T(8,128)(2,1)S(1)}, u32[]{:S(2)}, u32[]{:S(2)}) %collective-permute-start.21) | collective-permute-done | bytes 122912 | tf_op jit(solution)/shard_map/ppermute | solution.py:56
  107.8 1.3 %collective-permute-done.22.refs_3_ = bf16[480,128]{1,0:T(8,128)(2,1)S(1)} collective-permute-done((bf16[480,128]{1,0:T(8,128)(2,1)S(1)}, bf16[480,128]{1,0:T(8,128)(2,1)S(1)}, u32[]{:S(2)}, u32[]{:S(2)}) %collective-permute-start.22) | collective-permute-done | bytes 122912 | tf_op jit(solution)/shard_map/ppermute | solution.py:56
  109.2 0.3 to_slabs.1
  109.5 12.6 %all_to_all.16.slabs = bf16[8,64,128]{2,1,0:T(8,128)(2,1)S(1)} all-to-all(bf16[8,64,128]{2,1,0:T(8,128)(2,1)S(1)} %to_slabs.1), channel_id=1, replica_groups={{224,192,160,128,96,64,32,0},{232,200,168,136,104,72,40,8},{240,208,176..., dimensions={0} | all-to-all | bytes 262144 | tf_op jit(solution)/shard_map/all_to_all | solution.py:549
  122.2 0.0 copy-done.2
  122.2 0.8 combine.1
  (10 shorter events, 0.0 us)
Async XLA Ops:
  3.1 34.6 %all-to-all-start = ((bf16[128,16,256]{2,1,0:T(8,128)(2,1)}), bf16[128,16,256]{2,1,0:T(8,128)(2,1)}, u32[]{:S(2)}, u32[]{:S(2)}) async-start(bf16[128,16,256]{2,1,0:T(8,128)(2,1)} %pack_pages.1), calls=%async_computation | async-start | bytes 2097152 | tf_op jit(solution)/shard_map/all_to_all | solution.py:578
  14.1 12.5 %copy-start.5 = (bf16[768]{0:T(1024)(128)(2,1)S(1)}, bf16[768]{0:T(1024)(128)(2,1)}, u32[]{:S(2)}) copy-start(bf16[768]{0:T(1024)(128)(2,1)} %param.20) | copy-start | bytes 4612
  20.1 37.1 %collective-permute-start.7 = (bf16[1536,256]{1,0:T(8,128)(2,1)}, bf16[1536,256]{1,0:T(8,128)(2,1)S(1)}, u32[]{:S(2)}, u32[]{:S(2)}) collective-permute-start(bf16[1536,256]{1,0:T(8,128)(2,1)} %get-tuple-element.37), channel_id=1, source_target_pairs={{0,1},{8,9},{1,2},{9,10},{2,3},{10,11},{3,0},{11,8},{16,17},{24,25... | collective-permute-start | bytes 2359304 | tf_op jit(solution)/shard_map/ppermute | solution.py:56
  20.6 39.9 %collective-permute-start.8 = (bf16[1536,256]{1,0:T(8,128)(2,1)}, bf16[1536,256]{1,0:T(8,128)(2,1)S(1)}, u32[]{:S(2)}, u32[]{:S(2)}) collective-permute-start(bf16[1536,256]{1,0:T(8,128)(2,1)} %get-tuple-element.38), channel_id=1, source_target_pairs={{0,2},{8,10},{1,3},{9,11},{2,0},{10,8},{3,1},{11,9},{16,18},{24,26... | collective-permute-start | bytes 2359304 | tf_op jit(solution)/shard_map/ppermute | solution.py:56
  23.0 37.9 %collective-permute-start.9 = (bf16[1536,256]{1,0:T(8,128)(2,1)}, bf16[1536,256]{1,0:T(8,128)(2,1)}, u32[]{:S(2)}, u32[]{:S(2)}) collective-permute-start(bf16[1536,256]{1,0:T(8,128)(2,1)} %get-tuple-element.39), channel_id=1, source_target_pairs={{0,3},{8,11},{1,0},{9,8},{2,1},{10,9},{3,2},{11,10},{16,19},{24,27... | collective-permute-start | bytes 2359304 | tf_op jit(solution)/shard_map/ppermute | solution.py:56
  23.0 38.5 %collective-permute-start.11 = (bf16[1536,256]{1,0:T(8,128)(2,1)}, bf16[1536,256]{1,0:T(8,128)(2,1)S(1)}, u32[]{:S(2)}, u32[]{:S(2)}) collective-permute-start(bf16[1536,256]{1,0:T(8,128)(2,1)} %get-tuple-element.40), channel_id=1, source_target_pairs={{0,20},{8,28},{1,21},{9,29},{2,22},{10,30},{3,23},{11,31},{16,4},{... | collective-permute-start | bytes 2359304 | tf_op jit(solution)/shard_map/ppermute | solution.py:56
  26.2 41.8 %collective-permute-start.10 = (bf16[1536,256]{1,0:T(8,128)(2,1)}, bf16[1536,256]{1,0:T(8,128)(2,1)S(1)}, u32[]{:S(2)}, u32[]{:S(2)}) collective-permute-start(bf16[1536,256]{1,0:T(8,128)(2,1)} %get-tuple-element.40), channel_id=1, source_target_pairs={{0,4},{8,12},{1,5},{9,13},{2,6},{10,14},{3,7},{11,15},{16,20},{24,... | collective-permute-start | bytes 2359304 | tf_op jit(solution)/shard_map/ppermute | solution.py:56
  37.7 31.3 %copy-start.1 = (bf16[1536,256]{1,0:T(8,128)(2,1)S(1)}, bf16[1536,256]{1,0:T(8,128)(2,1)}, u32[]{:S(2)}) copy-start(bf16[1536,256]{1,0:T(8,128)(2,1)} %get-tuple-element.36.refs_8_) | copy-start | bytes 2359300
  37.8 31.3 %copy-start.4 = (s32[2]{0:T(128)S(1)}, s32[2]{0:T(128)}, u32[]{:S(2)}) copy-start(s32[2]{0:T(128)} %pad_add_fusion.where) | copy-start | bytes 28
  57.2 8.1 %collective-permute-start.2 = (bf16[496,128]{1,0:T(8,128)(2,1)S(1)}, bf16[496,128]{1,0:T(8,128)(2,1)S(1)}, u32[]{:S(2)}, u32[]{:S(2)}) collective-permute-start(bf16[496,128]{1,0:T(8,128)(2,1)S(1)} %to_rows.1.refs_0_), channel_id=1, source_target_pairs={{0,20},{8,28},{1,21},{9,29},{2,22},{10,30},{3,23},{11,31},{16,4},{... | collective-permute-start | bytes 380936 | tf_op jit(solution)/shard_map/ppermute | solution.py:56
  60.5 6.9 %collective-permute-start.1 = (bf16[496,128]{1,0:T(8,128)(2,1)S(1)}, bf16[496,128]{1,0:T(8,128)(2,1)S(1)}, u32[]{:S(2)}, u32[]{:S(2)}) collective-permute-start(bf16[496,128]{1,0:T(8,128)(2,1)S(1)} %to_rows.1.refs_0_), channel_id=1, source_target_pairs={{0,4},{8,12},{1,5},{9,13},{2,6},{10,14},{3,7},{11,15},{16,20},{24,... | collective-permute-start | bytes 380936 | tf_op jit(solution)/shard_map/ppermute | solution.py:56
  61.0 6.5 %collective-permute-start = (bf16[496,128]{1,0:T(8,128)(2,1)S(1)}, bf16[496,128]{1,0:T(8,128)(2,1)S(1)}, u32[]{:S(2)}, u32[]{:S(2)}) collective-permute-start(bf16[496,128]{1,0:T(8,128)(2,1)S(1)} %to_rows.1.refs_0_), channel_id=1, source_target_pairs={{0,16},{8,24},{1,17},{9,25},{2,18},{10,26},{3,19},{11,27},{16,0},{... | collective-permute-start | bytes 380936 | tf_op jit(solution)/shard_map/ppermute | solution.py:56
  61.5 6.5 %collective-permute-start.3 = (bf16[496,128]{1,0:T(8,128)(2,1)S(1)}, bf16[496,128]{1,0:T(8,128)(2,1)S(1)}, u32[]{:S(2)}, u32[]{:S(2)}) collective-permute-start(bf16[496,128]{1,0:T(8,128)(2,1)S(1)} %to_rows.1.refs_0_), channel_id=1, source_target_pairs={{0,8},{8,0},{1,9},{9,1},{2,10},{10,2},{3,11},{11,3},{16,24},{24,16... | collective-permute-start | bytes 380936 | tf_op jit(solution)/shard_map/ppermute | solution.py:56
  65.3 2.7 %collective-permute-start.6 = (bf16[496,128]{1,0:T(8,128)(2,1)S(1)}, bf16[496,128]{1,0:T(8,128)(2,1)S(1)}, u32[]{:S(2)}, u32[]{:S(2)}) collective-permute-start(bf16[496,128]{1,0:T(8,128)(2,1)S(1)} %collective-permute-done.2.refs_3_), channel_id=1, source_target_pairs={{0,8},{8,0},{1,9},{9,1},{2,10},{10,2},{3,11},{11,3},{16,24},{24,16... | collective-permute-start | bytes 380936 | tf_op jit(solution)/shard_map/ppermute | solution.py:56
  67.5 1.3 %collective-permute-start.5 = (bf16[496,128]{1,0:T(8,128)(2,1)S(1)}, bf16[496,128]{1,0:T(8,128)(2,1)S(1)}, u32[]{:S(2)}, u32[]{:S(2)}) collective-permute-start(bf16[496,128]{1,0:T(8,128)(2,1)S(1)} %collective-permute-done.1.refs_2_), channel_id=1, source_target_pairs={{0,8},{8,0},{1,9},{9,1},{2,10},{10,2},{3,11},{11,3},{16,24},{24,16... | collective-permute-start | bytes 380936 | tf_op jit(solution)/shard_map/ppermute | solution.py:56
  67.5 1.5 %collective-permute-start.4 = (bf16[496,128]{1,0:T(8,128)(2,1)S(1)}, bf16[496,128]{1,0:T(8,128)(2,1)S(1)}, u32[]{:S(2)}, u32[]{:S(2)}) collective-permute-start(bf16[496,128]{1,0:T(8,128)(2,1)S(1)} %collective-permute-done.refs_1_), channel_id=1, source_target_pairs={{0,8},{8,0},{1,9},{9,1},{2,10},{10,2},{3,11},{11,3},{16,24},{24,16... | collective-permute-start | bytes 380936 | tf_op jit(solution)/shard_map/ppermute | solution.py:56
  69.0 2.4 %copy-start = (bf16[1536,256]{1,0:T(8,128)(2,1)S(1)}, bf16[1536,256]{1,0:T(8,128)(2,1)}, u32[]{:S(2)}) copy-start(bf16[1536,256]{1,0:T(8,128)(2,1)} %get-tuple-element.51.refs_4_) | copy-start | bytes 2359300
  71.4 22.3 %collective-permute-start.18 = (bf16[1536,256]{1,0:T(8,128)(2,1)S(1)}, bf16[1536,256]{1,0:T(8,128)(2,1)S(1)}, u32[]{:S(2)}, u32[]{:S(2)}) collective-permute-start(bf16[1536,256]{1,0:T(8,128)(2,1)S(1)} %copy-done), channel_id=1, source_target_pairs={{0,16},{8,24},{1,17},{9,25},{2,18},{10,26},{3,19},{11,27},{16,0},{... | collective-permute-start | bytes 2359304 | tf_op jit(solution)/shard_map/ppermute | solution.py:56
  71.5 9.1 %collective-permute-start.12 = (bf16[352,256]{1,0:T(8,128)(2,1)S(1)}, bf16[352,256]{1,0:T(8,128)(2,1)S(1)}, u32[]{:S(2)}, u32[]{:S(2)}) collective-permute-start(bf16[352,256]{1,0:T(8,128)(2,1)S(1)} %get-tuple-element.46), channel_id=1, source_target_pairs={{0,3},{8,11},{1,0},{9,8},{2,1},{10,9},{3,2},{11,10},{16,19},{24,27... | collective-permute-start | bytes 540680 | tf_op jit(solution)/shard_map/ppermute | solution.py:56
  72.4 11.1 %collective-permute-start.13 = (bf16[352,256]{1,0:T(8,128)(2,1)S(1)}, bf16[352,256]{1,0:T(8,128)(2,1)S(1)}, u32[]{:S(2)}, u32[]{:S(2)}) collective-permute-start(bf16[352,256]{1,0:T(8,128)(2,1)S(1)} %get-tuple-element.47), channel_id=1, source_target_pairs={{0,2},{8,10},{1,3},{9,11},{2,0},{10,8},{3,1},{11,9},{16,18},{24,26... | collective-permute-start | bytes 540680 | tf_op jit(solution)/shard_map/ppermute | solution.py:56
  75.4 8.7 %collective-permute-start.14 = (bf16[352,256]{1,0:T(8,128)(2,1)S(1)}, bf16[352,256]{1,0:T(8,128)(2,1)S(1)}, u32[]{:S(2)}, u32[]{:S(2)}) collective-permute-start(bf16[352,256]{1,0:T(8,128)(2,1)S(1)} %get-tuple-element.48), channel_id=1, source_target_pairs={{0,1},{8,9},{1,2},{9,10},{2,3},{10,11},{3,0},{11,8},{16,17},{24,25... | collective-permute-start | bytes 540680 | tf_op jit(solution)/shard_map/ppermute | solution.py:56
  84.4 9.3 %collective-permute-start.16 = (bf16[160,128]{1,0:T(8,128)(2,1)S(1)}, bf16[160,128]{1,0:T(8,128)(2,1)S(1)}, u32[]{:S(2)}, u32[]{:S(2)}) collective-permute-start(bf16[160,128]{1,0:T(8,128)(2,1)S(1)} %get-tuple-element.49.refs_0_), channel_id=1, source_target_pairs={{0,4},{8,12},{1,5},{9,13},{2,6},{10,14},{3,7},{11,15},{16,20},{24,... | collective-permute-start | bytes 122888 | tf_op jit(solution)/shard_map/ppermute | solution.py:56
  87.8 5.9 %collective-permute-start.17 = (bf16[160,128]{1,0:T(8,128)(2,1)S(1)}, bf16[160,128]{1,0:T(8,128)(2,1)S(1)}, u32[]{:S(2)}, u32[]{:S(2)}) collective-permute-start(bf16[160,128]{1,0:T(8,128)(2,1)S(1)} %get-tuple-element.50), channel_id=1, source_target_pairs={{0,20},{8,28},{1,21},{9,29},{2,22},{10,30},{3,23},{11,31},{16,4},{... | collective-permute-start | bytes 122888 | tf_op jit(solution)/shard_map/ppermute | solution.py:56
  88.8 4.9 %collective-permute-start.15 = (bf16[160,128]{1,0:T(8,128)(2,1)S(1)}, bf16[160,128]{1,0:T(8,128)(2,1)S(1)}, u32[]{:S(2)}, u32[]{:S(2)}) collective-permute-start(bf16[160,128]{1,0:T(8,128)(2,1)S(1)} %get-tuple-element.50), channel_id=1, source_target_pairs={{0,16},{8,24},{1,17},{9,25},{2,18},{10,26},{3,19},{11,27},{16,0},{... | collective-permute-start | bytes 122888 | tf_op jit(solution)/shard_map/ppermute | solution.py:56
  95.0 27.1 %copy-start.2 = (bf16[256,128]{1,0:T(8,128)(2,1)S(1)}, bf16[256,128]{1,0:T(8,128)(2,1)}, u32[]{:S(2)}) copy-start(bf16[256,128]{1,0:T(8,128)(2,1)} %get-tuple-element.33.refs_6_.select) | copy-start | bytes 196612
  95.0 27.1 %copy-start.3 = (bf16[16,768]{1,0:T(8,128)(2,1)S(1)}, bf16[16,768]{1,0:T(8,128)(2,1)}, u32[]{:S(2)}) copy-start(bf16[16,768]{1,0:T(8,128)(2,1)} %get-tuple-element.58.hidden) | copy-start | bytes 73732
  95.0 2.0 %collective-permute-start.19 = (bf16[4,480,128]{2,1,0:T(8,128)(2,1)S(1)}, bf16[4,480,128]{2,1,0:T(8,128)(2,1)S(1)}, u32[]{:S(2)}, u32[]{:S(2)}) collective-permute-start(bf16[4,480,128]{2,1,0:T(8,128)(2,1)S(1)} %get-tuple-element.53), channel_id=1, source_target_pairs={{0,8},{8,0},{1,9},{9,1},{2,10},{10,2},{3,11},{11,3},{16,24},{24,16... | collective-permute-start | bytes 1474568 | tf_op jit(solution)/shard_map/ppermute | solution.py:56
  97.1 8.5 %collective-permute-start.20 = (bf16[480,128]{1,0:T(8,128)(2,1)S(1)}, bf16[480,128]{1,0:T(8,128)(2,1)S(1)}, u32[]{:S(2)}, u32[]{:S(2)}) collective-permute-start(bf16[480,128]{1,0:T(8,128)(2,1)S(1)} %get-tuple-element.55), channel_id=1, source_target_pairs={{0,1},{8,9},{1,2},{9,10},{2,3},{10,11},{3,0},{11,8},{16,17},{24,25... | collective-permute-start | bytes 368648 | tf_op jit(solution)/shard_map/ppermute | solution.py:56
  100.1 7.7 %collective-permute-start.21 = (bf16[480,128]{1,0:T(8,128)(2,1)S(1)}, bf16[480,128]{1,0:T(8,128)(2,1)S(1)}, u32[]{:S(2)}, u32[]{:S(2)}) collective-permute-start(bf16[480,128]{1,0:T(8,128)(2,1)S(1)} %get-tuple-element.56), channel_id=1, source_target_pairs={{0,2},{8,10},{1,3},{9,11},{2,0},{10,8},{3,1},{11,9},{16,18},{24,26... | collective-permute-start | bytes 368648 | tf_op jit(solution)/shard_map/ppermute | solution.py:56
  100.3 8.9 %collective-permute-start.22 = (bf16[480,128]{1,0:T(8,128)(2,1)S(1)}, bf16[480,128]{1,0:T(8,128)(2,1)S(1)}, u32[]{:S(2)}, u32[]{:S(2)}) collective-permute-start(bf16[480,128]{1,0:T(8,128)(2,1)S(1)} %get-tuple-element.57), channel_id=1, source_target_pairs={{0,3},{8,11},{1,0},{9,8},{2,1},{10,9},{3,2},{11,10},{16,19},{24,27... | collective-permute-start | bytes 368648 | tf_op jit(solution)/shard_map/ppermute | solution.py:56

commit v4 on v3

--- a/solution.py
+++ b/solution.py
@@ -573,7 +573,7 @@
         where, w_gate, w_up, w_down, expert_ids.T, queries
     )
     first = [blocks[0]] + [permute(blocks[n], along_x(n)) for n in (1, 2, 3)]
-    second = [permute(blocks[5], along_y(m)) for m in (2, 3)]
+    second = [permute(blocks[4], along_y(1)), permute(blocks[5], along_y(3))]
     outgoing = pack_pages(fresh_owner.T, fresh_kv.reshape(-1, page_len, page_width), n_attn)
     arrived = lax.all_to_all(
         outgoing, "attn", 0, 0, axis_index_groups=PAGE_GROUPS, tiled=True
@@ -594,8 +594,8 @@
     own = gather4(to_rows(exchange_z(payload)), along_y)
     other = [permute(v, OTHER_CORE) for v in own]
     parts = gate_up(where, own, other, first, second)
-    near, *parts = lax.optimization_barrier((blocks[4], *parts))
-    second = [blocks[4], permute(near, along_y(1))] + second
+    far, *parts = lax.optimization_barrier((blocks[5], *parts))
+    second = [blocks[4], second[0], permute(far, along_y(2)), second[1]]
     active = activate([parts[0]] + [permute(parts[n], along_x(-n)) for n in (1, 2, 3)])
     active = [active[0]] + [permute(active[m % 2], along_y(m)) for m in (1, 2, 3)]
     made, for_other = down(where, active, second)

time: 123 us -> 123 us (level)
  starting transfers between devices: 35.4 us -> 33.9 us
    ppermute x23, starting transfers between devices: 25 us -> 23.6 us  [permute(): return lax.ppermute(value, AXES, perm)]
where the time goes in v4:
time: 123 us; the launch traced here: 122 us
  waiting for transfers between devices  40.8 us (33%)
  starting transfers between devices  33.9 us (28%)
  blocking collectives  26.3 us (21%)
  Pallas kernels  19 us (15%)
    ppermute x23, waiting for transfers between devices, permute(): return lax.ppermute(value, AXES, perm)  29.7 us
    all_to_all x2, blocking collectives, exchange_z(): lax.all_to_all(slabs, 'attn', 0, 0, axis_index_groups=Z_GROUPS, tiled=True)  26.3 us
    ppermute x23, starting transfers between devices, permute(): return lax.ppermute(value, AXES, perm)  23.6 us
    all_to_all x1, waiting for transfers between devices, on_device(): lax.all_to_all(outgoing, 'attn', 0, 0, axis_index_groups=PAGE_GROUPS, til...  11 us
    all_to_all x1, starting transfers between devices, on_device(): lax.all_to_all(outgoing, 'attn', 0, 0, axis_index_groups=PAGE_GROUPS, til...  10.3 us
    pallas_call x1, Pallas kernels, prepare(): pl.pallas_call(prepare_kernel, out_shape=(shape(block, BF16),) * 6 + (sha...  5.9 us
    pallas_call x1, Pallas kernels, attend(): pl.pallas_call(attend_kernel, out_shape=(shape(kv_pool.shape, kv_pool.dty...  5.06 us
    pallas_call x1, Pallas kernels, pack_pages(): pl.pallas_call(pack_pages_kernel, out_shape=jax.ShapeDtypeStruct((n_attn...  2.5 us
  transfers between devices with their start and end apart: 24, of which 13 were waited for; matrix products, arithmetic and copies ran while one was open for 1% of the time, Pallas kernels for 9%

profile of v4, /device:TPU:6, one launch (start us, length us, event | category | flops | bytes accessed | tf_op | source)
XLA Modules:
  0.0 122.0 jit_solution(6677937650233287639)
XLA Ops:
  0.6 2.5 %pack_pages.1 = bf16[128,16,256]{2,1,0:T(8,128)(2,1)} custom-call(s32[1,32]{1,0:T(1,128)} %bitcast.14, bf16[32,16,256]{2,1,0:T(8,128)(2,1)} %bitcast.11), custom_call_target="tpu_custom_call" | custom-call | tf_op jit(solution)/shard_map/pack_pages/pallas_call | solution.py:108
  3.1 10.3 %all-to-all-start = ((bf16[128,16,256]{2,1,0:T(8,128)(2,1)}), bf16[128,16,256]{2,1,0:T(8,128)(2,1)}, u32[]{:S(2)}, u32[]{:S(2)}) async-start(bf16[128,16,256]{2,1,0:T(8,128)(2,1)} %pack_pages.1), calls=%async_computation | async-start | bytes 2097152 | tf_op jit(solution)/shard_map/all_to_all | solution.py:578
  13.5 0.6 pad_add_fusion.where
  14.1 5.9 %prepare.1 = (bf16[1536,256]{1,0:T(8,128)(2,1)}, bf16[1536,256]{1,0:T(8,128)(2,1)}, bf16[1536,256]{1,0:T(8,128)(2,1)}, bf16[1536,256]{1,0:T(8,128)(2,1)}, bf16[1...) custom-call(s32[2]{0:T(128)} %pad_add_fusion.where, ...), custom_call_target="tpu_custom_call" | custom-call | tf_op jit(solution)/shard_map/prepare/pallas_call | solution.py:333
  20.0 0.6 collective-permute-start.7
  20.5 2.4 %collective-permute-start.8 = (bf16[1536,256]{1,0:T(8,128)(2,1)}, bf16[1536,256]{1,0:T(8,128)(2,1)S(1)}, u32[]{:S(2)}, u32[]{:S(2)}) collective-permute-start(bf16[1536,256]{1,0:T(8,128)(2,1)} %get-tuple-element.38), channel_id=1, source_target_pairs={{0,2},{8,10},{1,3},{9,11},{2,0},{10,8},{3,1},{11,9},{16,18},{24,26... | collective-permute-start | bytes 2359304 | tf_op jit(solution)/shard_map/ppermute | solution.py:56
  22.9 0.0 collective-permute-start.9
  22.9 3.2 %collective-permute-start.11 = (bf16[1536,256]{1,0:T(8,128)(2,1)}, bf16[1536,256]{1,0:T(8,128)(2,1)S(1)}, u32[]{:S(2)}, u32[]{:S(2)}) collective-permute-start(bf16[1536,256]{1,0:T(8,128)(2,1)} %get-tuple-element.51), channel_id=1, source_target_pairs={{0,20},{8,28},{1,21},{9,29},{2,22},{10,30},{3,23},{11,31},{16,4},{... | collective-permute-start | bytes 2359304 | tf_op jit(solution)/shard_map/ppermute | solution.py:56
  26.1 0.0 collective-permute-start.10
  26.1 0.6 reshape.18.refs_4_
  26.7 11.0 %all-to-all-done.refs_1_ = bf16[128,16,256]{2,1,0:T(8,128)(2,1)} async-done(((bf16[128,16,256]{2,1,0:T(8,128)(2,1)}), bf16[128,16,256]{2,1,0:T(8,128)(2,1)}, u32[]{:S(2)}, u32[]{:S(2)}) %all-to-all-start) | async-done | bytes 1048608 | tf_op jit(solution)/shard_map/all_to_all | solution.py:578
  37.8 5.1 %attend.1 = (bf16[320,16,256]{2,1,0:T(8,128)(2,1)}, bf16[16,768]{1,0:T(8,128)(2,1)}, bf16[8,64,128]{2,1,0:T(8,128)(2,1)}) custom-call(s32[16,16]{1,0:T(8,128)} %table.1, s32[1,16]{1,0:T(1,128)} %lengths.1, bf16[320,16,256]{2,1,0:T(8,128)(2,1)} %bitcast.10, bf16[128,16,256]{2,1,0:T(8,128)(2,1)} %all-to-all-done.refs_1_, ...), custom_call_target="tpu_custom_call" | custom-call | tf_op jit(solution)/shard_map/attend/pallas_call | solution.py:269
  42.8 14.0 %all_to_all.15.slabs = bf16[8,64,128]{2,1,0:T(8,128)(2,1)S(1)} all-to-all(bf16[8,64,128]{2,1,0:T(8,128)(2,1)} %get-tuple-element.35), channel_id=1, replica_groups={{224,192,160,128,96,64,32,0},{232,200,168,136,104,72,40,8},{240,208,176..., dimensions={0} | all-to-all | bytes 262144 | tf_op jit(solution)/shard_map/all_to_all | solution.py:549
  56.9 0.3 to_rows.1.refs_0_
  57.2 0.0 collective-permute-done.7.refs_9_
  57.2 3.4 %collective-permute-start.2 = (bf16[496,128]{1,0:T(8,128)(2,1)S(1)}, bf16[496,128]{1,0:T(8,128)(2,1)S(1)}, u32[]{:S(2)}, u32[]{:S(2)}) collective-permute-start(bf16[496,128]{1,0:T(8,128)(2,1)S(1)} %to_rows.1.refs_0_), channel_id=1, source_target_pairs={{0,20},{8,28},{1,21},{9,29},{2,22},{10,30},{3,23},{11,31},{16,4},{... | collective-permute-start | bytes 380936 | tf_op jit(solution)/shard_map/ppermute | solution.py:56
  60.5 0.0 collective-permute-done.8.refs_10_
  60.5 0.5 collective-permute-start.1
  61.1 0.0 collective-permute-done.9.refs_11_
  61.1 0.4 collective-permute-start
  61.5 0.0 collective-permute-done.11.refs_13_.refs_7_
  61.5 0.0 collective-permute-start.3
  61.5 3.6 %collective-permute-done.2.refs_3_ = bf16[496,128]{1,0:T(8,128)(2,1)S(1)} collective-permute-done((bf16[496,128]{1,0:T(8,128)(2,1)S(1)}, bf16[496,128]{1,0:T(8,128)(2,1)S(1)}, u32[]{:S(2)}, u32[]{:S(2)}) %collective-permute-start.2) | collective-permute-done | bytes 127008 | tf_op jit(solution)/shard_map/ppermute | solution.py:56
  65.1 0.0 collective-permute-start.6
  65.1 2.3 %collective-permute-done.1.refs_2_ = bf16[496,128]{1,0:T(8,128)(2,1)S(1)} collective-permute-done((bf16[496,128]{1,0:T(8,128)(2,1)S(1)}, bf16[496,128]{1,0:T(8,128)(2,1)S(1)}, u32[]{:S(2)}, u32[]{:S(2)}) %collective-permute-start.1) | collective-permute-done | bytes 127008 | tf_op jit(solution)/shard_map/ppermute | solution.py:56
  67.5 0.0 collective-permute-start.5
  67.5 0.0 collective-permute-done.refs_1_
  67.5 0.5 collective-permute-start.4
  68.0 0.0 collective-permute-done.10.refs_12_.refs_5_
  68.0 0.0 collective-permute-done.3.refs_4_
  68.0 0.0 collective-permute-done.6.refs_7_
  68.0 0.8 collective-permute-done.5.refs_6_
  68.8 0.2 collective-permute-done.4.refs_5_
  69.0 0.0 copy-done.4
  69.0 2.5 %gate_up.1 = (f32[352,256]{1,0:T(8,128)S(1)}, bf16[352,256]{1,0:T(8,128)(2,1)S(1)}, bf16[352,256]{1,0:T(8,128)(2,1)S(1)}, bf16[352,256]{1,0:T(8,128)(2,1)S(1)}) custom-call(s32[2]{0:T(128)S(1)} %copy-done.4, bf16[496,128]{1,0:T(8,128)(2,1)S(1)} %to_rows.1.refs_0_, bf16[496,128]{1,0:T(8,128)(2,1)S(1)} %collective-permute-done.refs_1_, ...), custom_call_target="tpu_custom_call" | custom-call | tf_op jit(solution)/shard_map/gate_up/pallas_call | solution.py:405
  71.5 1.8 %collective-permute-start.18 = (bf16[1536,256]{1,0:T(8,128)(2,1)S(1)}, bf16[1536,256]{1,0:T(8,128)(2,1)S(1)}, u32[]{:S(2)}, u32[]{:S(2)}) collective-permute-start(bf16[1536,256]{1,0:T(8,128)(2,1)S(1)} %copy-done.6), channel_id=1, source_target_pairs={{0,4},{8,12},{1,5},{9,13},{2,6},{10,14},{3,7},{11,15},{16,20},{24,... | collective-permute-start | bytes 2359304 | tf_op jit(solution)/shard_map/ppermute | solution.py:56
  73.2 0.8 collective-permute-start.12
  74.1 1.6 %collective-permute-start.13 = (bf16[352,256]{1,0:T(8,128)(2,1)S(1)}, bf16[352,256]{1,0:T(8,128)(2,1)S(1)}, u32[]{:S(2)}, u32[]{:S(2)}) collective-permute-start(bf16[352,256]{1,0:T(8,128)(2,1)S(1)} %get-tuple-element.47), channel_id=1, source_target_pairs={{0,2},{8,10},{1,3},{9,11},{2,0},{10,8},{3,1},{11,9},{16,18},{24,26... | collective-permute-start | bytes 540680 | tf_op jit(solution)/shard_map/ppermute | solution.py:56
  75.7 1.6 %collective-permute-start.14 = (bf16[352,256]{1,0:T(8,128)(2,1)S(1)}, bf16[352,256]{1,0:T(8,128)(2,1)S(1)}, u32[]{:S(2)}, u32[]{:S(2)}) collective-permute-start(bf16[352,256]{1,0:T(8,128)(2,1)S(1)} %get-tuple-element.48), channel_id=1, source_target_pairs={{0,1},{8,9},{1,2},{9,10},{2,3},{10,11},{3,0},{11,8},{16,17},{24,25... | collective-permute-start | bytes 540680 | tf_op jit(solution)/shard_map/ppermute | solution.py:56
  77.3 7.4 %collective-permute-done.12.refs_1_ = bf16[352,256]{1,0:T(8,128)(2,1)S(1)} collective-permute-done((bf16[352,256]{1,0:T(8,128)(2,1)S(1)}, bf16[352,256]{1,0:T(8,128)(2,1)S(1)}, u32[]{:S(2)}, u32[]{:S(2)}) %collective-permute-start.12) | collective-permute-done | bytes 180256 | tf_op jit(solution)/shard_map/ppermute | solution.py:56
  84.6 0.0 collective-permute-done.13.refs_2_
  84.6 0.6 collective-permute-done.14.refs_3_
  85.3 0.3 activate.1
  85.6 2.1 %collective-permute-start.16 = (bf16[160,128]{1,0:T(8,128)(2,1)S(1)}, bf16[160,128]{1,0:T(8,128)(2,1)S(1)}, u32[]{:S(2)}, u32[]{:S(2)}) collective-permute-start(bf16[160,128]{1,0:T(8,128)(2,1)S(1)} %get-tuple-element.49.refs_0_), channel_id=1, source_target_pairs={{0,4},{8,12},{1,5},{9,13},{2,6},{10,14},{3,7},{11,15},{16,20},{24,... | collective-permute-start | bytes 122888 | tf_op jit(solution)/shard_map/ppermute | solution.py:56
  87.7 1.6 %collective-permute-start.17 = (bf16[160,128]{1,0:T(8,128)(2,1)S(1)}, bf16[160,128]{1,0:T(8,128)(2,1)S(1)}, u32[]{:S(2)}, u32[]{:S(2)}) collective-permute-start(bf16[160,128]{1,0:T(8,128)(2,1)S(1)} %get-tuple-element.50), channel_id=1, source_target_pairs={{0,20},{8,28},{1,21},{9,29},{2,22},{10,30},{3,23},{11,31},{16,4},{... | collective-permute-start | bytes 122888 | tf_op jit(solution)/shard_map/ppermute | solution.py:56
  89.3 0.0 collective-permute-start.15
  89.3 5.0 %collective-permute-done.16.refs_2_ = bf16[160,128]{1,0:T(8,128)(2,1)S(1)} collective-permute-done((bf16[160,128]{1,0:T(8,128)(2,1)S(1)}, bf16[160,128]{1,0:T(8,128)(2,1)S(1)}, u32[]{:S(2)}, u32[]{:S(2)}) %collective-permute-start.16) | collective-permute-done | bytes 40992 | tf_op jit(solution)/shard_map/ppermute | solution.py:56
  94.2 0.4 collective-permute-done.17.refs_3_
  94.6 0.0 collective-permute-done.15.refs_1_
  94.6 0.0 collective-permute-done.18.refs_6_
  94.6 1.2 %down.1 = (bf16[4,480,128]{2,1,0:T(8,128)(2,1)S(1)}, bf16[4,480,128]{2,1,0:T(8,128)(2,1)S(1)}) custom-call(s32[2]{0:T(128)S(1)} %copy-done.4, bf16[160,128]{1,0:T(8,128)(2,1)S(1)} %get-tuple-element.49.refs_0_, bf16[160,128]{1,0:T(8,128)(2,1)S(1)} %collective-permute-done.15.refs_1_, bf16[160,128]{1,0:T(8,128)(2,1)S(1)} %collective-permute-done.16.refs_2_, ...), custom_call_target="tpu_custom_call" | custom-call | tf_op jit(solution)/shard_map/down/pallas_call | solution.py:473
  95.9 0.0 copy-start.3
  95.9 0.1 collective-permute-start.19
  96.0 1.8 %collective-permute-done.19.other = bf16[4,480,128]{2,1,0:T(8,128)(2,1)S(1)} collective-permute-done((bf16[4,480,128]{2,1,0:T(8,128)(2,1)S(1)}, bf16[4,480,128]{2,1,0:T(8,128)(2,1)S(1)}, u32[]{:S(2)}, u32[]{:S(2)}) %collective-permute-start.19) | collective-permute-done | bytes 491552 | tf_op jit(solution)/shard_map/ppermute | solution.py:56
  97.8 0.1 add_cores.1
  98.0 1.4 %collective-permute-start.20 = (bf16[480,128]{1,0:T(8,128)(2,1)S(1)}, bf16[480,128]{1,0:T(8,128)(2,1)S(1)}, u32[]{:S(2)}, u32[]{:S(2)}) collective-permute-start(bf16[480,128]{1,0:T(8,128)(2,1)S(1)} %get-tuple-element.55), channel_id=1, source_target_pairs={{0,1},{8,9},{1,2},{9,10},{2,3},{10,11},{3,0},{11,8},{16,17},{24,25... | collective-permute-start | bytes 368648 | tf_op jit(solution)/shard_map/ppermute | solution.py:56
  99.3 1.6 %collective-permute-start.21 = (bf16[480,128]{1,0:T(8,128)(2,1)S(1)}, bf16[480,128]{1,0:T(8,128)(2,1)S(1)}, u32[]{:S(2)}, u32[]{:S(2)}) collective-permute-start(bf16[480,128]{1,0:T(8,128)(2,1)S(1)} %get-tuple-element.56), channel_id=1, source_target_pairs={{0,2},{8,10},{1,3},{9,11},{2,0},{10,8},{3,1},{11,9},{16,18},{24,26... | collective-permute-start | bytes 368648 | tf_op jit(solution)/shard_map/ppermute | solution.py:56
  100.9 0.0 collective-permute-start.22
  100.9 3.3 %collective-permute-done.20.refs_1_ = bf16[480,128]{1,0:T(8,128)(2,1)S(1)} collective-permute-done((bf16[480,128]{1,0:T(8,128)(2,1)S(1)}, bf16[480,128]{1,0:T(8,128)(2,1)S(1)}, u32[]{:S(2)}, u32[]{:S(2)}) %collective-permute-start.20) | collective-permute-done | bytes 122912 | tf_op jit(solution)/shard_map/ppermute | solution.py:56
  104.2 2.8 %collective-permute-done.21.refs_2_ = bf16[480,128]{1,0:T(8,128)(2,1)S(1)} collective-permute-done((bf16[480,128]{1,0:T(8,128)(2,1)S(1)}, bf16[480,128]{1,0:T(8,128)(2,1)S(1)}, u32[]{:S(2)}, u32[]{:S(2)}) %collective-permute-start.21) | collective-permute-done | bytes 122912 | tf_op jit(solution)/shard_map/ppermute | solution.py:56
  107.0 1.5 %collective-permute-done.22.refs_3_ = bf16[480,128]{1,0:T(8,128)(2,1)S(1)} collective-permute-done((bf16[480,128]{1,0:T(8,128)(2,1)S(1)}, bf16[480,128]{1,0:T(8,128)(2,1)S(1)}, u32[]{:S(2)}, u32[]{:S(2)}) %collective-permute-start.22) | collective-permute-done | bytes 122912 | tf_op jit(solution)/shard_map/ppermute | solution.py:56
  108.5 0.3 to_slabs.1
  108.9 12.3 %all_to_all.16.slabs = bf16[8,64,128]{2,1,0:T(8,128)(2,1)S(1)} all-to-all(bf16[8,64,128]{2,1,0:T(8,128)(2,1)S(1)} %to_slabs.1), channel_id=1, replica_groups={{224,192,160,128,96,64,32,0},{232,200,168,136,104,72,40,8},{240,208,176..., dimensions={0} | all-to-all | bytes 262144 | tf_op jit(solution)/shard_map/all_to_all | solution.py:549
  121.1 0.8 combine.1
  (12 shorter events, 0.0 us)
Async XLA Ops:
  3.1 34.6 %all-to-all-start = ((bf16[128,16,256]{2,1,0:T(8,128)(2,1)}), bf16[128,16,256]{2,1,0:T(8,128)(2,1)}, u32[]{:S(2)}, u32[]{:S(2)}) async-start(bf16[128,16,256]{2,1,0:T(8,128)(2,1)} %pack_pages.1), calls=%async_computation | async-start | bytes 2097152 | tf_op jit(solution)/shard_map/all_to_all | solution.py:578
  14.1 12.1 %copy-start.5 = (bf16[768]{0:T(1024)(128)(2,1)S(1)}, bf16[768]{0:T(1024)(128)(2,1)}, u32[]{:S(2)}) copy-start(bf16[768]{0:T(1024)(128)(2,1)} %param.20) | copy-start | bytes 4612
  20.0 37.2 %collective-permute-start.7 = (bf16[1536,256]{1,0:T(8,128)(2,1)}, bf16[1536,256]{1,0:T(8,128)(2,1)S(1)}, u32[]{:S(2)}, u32[]{:S(2)}) collective-permute-start(bf16[1536,256]{1,0:T(8,128)(2,1)} %get-tuple-element.37), channel_id=1, source_target_pairs={{0,1},{8,9},{1,2},{9,10},{2,3},{10,11},{3,0},{11,8},{16,17},{24,25... | collective-permute-start | bytes 2359304 | tf_op jit(solution)/shard_map/ppermute | solution.py:56
  20.5 40.0 %collective-permute-start.8 = (bf16[1536,256]{1,0:T(8,128)(2,1)}, bf16[1536,256]{1,0:T(8,128)(2,1)S(1)}, u32[]{:S(2)}, u32[]{:S(2)}) collective-permute-start(bf16[1536,256]{1,0:T(8,128)(2,1)} %get-tuple-element.38), channel_id=1, source_target_pairs={{0,2},{8,10},{1,3},{9,11},{2,0},{10,8},{3,1},{11,9},{16,18},{24,26... | collective-permute-start | bytes 2359304 | tf_op jit(solution)/shard_map/ppermute | solution.py:56
  22.9 38.1 %collective-permute-start.9 = (bf16[1536,256]{1,0:T(8,128)(2,1)}, bf16[1536,256]{1,0:T(8,128)(2,1)}, u32[]{:S(2)}, u32[]{:S(2)}) collective-permute-start(bf16[1536,256]{1,0:T(8,128)(2,1)} %get-tuple-element.39), channel_id=1, source_target_pairs={{0,3},{8,11},{1,0},{9,8},{2,1},{10,9},{3,2},{11,10},{16,19},{24,27... | collective-permute-start | bytes 2359304 | tf_op jit(solution)/shard_map/ppermute | solution.py:56
  22.9 38.6 %collective-permute-start.11 = (bf16[1536,256]{1,0:T(8,128)(2,1)}, bf16[1536,256]{1,0:T(8,128)(2,1)S(1)}, u32[]{:S(2)}, u32[]{:S(2)}) collective-permute-start(bf16[1536,256]{1,0:T(8,128)(2,1)} %get-tuple-element.51), channel_id=1, source_target_pairs={{0,20},{8,28},{1,21},{9,29},{2,22},{10,30},{3,23},{11,31},{16,4},{... | collective-permute-start | bytes 2359304 | tf_op jit(solution)/shard_map/ppermute | solution.py:56
  26.1 41.9 %collective-permute-start.10 = (bf16[1536,256]{1,0:T(8,128)(2,1)}, bf16[1536,256]{1,0:T(8,128)(2,1)S(1)}, u32[]{:S(2)}, u32[]{:S(2)}) collective-permute-start(bf16[1536,256]{1,0:T(8,128)(2,1)} %get-tuple-element.40.refs_4_), channel_id=1, source_target_pairs={{0,16},{8,24},{1,17},{9,25},{2,18},{10,26},{3,19},{11,27},{16,0},{... | collective-permute-start | bytes 2359304 | tf_op jit(solution)/shard_map/ppermute | solution.py:56
  37.7 31.2 %copy-start.1 = (bf16[1536,256]{1,0:T(8,128)(2,1)S(1)}, bf16[1536,256]{1,0:T(8,128)(2,1)}, u32[]{:S(2)}) copy-start(bf16[1536,256]{1,0:T(8,128)(2,1)} %get-tuple-element.36.refs_8_) | copy-start | bytes 2359300
  37.8 31.2 %copy-start.4 = (s32[2]{0:T(128)S(1)}, s32[2]{0:T(128)}, u32[]{:S(2)}) copy-start(s32[2]{0:T(128)} %pad_add_fusion.where) | copy-start | bytes 28
  57.2 8.0 %collective-permute-start.2 = (bf16[496,128]{1,0:T(8,128)(2,1)S(1)}, bf16[496,128]{1,0:T(8,128)(2,1)S(1)}, u32[]{:S(2)}, u32[]{:S(2)}) collective-permute-start(bf16[496,128]{1,0:T(8,128)(2,1)S(1)} %to_rows.1.refs_0_), channel_id=1, source_target_pairs={{0,20},{8,28},{1,21},{9,29},{2,22},{10,30},{3,23},{11,31},{16,4},{... | collective-permute-start | bytes 380936 | tf_op jit(solution)/shard_map/ppermute | solution.py:56
  60.5 6.9 %collective-permute-start.1 = (bf16[496,128]{1,0:T(8,128)(2,1)S(1)}, bf16[496,128]{1,0:T(8,128)(2,1)S(1)}, u32[]{:S(2)}, u32[]{:S(2)}) collective-permute-start(bf16[496,128]{1,0:T(8,128)(2,1)S(1)} %to_rows.1.refs_0_), channel_id=1, source_target_pairs={{0,4},{8,12},{1,5},{9,13},{2,6},{10,14},{3,7},{11,15},{16,20},{24,... | collective-permute-start | bytes 380936 | tf_op jit(solution)/shard_map/ppermute | solution.py:56
  61.1 6.4 %collective-permute-start = (bf16[496,128]{1,0:T(8,128)(2,1)S(1)}, bf16[496,128]{1,0:T(8,128)(2,1)S(1)}, u32[]{:S(2)}, u32[]{:S(2)}) collective-permute-start(bf16[496,128]{1,0:T(8,128)(2,1)S(1)} %to_rows.1.refs_0_), channel_id=1, source_target_pairs={{0,16},{8,24},{1,17},{9,25},{2,18},{10,26},{3,19},{11,27},{16,0},{... | collective-permute-start | bytes 380936 | tf_op jit(solution)/shard_map/ppermute | solution.py:56
  61.5 6.5 %collective-permute-start.3 = (bf16[496,128]{1,0:T(8,128)(2,1)S(1)}, bf16[496,128]{1,0:T(8,128)(2,1)S(1)}, u32[]{:S(2)}, u32[]{:S(2)}) collective-permute-start(bf16[496,128]{1,0:T(8,128)(2,1)S(1)} %to_rows.1.refs_0_), channel_id=1, source_target_pairs={{0,8},{8,0},{1,9},{9,1},{2,10},{10,2},{3,11},{11,3},{16,24},{24,16... | collective-permute-start | bytes 380936 | tf_op jit(solution)/shard_map/ppermute | solution.py:56
  65.1 2.9 %collective-permute-start.6 = (bf16[496,128]{1,0:T(8,128)(2,1)S(1)}, bf16[496,128]{1,0:T(8,128)(2,1)S(1)}, u32[]{:S(2)}, u32[]{:S(2)}) collective-permute-start(bf16[496,128]{1,0:T(8,128)(2,1)S(1)} %collective-permute-done.2.refs_3_), channel_id=1, source_target_pairs={{0,8},{8,0},{1,9},{9,1},{2,10},{10,2},{3,11},{11,3},{16,24},{24,16... | collective-permute-start | bytes 380936 | tf_op jit(solution)/shard_map/ppermute | solution.py:56
  67.5 1.3 %collective-permute-start.5 = (bf16[496,128]{1,0:T(8,128)(2,1)S(1)}, bf16[496,128]{1,0:T(8,128)(2,1)S(1)}, u32[]{:S(2)}, u32[]{:S(2)}) collective-permute-start(bf16[496,128]{1,0:T(8,128)(2,1)S(1)} %collective-permute-done.1.refs_2_), channel_id=1, source_target_pairs={{0,8},{8,0},{1,9},{9,1},{2,10},{10,2},{3,11},{11,3},{16,24},{24,16... | collective-permute-start | bytes 380936 | tf_op jit(solution)/shard_map/ppermute | solution.py:56
  67.5 1.5 %collective-permute-start.4 = (bf16[496,128]{1,0:T(8,128)(2,1)S(1)}, bf16[496,128]{1,0:T(8,128)(2,1)S(1)}, u32[]{:S(2)}, u32[]{:S(2)}) collective-permute-start(bf16[496,128]{1,0:T(8,128)(2,1)S(1)} %collective-permute-done.refs_1_), channel_id=1, source_target_pairs={{0,8},{8,0},{1,9},{9,1},{2,10},{10,2},{3,11},{11,3},{16,24},{24,16... | collective-permute-start | bytes 380936 | tf_op jit(solution)/shard_map/ppermute | solution.py:56
  69.0 2.5 %copy-start.6 = (bf16[1536,256]{1,0:T(8,128)(2,1)S(1)}, bf16[1536,256]{1,0:T(8,128)(2,1)}, u32[]{:S(2)}) copy-start(bf16[1536,256]{1,0:T(8,128)(2,1)} %get-tuple-element.51) | copy-start | bytes 2359300
  69.0 25.6 %copy-start = (bf16[1536,256]{1,0:T(8,128)(2,1)S(1)}, bf16[1536,256]{1,0:T(8,128)(2,1)}, u32[]{:S(2)}) copy-start(bf16[1536,256]{1,0:T(8,128)(2,1)} %get-tuple-element.40.refs_4_) | copy-start | bytes 2359300
  71.5 23.1 %collective-permute-start.18 = (bf16[1536,256]{1,0:T(8,128)(2,1)S(1)}, bf16[1536,256]{1,0:T(8,128)(2,1)S(1)}, u32[]{:S(2)}, u32[]{:S(2)}) collective-permute-start(bf16[1536,256]{1,0:T(8,128)(2,1)S(1)} %copy-done.6), channel_id=1, source_target_pairs={{0,4},{8,12},{1,5},{9,13},{2,6},{10,14},{3,7},{11,15},{16,20},{24,... | collective-permute-start | bytes 2359304 | tf_op jit(solution)/shard_map/ppermute | solution.py:56
  73.2 11.4 %collective-permute-start.12 = (bf16[352,256]{1,0:T(8,128)(2,1)S(1)}, bf16[352,256]{1,0:T(8,128)(2,1)S(1)}, u32[]{:S(2)}, u32[]{:S(2)}) collective-permute-start(bf16[352,256]{1,0:T(8,128)(2,1)S(1)} %get-tuple-element.46), channel_id=1, source_target_pairs={{0,3},{8,11},{1,0},{9,8},{2,1},{10,9},{3,2},{11,10},{16,19},{24,27... | collective-permute-start | bytes 540680 | tf_op jit(solution)/shard_map/ppermute | solution.py:56
  74.1 10.6 %collective-permute-start.13 = (bf16[352,256]{1,0:T(8,128)(2,1)S(1)}, bf16[352,256]{1,0:T(8,128)(2,1)S(1)}, u32[]{:S(2)}, u32[]{:S(2)}) collective-permute-start(bf16[352,256]{1,0:T(8,128)(2,1)S(1)} %get-tuple-element.47), channel_id=1, source_target_pairs={{0,2},{8,10},{1,3},{9,11},{2,0},{10,8},{3,1},{11,9},{16,18},{24,26... | collective-permute-start | bytes 540680 | tf_op jit(solution)/shard_map/ppermute | solution.py:56
  75.7 9.5 %collective-permute-start.14 = (bf16[352,256]{1,0:T(8,128)(2,1)S(1)}, bf16[352,256]{1,0:T(8,128)(2,1)S(1)}, u32[]{:S(2)}, u32[]{:S(2)}) collective-permute-start(bf16[352,256]{1,0:T(8,128)(2,1)S(1)} %get-tuple-element.48), channel_id=1, source_target_pairs={{0,1},{8,9},{1,2},{9,10},{2,3},{10,11},{3,0},{11,8},{16,17},{24,25... | collective-permute-start | bytes 540680 | tf_op jit(solution)/shard_map/ppermute | solution.py:56
  85.6 8.6 %collective-permute-start.16 = (bf16[160,128]{1,0:T(8,128)(2,1)S(1)}, bf16[160,128]{1,0:T(8,128)(2,1)S(1)}, u32[]{:S(2)}, u32[]{:S(2)}) collective-permute-start(bf16[160,128]{1,0:T(8,128)(2,1)S(1)} %get-tuple-element.49.refs_0_), channel_id=1, source_target_pairs={{0,4},{8,12},{1,5},{9,13},{2,6},{10,14},{3,7},{11,15},{16,20},{24,... | collective-permute-start | bytes 122888 | tf_op jit(solution)/shard_map/ppermute | solution.py:56
  87.7 6.9 %collective-permute-start.17 = (bf16[160,128]{1,0:T(8,128)(2,1)S(1)}, bf16[160,128]{1,0:T(8,128)(2,1)S(1)}, u32[]{:S(2)}, u32[]{:S(2)}) collective-permute-start(bf16[160,128]{1,0:T(8,128)(2,1)S(1)} %get-tuple-element.50), channel_id=1, source_target_pairs={{0,20},{8,28},{1,21},{9,29},{2,22},{10,30},{3,23},{11,31},{16,4},{... | collective-permute-start | bytes 122888 | tf_op jit(solution)/shard_map/ppermute | solution.py:56
  89.3 5.3 %collective-permute-start.15 = (bf16[160,128]{1,0:T(8,128)(2,1)S(1)}, bf16[160,128]{1,0:T(8,128)(2,1)S(1)}, u32[]{:S(2)}, u32[]{:S(2)}) collective-permute-start(bf16[160,128]{1,0:T(8,128)(2,1)S(1)} %get-tuple-element.50), channel_id=1, source_target_pairs={{0,16},{8,24},{1,17},{9,25},{2,18},{10,26},{3,19},{11,27},{16,0},{... | collective-permute-start | bytes 122888 | tf_op jit(solution)/shard_map/ppermute | solution.py:56
  95.9 25.3 %copy-start.2 = (bf16[256,128]{1,0:T(8,128)(2,1)S(1)}, bf16[256,128]{1,0:T(8,128)(2,1)}, u32[]{:S(2)}) copy-start(bf16[256,128]{1,0:T(8,128)(2,1)} %get-tuple-element.33.refs_6_.select) | copy-start | bytes 196612
  95.9 25.3 %copy-start.3 = (bf16[16,768]{1,0:T(8,128)(2,1)S(1)}, bf16[16,768]{1,0:T(8,128)(2,1)}, u32[]{:S(2)}) copy-start(bf16[16,768]{1,0:T(8,128)(2,1)} %get-tuple-element.58.hidden) | copy-start | bytes 73732
  95.9 2.0 %collective-permute-start.19 = (bf16[4,480,128]{2,1,0:T(8,128)(2,1)S(1)}, bf16[4,480,128]{2,1,0:T(8,128)(2,1)S(1)}, u32[]{:S(2)}, u32[]{:S(2)}) collective-permute-start(bf16[4,480,128]{2,1,0:T(8,128)(2,1)S(1)} %get-tuple-element.53), channel_id=1, source_target_pairs={{0,8},{8,0},{1,9},{9,1},{2,10},{10,2},{3,11},{11,3},{16,24},{24,16... | collective-permute-start | bytes 1474568 | tf_op jit(solution)/shard_map/ppermute | solution.py:56
  98.0 6.2 %collective-permute-start.20 = (bf16[480,128]{1,0:T(8,128)(2,1)S(1)}, bf16[480,128]{1,0:T(8,128)(2,1)S(1)}, u32[]{:S(2)}, u32[]{:S(2)}) collective-permute-start(bf16[480,128]{1,0:T(8,128)(2,1)S(1)} %get-tuple-element.55), channel_id=1, source_target_pairs={{0,1},{8,9},{1,2},{9,10},{2,3},{10,11},{3,0},{11,8},{16,17},{24,25... | collective-permute-start | bytes 368648 | tf_op jit(solution)/shard_map/ppermute | solution.py:56
  99.3 7.7 %collective-permute-start.21 = (bf16[480,128]{1,0:T(8,128)(2,1)S(1)}, bf16[480,128]{1,0:T(8,128)(2,1)S(1)}, u32[]{:S(2)}, u32[]{:S(2)}) collective-permute-start(bf16[480,128]{1,0:T(8,128)(2,1)S(1)} %get-tuple-element.56), channel_id=1, source_target_pairs={{0,2},{8,10},{1,3},{9,11},{2,0},{10,8},{3,1},{11,9},{16,18},{24,26... | collective-permute-start | bytes 368648 | tf_op jit(solution)/shard_map/ppermute | solution.py:56
  100.9 7.6 %collective-permute-start.22 = (bf16[480,128]{1,0:T(8,128)(2,1)S(1)}, bf16[480,128]{1,0:T(8,128)(2,1)S(1)}, u32[]{:S(2)}, u32[]{:S(2)}) collective-permute-start(bf16[480,128]{1,0:T(8,128)(2,1)S(1)} %get-tuple-element.57), channel_id=1, source_target_pairs={{0,3},{8,11},{1,0},{9,8},{2,1},{10,9},{3,2},{11,10},{16,19},{24,27... | collective-permute-start | bytes 368648 | tf_op jit(solution)/shard_map/ppermute | solution.py:56

commit v5 on v4

--- a/solution.py
+++ b/solution.py
@@ -172,10 +172,9 @@
     lengths,
     *refs,
 ):
-    in_hbm_refs = refs[:8]
-    kv_out, hidden_out, payload = refs[8:11]
-    pool, heads_v, stream, gain, router, select, places, scores_v, o_scr, sems = refs[11:]
-    kv_pool, arrived = in_hbm_refs[:2]
+    kv_pool, arrived, queries, ids = refs[:4]
+    kv_out, hidden_out, payload, select = refs[7:11]
+    pool, heads_v, stream, gain, router, places, scores_v, o_scr, sems = refs[11:]
     rows, width = stream.shape
     heads = width // LANES
     pages = table.shape[1]
@@ -186,12 +185,9 @@
         for i, (source, target) in enumerate(
             [
                 (kv_pool.at[kept], pool.at[kept]),
-                (in_hbm_refs[2], heads_v),
-                (in_hbm_refs[3], stream),
-                (in_hbm_refs[4], gain),
-                (in_hbm_refs[5], router),
-                (in_hbm_refs[6], select),
-                (in_hbm_refs[7], places),
+                (refs[4], stream),
+                (refs[5], gain),
+                (refs[6], router),
             ]
         )
     ]
@@ -200,9 +196,9 @@
     for z in range(NZ):
         to, at = OLD_PAGES + z * share, (NZ - 1 - z) * share
         pool[to : to + share] = arrived[at : at + share]
-    for load in loads[:2]:
-        load.wait()
-    store = pltpu.make_async_copy(pool, kv_out, sems.at[7])
+    find_places(ids, queries, select, places, heads_v)
+    loads[0].wait()
+    store = pltpu.make_async_copy(pool, kv_out, sems.at[4])
     store.start()
     scale = float(LANES) ** (-0.5)
     length = jnp.concatenate(
@@ -227,7 +223,7 @@
         weight = jnp.concatenate([weight, weight], axis=0).astype(BF16)
         o_scr[r * 8 : (r + 1) * 8, :] = jnp.dot(weight, values, preferred_element_type=F32)[:8]
     o_scr[...] = o_scr[...] / total
-    for load in loads[2:]:
+    for load in loads[1:]:
         load.wait()
     attended = jnp.concatenate([o_scr[pl.ds(h, rows, stride=8), :] for h in range(heads)], axis=1)
     hidden = (stream[...].astype(F32) + attended).astype(BF16)
@@ -263,7 +259,7 @@
     store.wait()
 
 
-def attend(table, lengths, kv_pool, arrived, heads, stream, gain, router, select, places):
+def attend(table, lengths, kv_pool, arrived, queries, ids, stream, gain, router):
     rows, width = stream.shape
     shape = jax.ShapeDtypeStruct
     return pl.pallas_call(
@@ -272,28 +268,28 @@
             shape(kv_pool.shape, kv_pool.dtype),
             shape((rows, width), BF16),
             shape((NZ, SLAB, LANES), BF16),
+            shape((EXPERTS * SLAB, LANES), BF16),
         ),
-        in_specs=in_smem(2) + in_hbm(1) + in_vmem(1) + in_hbm(6),
-        out_specs=tuple(in_hbm(1) + in_vmem(2)),
+        in_specs=in_smem(2) + in_hbm(1) + in_vmem(3) + in_hbm(3),
+        out_specs=tuple(in_hbm(1) + in_vmem(3)),
         scratch_shapes=[
             pltpu.VMEM(kv_pool.shape, kv_pool.dtype),
-            pltpu.VMEM(heads.shape, F32),
+            pltpu.VMEM((rows * 8, LANES), F32),
             pltpu.VMEM(stream.shape, BF16),
             pltpu.VMEM(gain.shape, BF16),
             pltpu.VMEM(router.shape, BF16),
-            pltpu.VMEM(select.shape, BF16),
-            pltpu.VMEM(places.shape, jnp.int32),
+            pltpu.VMEM((4 * rows, LANES), jnp.int32),
             pltpu.VMEM((rows * 8, table.shape[1] * kv_pool.shape[1]), F32),
             pltpu.VMEM((rows * 8, LANES), F32),
-            pltpu.SemaphoreType.DMA((8,)),
+            pltpu.SemaphoreType.DMA((5,)),
         ],
-        compiler_params=params(56),
+        compiler_params=params(53),
         name="attend",
-    )(table, lengths, kv_pool, arrived, heads, stream, gain, router, select, places)
-
-
-def prepare_kernel(where, w_gate, w_up, w_down, ids, queries, *refs):
-    made, places, blocks, sems = refs[:6], refs[6:9], refs[9:15], refs[15]
+    )(table, lengths, kv_pool, arrived, queries, ids, stream, gain, router)
+
+
+def prepare_kernel(where, w_gate, w_up, w_down, *refs):
+    made, blocks, sems = refs[:6], refs[6:12], refs[12]
     pieces = []
     for n in range(4):
         x = jnp.bitwise_and(where[1] + n, 3)
@@ -321,29 +317,22 @@
                 load.wait()
         stores.append(pltpu.make_async_copy(blocks[n], made[n], sems.at[40 + n]))
         stores[n].start()
-    find_places(ids, queries, *places)
     for store in stores:
         store.wait()
 
 
-def prepare(where, w_gate, w_up, w_down, ids, queries):
-    rows = queries.shape[0]
+def prepare(where, w_gate, w_up, w_down):
     block = (2 * WIDTH, 2 * LANES)
     shape = jax.ShapeDtypeStruct
     return pl.pallas_call(
         prepare_kernel,
-        out_shape=(shape(block, BF16),) * 6
-        + (
-            shape((EXPERTS * SLAB, LANES), BF16),
-            shape((4 * rows, LANES), jnp.int32),
-            shape((rows * 8, LANES), F32),
-        ),
-        in_specs=in_smem(1) + in_hbm(3) + in_vmem(2),
-        out_specs=tuple(in_hbm(6) + in_vmem(3)),
+        out_shape=(shape(block, BF16),) * 6,
+        in_specs=in_smem(1) + in_hbm(3),
+        out_specs=tuple(in_hbm(6)),
         scratch_shapes=[pltpu.VMEM(block, BF16)] * 6 + [pltpu.SemaphoreType.DMA((46,))],
         compiler_params=params(56),
         name="prepare",
-    )(where, w_gate, w_up, w_down, ids, queries)
+    )(where, w_gate, w_up, w_down)
 
 
 def to_rows_kernel(slabs, out):
@@ -569,26 +558,23 @@
     sect = lax.axis_index("sect")
     where = jnp.stack([sect // 4, sect % 4]).astype(jnp.int32)
 
-    *blocks, select, places, heads = prepare(
-        where, w_gate, w_up, w_down, expert_ids.T, queries
-    )
+    blocks = prepare(where, w_gate, w_up, w_down)
     first = [blocks[0]] + [permute(blocks[n], along_x(n)) for n in (1, 2, 3)]
     second = [permute(blocks[4], along_y(1)), permute(blocks[5], along_y(3))]
     outgoing = pack_pages(fresh_owner.T, fresh_kv.reshape(-1, page_len, page_width), n_attn)
     arrived = lax.all_to_all(
         outgoing, "attn", 0, 0, axis_index_groups=PAGE_GROUPS, tiled=True
     )
-    kv_out, hidden, payload = attend(
+    kv_out, hidden, payload, select = attend(
         page_table,
         lengths,
         kv_pool.reshape(pages, page_len, page_width),
         arrived,
-        heads,
+        queries,
+        expert_ids.T,
         stream,
         norm_gain.reshape(1, -1),
         router.T,
-        select,
-        places,
     )
 
     own = gather4(to_rows(exchange_z(payload)), along_y)

time: 123 us -> 122 us (level)
  waiting for transfers between devices: 40.8 us -> 42.7 us
  Pallas kernels: 19 us -> 17.7 us
  transfers between devices with their start and end apart: 24 -> 24, of which waited for: 13 -> 14; matrix products, arithmetic and copies ran while one was open for 1% -> 1% of each run, Pallas kernels for 9% -> 8%
where the time goes in v5:
time: 122 us; the launch traced here: 121 us
  waiting for transfers between devices  42.7 us (35%)
  starting transfers between devices  33.8 us (28%)
  blocking collectives  25.4 us (21%)
  Pallas kernels  17.7 us (15%)
    ppermute x23, waiting for transfers between devices, permute(): return lax.ppermute(value, AXES, perm)  30.5 us
    all_to_all x2, blocking collectives, exchange_z(): lax.all_to_all(slabs, 'attn', 0, 0, axis_index_groups=Z_GROUPS, tiled=True)  25.4 us
    ppermute x23, starting transfers between devices, permute(): return lax.ppermute(value, AXES, perm)  23.4 us
    all_to_all x1, waiting for transfers between devices, on_device(): lax.all_to_all(outgoing, 'attn', 0, 0, axis_index_groups=PAGE_GROUPS, til...  12.2 us
    all_to_all x1, starting transfers between devices, on_device(): lax.all_to_all(outgoing, 'attn', 0, 0, axis_index_groups=PAGE_GROUPS, til...  10.3 us
    pallas_call x1, Pallas kernels, prepare(): pl.pallas_call(prepare_kernel, out_shape=(shape(block, BF16),) * 6, in_sp...  5.22 us
    pallas_call x1, Pallas kernels, attend(): pl.pallas_call(attend_kernel, out_shape=(shape(kv_pool.shape, kv_pool.dty...  4.35 us
    pallas_call x1, Pallas kernels, pack_pages(): pl.pallas_call(pack_pages_kernel, out_shape=jax.ShapeDtypeStruct((n_attn...  2.5 us
  transfers between devices with their start and end apart: 24, of which 14 were waited for; matrix products, arithmetic and copies ran while one was open for 1% of the time, Pallas kernels for 8%

profile of v5, /device:TPU:6, one launch (start us, length us, event | category | flops | bytes accessed | tf_op | source)
XLA Modules:
  0.0 121.1 jit_solution(4596873108302828398)
XLA Ops:
  0.6 2.5 %pack_pages.1 = bf16[128,16,256]{2,1,0:T(8,128)(2,1)} custom-call(s32[1,32]{1,0:T(1,128)} %bitcast.14, bf16[32,16,256]{2,1,0:T(8,128)(2,1)} %bitcast.13), custom_call_target="tpu_custom_call" | custom-call | tf_op jit(solution)/shard_map/pack_pages/pallas_call | solution.py:108
  3.1 10.3 %all-to-all-start = ((bf16[128,16,256]{2,1,0:T(8,128)(2,1)}), bf16[128,16,256]{2,1,0:T(8,128)(2,1)}, u32[]{:S(2)}, u32[]{:S(2)}) async-start(bf16[128,16,256]{2,1,0:T(8,128)(2,1)} %pack_pages.1), calls=%async_computation | async-start | bytes 2097152 | tf_op jit(solution)/shard_map/all_to_all | solution.py:565
  13.5 0.6 pad_add_fusion.where
  14.1 0.0 copy-start.5
  14.1 0.0 copy-start.7
  14.1 0.0 copy-start.8
  14.1 5.2 %prepare.1 = (bf16[1536,256]{1,0:T(8,128)(2,1)}, bf16[1536,256]{1,0:T(8,128)(2,1)}, bf16[1536,256]{1,0:T(8,128)(2,1)}, bf16[1536,256]{1,0:T(8,128)(2,1)}, bf16[1...) custom-call(s32[2]{0:T(128)} %pad_add_fusion.where, bf16[6144,128]{1,0:T(8,128)(2,1)} %w_gate.1, bf16[6144,128]{1,0:T(8,128)(2,1)} %w_up.1, ...), custom_call_target="tpu_custom_call" | custom-call | tf_op jit(solution)/shard_map/prepare/pallas_call | solution.py:327
  19.4 0.6 collective-permute-start.7
  19.9 2.4 %collective-permute-start.8 = (bf16[1536,256]{1,0:T(8,128)(2,1)}, bf16[1536,256]{1,0:T(8,128)(2,1)S(1)}, u32[]{:S(2)}, u32[]{:S(2)}) collective-permute-start(bf16[1536,256]{1,0:T(8,128)(2,1)} %get-tuple-element.33), channel_id=1, source_target_pairs={{0,2},{8,10},{1,3},{9,11},{2,0},{10,8},{3,1},{11,9},{16,18},{24,26... | collective-permute-start | bytes 2359304 | tf_op jit(solution)/shard_map/ppermute | solution.py:56
  22.4 0.0 collective-permute-start.9
  22.4 3.2 %collective-permute-start.11 = (bf16[1536,256]{1,0:T(8,128)(2,1)}, bf16[1536,256]{1,0:T(8,128)(2,1)S(1)}, u32[]{:S(2)}, u32[]{:S(2)}) collective-permute-start(bf16[1536,256]{1,0:T(8,128)(2,1)} %get-tuple-element.46), channel_id=1, source_target_pairs={{0,20},{8,28},{1,21},{9,29},{2,22},{10,30},{3,23},{11,31},{16,4},{... | collective-permute-start | bytes 2359304 | tf_op jit(solution)/shard_map/ppermute | solution.py:56
  25.5 0.0 collective-permute-start.10
  25.5 12.2 %all-to-all-done.refs_1_ = bf16[128,16,256]{2,1,0:T(8,128)(2,1)} async-done(((bf16[128,16,256]{2,1,0:T(8,128)(2,1)}), bf16[128,16,256]{2,1,0:T(8,128)(2,1)}, u32[]{:S(2)}, u32[]{:S(2)}) %all-to-all-start) | async-done | bytes 1048608 | tf_op jit(solution)/shard_map/all_to_all | solution.py:565
  37.8 4.4 %attend.1 = (bf16[320,16,256]{2,1,0:T(8,128)(2,1)}, bf16[16,768]{1,0:T(8,128)(2,1)S(1)}, bf16[8,64,128]{2,1,0:T(8,128)(2,1)S(1)}, bf16[256,128]{1,0:T(8,128)(2,1)S(1)}) custom-call(s32[16,16]{1,0:T(8,128)S(1)} %copy-done.4, s32[1,16]{1,0:T(1,128)S(1)} %copy-done.8, bf16[320,16,256]{2,1,0:T(8,128)(2,1)} %bitcast.12, ...), custom_call_target="tpu_custom_call" | custom-call | tf_op jit(solution)/shard_map/attend/pallas_call | solution.py:265
  42.2 13.1 %all_to_all.15.slabs = bf16[8,64,128]{2,1,0:T(8,128)(2,1)S(1)} all-to-all(bf16[8,64,128]{2,1,0:T(8,128)(2,1)S(1)} %get-tuple-element.30), channel_id=1, replica_groups={{224,192,160,128,96,64,32,0},{232,200,168,136,104,72,40,8},{240,208,176..., dimensions={0} | all-to-all | bytes 262144 | tf_op jit(solution)/shard_map/all_to_all | solution.py:538
  55.3 0.3 to_rows.1.refs_0_
  55.6 0.0 collective-permute-done.7.refs_9_
  55.6 3.4 %collective-permute-start.2 = (bf16[496,128]{1,0:T(8,128)(2,1)S(1)}, bf16[496,128]{1,0:T(8,128)(2,1)S(1)}, u32[]{:S(2)}, u32[]{:S(2)}) collective-permute-start(bf16[496,128]{1,0:T(8,128)(2,1)S(1)} %to_rows.1.refs_0_), channel_id=1, source_target_pairs={{0,20},{8,28},{1,21},{9,29},{2,22},{10,30},{3,23},{11,31},{16,4},{... | collective-permute-start | bytes 380936 | tf_op jit(solution)/shard_map/ppermute | solution.py:56
  59.0 0.0 collective-permute-done.8.refs_10_
  59.0 0.4 collective-permute-start.1
  59.4 0.0 collective-permute-done.9.refs_11_
  59.4 0.6 collective-permute-start
  60.0 0.0 collective-permute-done.11.refs_13_.refs_7_
  60.0 0.0 collective-permute-start.3
  60.0 3.6 %collective-permute-done.2.refs_3_ = bf16[496,128]{1,0:T(8,128)(2,1)S(1)} collective-permute-done((bf16[496,128]{1,0:T(8,128)(2,1)S(1)}, bf16[496,128]{1,0:T(8,128)(2,1)S(1)}, u32[]{:S(2)}, u32[]{:S(2)}) %collective-permute-start.2) | collective-permute-done | bytes 127008 | tf_op jit(solution)/shard_map/ppermute | solution.py:56
  63.6 0.0 collective-permute-start.6
  63.6 2.3 %collective-permute-done.1.refs_2_ = bf16[496,128]{1,0:T(8,128)(2,1)S(1)} collective-permute-done((bf16[496,128]{1,0:T(8,128)(2,1)S(1)}, bf16[496,128]{1,0:T(8,128)(2,1)S(1)}, u32[]{:S(2)}, u32[]{:S(2)}) %collective-permute-start.1) | collective-permute-done | bytes 127008 | tf_op jit(solution)/shard_map/ppermute | solution.py:56
  65.9 0.0 collective-permute-start.5
  65.9 0.0 collective-permute-done.refs_1_
  65.9 0.5 collective-permute-start.4
  66.4 0.0 collective-permute-done.10.refs_12_.refs_5_
  66.4 0.0 collective-permute-done.3.refs_4_
  66.4 0.0 collective-permute-done.6.refs_7_
  66.4 0.8 collective-permute-done.5.refs_6_
  67.3 0.2 collective-permute-done.4.refs_5_
  67.4 2.5 %gate_up.1 = (f32[352,256]{1,0:T(8,128)S(1)}, bf16[352,256]{1,0:T(8,128)(2,1)S(1)}, bf16[352,256]{1,0:T(8,128)(2,1)S(1)}, bf16[352,256]{1,0:T(8,128)(2,1)S(1)}) custom-call(s32[2]{0:T(128)S(1)} %copy-done.6, bf16[496,128]{1,0:T(8,128)(2,1)S(1)} %to_rows.1.refs_0_, bf16[496,128]{1,0:T(8,128)(2,1)S(1)} %collective-permute-done.refs_1_, ...), custom_call_target="tpu_custom_call" | custom-call | tf_op jit(solution)/shard_map/gate_up/pallas_call | solution.py:394
  69.9 1.8 %collective-permute-start.18 = (bf16[1536,256]{1,0:T(8,128)(2,1)S(1)}, bf16[1536,256]{1,0:T(8,128)(2,1)S(1)}, u32[]{:S(2)}, u32[]{:S(2)}) collective-permute-start(bf16[1536,256]{1,0:T(8,128)(2,1)S(1)} %copy-done.10), channel_id=1, source_target_pairs={{0,4},{8,12},{1,5},{9,13},{2,6},{10,14},{3,7},{11,15},{16,20},{24,... | collective-permute-start | bytes 2359304 | tf_op jit(solution)/shard_map/ppermute | solution.py:56
  71.7 0.7 collective-permute-start.12
  72.4 2.7 %collective-permute-start.13 = (bf16[352,256]{1,0:T(8,128)(2,1)S(1)}, bf16[352,256]{1,0:T(8,128)(2,1)S(1)}, u32[]{:S(2)}, u32[]{:S(2)}) collective-permute-start(bf16[352,256]{1,0:T(8,128)(2,1)S(1)} %get-tuple-element.42), channel_id=1, source_target_pairs={{0,2},{8,10},{1,3},{9,11},{2,0},{10,8},{3,1},{11,9},{16,18},{24,26... | collective-permute-start | bytes 540680 | tf_op jit(solution)/shard_map/ppermute | solution.py:56
  75.1 0.5 collective-permute-start.14
  75.6 4.4 %collective-permute-done.12.refs_1_ = bf16[352,256]{1,0:T(8,128)(2,1)S(1)} collective-permute-done((bf16[352,256]{1,0:T(8,128)(2,1)S(1)}, bf16[352,256]{1,0:T(8,128)(2,1)S(1)}, u32[]{:S(2)}, u32[]{:S(2)}) %collective-permute-start.12) | collective-permute-done | bytes 180256 | tf_op jit(solution)/shard_map/ppermute | solution.py:56
  80.0 3.4 %collective-permute-done.13.refs_2_ = bf16[352,256]{1,0:T(8,128)(2,1)S(1)} collective-permute-done((bf16[352,256]{1,0:T(8,128)(2,1)S(1)}, bf16[352,256]{1,0:T(8,128)(2,1)S(1)}, u32[]{:S(2)}, u32[]{:S(2)}) %collective-permute-start.13) | collective-permute-done | bytes 180256 | tf_op jit(solution)/shard_map/ppermute | solution.py:56
  83.4 0.4 collective-permute-done.14.refs_3_
  83.7 0.3 activate.1
  84.0 2.1 %collective-permute-start.16 = (bf16[160,128]{1,0:T(8,128)(2,1)S(1)}, bf16[160,128]{1,0:T(8,128)(2,1)S(1)}, u32[]{:S(2)}, u32[]{:S(2)}) collective-permute-start(bf16[160,128]{1,0:T(8,128)(2,1)S(1)} %get-tuple-element.44.refs_0_), channel_id=1, source_target_pairs={{0,4},{8,12},{1,5},{9,13},{2,6},{10,14},{3,7},{11,15},{16,20},{24,... | collective-permute-start | bytes 122888 | tf_op jit(solution)/shard_map/ppermute | solution.py:56
  86.2 1.6 %collective-permute-start.17 = (bf16[160,128]{1,0:T(8,128)(2,1)S(1)}, bf16[160,128]{1,0:T(8,128)(2,1)S(1)}, u32[]{:S(2)}, u32[]{:S(2)}) collective-permute-start(bf16[160,128]{1,0:T(8,128)(2,1)S(1)} %get-tuple-element.45), channel_id=1, source_target_pairs={{0,20},{8,28},{1,21},{9,29},{2,22},{10,30},{3,23},{11,31},{16,4},{... | collective-permute-start | bytes 122888 | tf_op jit(solution)/shard_map/ppermute | solution.py:56
  87.7 0.0 collective-permute-start.15
  87.7 5.0 %collective-permute-done.16.refs_2_ = bf16[160,128]{1,0:T(8,128)(2,1)S(1)} collective-permute-done((bf16[160,128]{1,0:T(8,128)(2,1)S(1)}, bf16[160,128]{1,0:T(8,128)(2,1)S(1)}, u32[]{:S(2)}, u32[]{:S(2)}) %collective-permute-start.16) | collective-permute-done | bytes 40992 | tf_op jit(solution)/shard_map/ppermute | solution.py:56
  92.7 0.4 collective-permute-done.17.refs_3_
  93.1 0.0 collective-permute-done.15.refs_1_
  93.1 0.0 collective-permute-done.18.refs_6_
  93.1 1.2 %down.1 = (bf16[4,480,128]{2,1,0:T(8,128)(2,1)S(1)}, bf16[4,480,128]{2,1,0:T(8,128)(2,1)S(1)}) custom-call(s32[2]{0:T(128)S(1)} %copy-done.6, bf16[160,128]{1,0:T(8,128)(2,1)S(1)} %get-tuple-element.44.refs_0_, bf16[160,128]{1,0:T(8,128)(2,1)S(1)} %collective-permute-done.15.refs_1_, bf16[160,128]{1,0:T(8,128)(2,1)S(1)} %collective-permute-done.16.refs_2_, ...), custom_call_target="tpu_custom_call" | custom-call | tf_op jit(solution)/shard_map/down/pallas_call | solution.py:462
  94.3 0.1 collective-permute-start.19
  94.4 1.9 %collective-permute-done.19.other = bf16[4,480,128]{2,1,0:T(8,128)(2,1)S(1)} collective-permute-done((bf16[4,480,128]{2,1,0:T(8,128)(2,1)S(1)}, bf16[4,480,128]{2,1,0:T(8,128)(2,1)S(1)}, u32[]{:S(2)}, u32[]{:S(2)}) %collective-permute-start.19) | collective-permute-done | bytes 491552 | tf_op jit(solution)/shard_map/ppermute | solution.py:56
  96.3 0.1 add_cores.1
  96.4 2.0 %collective-permute-start.20 = (bf16[480,128]{1,0:T(8,128)(2,1)S(1)}, bf16[480,128]{1,0:T(8,128)(2,1)S(1)}, u32[]{:S(2)}, u32[]{:S(2)}) collective-permute-start(bf16[480,128]{1,0:T(8,128)(2,1)S(1)} %get-tuple-element.50), channel_id=1, source_target_pairs={{0,1},{8,9},{1,2},{9,10},{2,3},{10,11},{3,0},{11,8},{16,17},{24,25... | collective-permute-start | bytes 368648 | tf_op jit(solution)/shard_map/ppermute | solution.py:56
  98.4 1.0 collective-permute-start.21
  99.4 0.0 collective-permute-start.22
  99.4 4.6 %collective-permute-done.20.refs_1_ = bf16[480,128]{1,0:T(8,128)(2,1)S(1)} collective-permute-done((bf16[480,128]{1,0:T(8,128)(2,1)S(1)}, bf16[480,128]{1,0:T(8,128)(2,1)S(1)}, u32[]{:S(2)}, u32[]{:S(2)}) %collective-permute-start.20) | collective-permute-done | bytes 122912 | tf_op jit(solution)/shard_map/ppermute | solution.py:56
  103.9 2.2 %collective-permute-done.21.refs_2_ = bf16[480,128]{1,0:T(8,128)(2,1)S(1)} collective-permute-done((bf16[480,128]{1,0:T(8,128)(2,1)S(1)}, bf16[480,128]{1,0:T(8,128)(2,1)S(1)}, u32[]{:S(2)}, u32[]{:S(2)}) %collective-permute-start.21) | collective-permute-done | bytes 122912 | tf_op jit(solution)/shard_map/ppermute | solution.py:56
  106.1 1.5 %collective-permute-done.22.refs_3_ = bf16[480,128]{1,0:T(8,128)(2,1)S(1)} collective-permute-done((bf16[480,128]{1,0:T(8,128)(2,1)S(1)}, bf16[480,128]{1,0:T(8,128)(2,1)S(1)}, u32[]{:S(2)}, u32[]{:S(2)}) %collective-permute-start.22) | collective-permute-done | bytes 122912 | tf_op jit(solution)/shard_map/ppermute | solution.py:56
  107.6 0.3 to_slabs.1
  107.9 12.3 %all_to_all.16.slabs = bf16[8,64,128]{2,1,0:T(8,128)(2,1)S(1)} all-to-all(bf16[8,64,128]{2,1,0:T(8,128)(2,1)S(1)} %to_slabs.1), channel_id=1, replica_groups={{224,192,160,128,96,64,32,0},{232,200,168,136,104,72,40,8},{240,208,176..., dimensions={0} | all-to-all | bytes 262144 | tf_op jit(solution)/shard_map/all_to_all | solution.py:538
  120.2 0.8 combine.1
  (20 shorter events, 0.0 us)
Async XLA Ops:
  3.1 34.6 %all-to-all-start = ((bf16[128,16,256]{2,1,0:T(8,128)(2,1)}), bf16[128,16,256]{2,1,0:T(8,128)(2,1)}, u32[]{:S(2)}, u32[]{:S(2)}) async-start(bf16[128,16,256]{2,1,0:T(8,128)(2,1)} %pack_pages.1), calls=%async_computation | async-start | bytes 2097152 | tf_op jit(solution)/shard_map/all_to_all | solution.py:565
  14.1 11.4 %copy-start.9 = (bf16[768]{0:T(1024)(128)(2,1)S(1)}, bf16[768]{0:T(1024)(128)(2,1)}, u32[]{:S(2)}) copy-start(bf16[768]{0:T(1024)(128)(2,1)} %param.20) | copy-start | bytes 4612
  14.1 23.7 %copy-start.2 = (bf16[16,768]{1,0:T(8,128)(2,1)S(1)}, bf16[16,768]{1,0:T(8,128)(2,1)}, u32[]{:S(2)}) copy-start(bf16[16,768]{1,0:T(8,128)(2,1)} %refs_2_.1) | copy-start | bytes 73732
  14.1 23.7 %copy-start.3 = (bf16[16,768]{1,0:T(8,128)(2,1)S(1)}, bf16[16,768]{1,0:T(8,128)(2,1)}, u32[]{:S(2)}) copy-start(bf16[16,768]{1,0:T(8,128)(2,1)} %refs_4_.1) | copy-start | bytes 73732
  14.1 23.7 %copy-start.4 = (s32[16,16]{1,0:T(8,128)S(1)}, s32[16,16]{1,0:T(8,128)}, u32[]{:S(2)}) copy-start(s32[16,16]{1,0:T(8,128)} %table.1) | copy-start | bytes 3076
  14.1 23.7 %copy-start.5 = (bf16[768,4]{0,1:T(4,128)(2,1)S(1)}, bf16[768,4]{0,1:T(4,128)(2,1)}, u32[]{:S(2)}) copy-start(bf16[768,4]{0,1:T(4,128)(2,1)} %param.21) | copy-start | bytes 18436
  14.1 23.7 %copy-start.7 = (s32[16,2]{0,1:T(2,128)S(1)}, s32[16,2]{0,1:T(2,128)}, u32[]{:S(2)}) copy-start(s32[16,2]{0,1:T(2,128)} %param.22) | copy-start | bytes 388
  14.1 23.6 %copy-start.8 = (s32[1,16]{1,0:T(1,128)S(1)}, s32[1,16]{1,0:T(1,128)}, u32[]{:S(2)}) copy-start(s32[1,16]{1,0:T(1,128)} %lengths.1) | copy-start | bytes 196
  19.4 36.2 %collective-permute-start.7 = (bf16[1536,256]{1,0:T(8,128)(2,1)}, bf16[1536,256]{1,0:T(8,128)(2,1)S(1)}, u32[]{:S(2)}, u32[]{:S(2)}) collective-permute-start(bf16[1536,256]{1,0:T(8,128)(2,1)} %get-tuple-element.32), channel_id=1, source_target_pairs={{0,1},{8,9},{1,2},{9,10},{2,3},{10,11},{3,0},{11,8},{16,17},{24,25... | collective-permute-start | bytes 2359304 | tf_op jit(solution)/shard_map/ppermute | solution.py:56
  19.9 39.1 %collective-permute-start.8 = (bf16[1536,256]{1,0:T(8,128)(2,1)}, bf16[1536,256]{1,0:T(8,128)(2,1)S(1)}, u32[]{:S(2)}, u32[]{:S(2)}) collective-permute-start(bf16[1536,256]{1,0:T(8,128)(2,1)} %get-tuple-element.33), channel_id=1, source_target_pairs={{0,2},{8,10},{1,3},{9,11},{2,0},{10,8},{3,1},{11,9},{16,18},{24,26... | collective-permute-start | bytes 2359304 | tf_op jit(solution)/shard_map/ppermute | solution.py:56
  22.4 37.0 %collective-permute-start.9 = (bf16[1536,256]{1,0:T(8,128)(2,1)}, bf16[1536,256]{1,0:T(8,128)(2,1)}, u32[]{:S(2)}, u32[]{:S(2)}) collective-permute-start(bf16[1536,256]{1,0:T(8,128)(2,1)} %get-tuple-element.34), channel_id=1, source_target_pairs={{0,3},{8,11},{1,0},{9,8},{2,1},{10,9},{3,2},{11,10},{16,19},{24,27... | collective-permute-start | bytes 2359304 | tf_op jit(solution)/shard_map/ppermute | solution.py:56
  22.4 37.6 %collective-permute-start.11 = (bf16[1536,256]{1,0:T(8,128)(2,1)}, bf16[1536,256]{1,0:T(8,128)(2,1)S(1)}, u32[]{:S(2)}, u32[]{:S(2)}) collective-permute-start(bf16[1536,256]{1,0:T(8,128)(2,1)} %get-tuple-element.46), channel_id=1, source_target_pairs={{0,20},{8,28},{1,21},{9,29},{2,22},{10,30},{3,23},{11,31},{16,4},{... | collective-permute-start | bytes 2359304 | tf_op jit(solution)/shard_map/ppermute | solution.py:56
  25.5 40.9 %collective-permute-start.10 = (bf16[1536,256]{1,0:T(8,128)(2,1)}, bf16[1536,256]{1,0:T(8,128)(2,1)S(1)}, u32[]{:S(2)}, u32[]{:S(2)}) collective-permute-start(bf16[1536,256]{1,0:T(8,128)(2,1)} %get-tuple-element.35.refs_4_), channel_id=1, source_target_pairs={{0,16},{8,24},{1,17},{9,25},{2,18},{10,26},{3,19},{11,27},{16,0},{... | collective-permute-start | bytes 2359304 | tf_op jit(solution)/shard_map/ppermute | solution.py:56
  37.8 29.6 %copy-start.1 = (bf16[1536,256]{1,0:T(8,128)(2,1)S(1)}, bf16[1536,256]{1,0:T(8,128)(2,1)}, u32[]{:S(2)}) copy-start(bf16[1536,256]{1,0:T(8,128)(2,1)} %get-tuple-element.31.refs_8_) | copy-start | bytes 2359300
  37.8 29.6 %copy-start.6 = (s32[2]{0:T(128)S(1)}, s32[2]{0:T(128)}, u32[]{:S(2)}) copy-start(s32[2]{0:T(128)} %pad_add_fusion.where) | copy-start | bytes 28
  55.6 8.0 %collective-permute-start.2 = (bf16[496,128]{1,0:T(8,128)(2,1)S(1)}, bf16[496,128]{1,0:T(8,128)(2,1)S(1)}, u32[]{:S(2)}, u32[]{:S(2)}) collective-permute-start(bf16[496,128]{1,0:T(8,128)(2,1)S(1)} %to_rows.1.refs_0_), channel_id=1, source_target_pairs={{0,20},{8,28},{1,21},{9,29},{2,22},{10,30},{3,23},{11,31},{16,4},{... | collective-permute-start | bytes 380936 | tf_op jit(solution)/shard_map/ppermute | solution.py:56
  59.0 6.9 %collective-permute-start.1 = (bf16[496,128]{1,0:T(8,128)(2,1)S(1)}, bf16[496,128]{1,0:T(8,128)(2,1)S(1)}, u32[]{:S(2)}, u32[]{:S(2)}) collective-permute-start(bf16[496,128]{1,0:T(8,128)(2,1)S(1)} %to_rows.1.refs_0_), channel_id=1, source_target_pairs={{0,4},{8,12},{1,5},{9,13},{2,6},{10,14},{3,7},{11,15},{16,20},{24,... | collective-permute-start | bytes 380936 | tf_op jit(solution)/shard_map/ppermute | solution.py:56
  59.4 6.5 %collective-permute-start = (bf16[496,128]{1,0:T(8,128)(2,1)S(1)}, bf16[496,128]{1,0:T(8,128)(2,1)S(1)}, u32[]{:S(2)}, u32[]{:S(2)}) collective-permute-start(bf16[496,128]{1,0:T(8,128)(2,1)S(1)} %to_rows.1.refs_0_), channel_id=1, source_target_pairs={{0,16},{8,24},{1,17},{9,25},{2,18},{10,26},{3,19},{11,27},{16,0},{... | collective-permute-start | bytes 380936 | tf_op jit(solution)/shard_map/ppermute | solution.py:56
  60.0 6.5 %collective-permute-start.3 = (bf16[496,128]{1,0:T(8,128)(2,1)S(1)}, bf16[496,128]{1,0:T(8,128)(2,1)S(1)}, u32[]{:S(2)}, u32[]{:S(2)}) collective-permute-start(bf16[496,128]{1,0:T(8,128)(2,1)S(1)} %to_rows.1.refs_0_), channel_id=1, source_target_pairs={{0,8},{8,0},{1,9},{9,1},{2,10},{10,2},{3,11},{11,3},{16,24},{24,16... | collective-permute-start | bytes 380936 | tf_op jit(solution)/shard_map/ppermute | solution.py:56
  63.6 2.9 %collective-permute-start.6 = (bf16[496,128]{1,0:T(8,128)(2,1)S(1)}, bf16[496,128]{1,0:T(8,128)(2,1)S(1)}, u32[]{:S(2)}, u32[]{:S(2)}) collective-permute-start(bf16[496,128]{1,0:T(8,128)(2,1)S(1)} %collective-permute-done.2.refs_3_), channel_id=1, source_target_pairs={{0,8},{8,0},{1,9},{9,1},{2,10},{10,2},{3,11},{11,3},{16,24},{24,16... | collective-permute-start | bytes 380936 | tf_op jit(solution)/shard_map/ppermute | solution.py:56
  65.9 1.3 %collective-permute-start.5 = (bf16[496,128]{1,0:T(8,128)(2,1)S(1)}, bf16[496,128]{1,0:T(8,128)(2,1)S(1)}, u32[]{:S(2)}, u32[]{:S(2)}) collective-permute-start(bf16[496,128]{1,0:T(8,128)(2,1)S(1)} %collective-permute-done.1.refs_2_), channel_id=1, source_target_pairs={{0,8},{8,0},{1,9},{9,1},{2,10},{10,2},{3,11},{11,3},{16,24},{24,16... | collective-permute-start | bytes 380936 | tf_op jit(solution)/shard_map/ppermute | solution.py:56
  65.9 1.5 %collective-permute-start.4 = (bf16[496,128]{1,0:T(8,128)(2,1)S(1)}, bf16[496,128]{1,0:T(8,128)(2,1)S(1)}, u32[]{:S(2)}, u32[]{:S(2)}) collective-permute-start(bf16[496,128]{1,0:T(8,128)(2,1)S(1)} %collective-permute-done.refs_1_), channel_id=1, source_target_pairs={{0,8},{8,0},{1,9},{9,1},{2,10},{10,2},{3,11},{11,3},{16,24},{24,16... | collective-permute-start | bytes 380936 | tf_op jit(solution)/shard_map/ppermute | solution.py:56
  67.4 2.5 %copy-start.10 = (bf16[1536,256]{1,0:T(8,128)(2,1)S(1)}, bf16[1536,256]{1,0:T(8,128)(2,1)}, u32[]{:S(2)}) copy-start(bf16[1536,256]{1,0:T(8,128)(2,1)} %get-tuple-element.46) | copy-start | bytes 2359300
  67.4 25.6 %copy-start = (bf16[1536,256]{1,0:T(8,128)(2,1)S(1)}, bf16[1536,256]{1,0:T(8,128)(2,1)}, u32[]{:S(2)}) copy-start(bf16[1536,256]{1,0:T(8,128)(2,1)} %get-tuple-element.35.refs_4_) | copy-start | bytes 2359300
  69.9 23.1 %collective-permute-start.18 = (bf16[1536,256]{1,0:T(8,128)(2,1)S(1)}, bf16[1536,256]{1,0:T(8,128)(2,1)S(1)}, u32[]{:S(2)}, u32[]{:S(2)}) collective-permute-start(bf16[1536,256]{1,0:T(8,128)(2,1)S(1)} %copy-done.10), channel_id=1, source_target_pairs={{0,4},{8,12},{1,5},{9,13},{2,6},{10,14},{3,7},{11,15},{16,20},{24,... | collective-permute-start | bytes 2359304 | tf_op jit(solution)/shard_map/ppermute | solution.py:56
  71.7 8.3 %collective-permute-start.12 = (bf16[352,256]{1,0:T(8,128)(2,1)S(1)}, bf16[352,256]{1,0:T(8,128)(2,1)S(1)}, u32[]{:S(2)}, u32[]{:S(2)}) collective-permute-start(bf16[352,256]{1,0:T(8,128)(2,1)S(1)} %get-tuple-element.41), channel_id=1, source_target_pairs={{0,3},{8,11},{1,0},{9,8},{2,1},{10,9},{3,2},{11,10},{16,19},{24,27... | collective-permute-start | bytes 540680 | tf_op jit(solution)/shard_map/ppermute | solution.py:56
  72.4 11.0 %collective-permute-start.13 = (bf16[352,256]{1,0:T(8,128)(2,1)S(1)}, bf16[352,256]{1,0:T(8,128)(2,1)S(1)}, u32[]{:S(2)}, u32[]{:S(2)}) collective-permute-start(bf16[352,256]{1,0:T(8,128)(2,1)S(1)} %get-tuple-element.42), channel_id=1, source_target_pairs={{0,2},{8,10},{1,3},{9,11},{2,0},{10,8},{3,1},{11,9},{16,18},{24,26... | collective-permute-start | bytes 540680 | tf_op jit(solution)/shard_map/ppermute | solution.py:56
  75.1 8.6 %collective-permute-start.14 = (bf16[352,256]{1,0:T(8,128)(2,1)S(1)}, bf16[352,256]{1,0:T(8,128)(2,1)S(1)}, u32[]{:S(2)}, u32[]{:S(2)}) collective-permute-start(bf16[352,256]{1,0:T(8,128)(2,1)S(1)} %get-tuple-element.43), channel_id=1, source_target_pairs={{0,1},{8,9},{1,2},{9,10},{2,3},{10,11},{3,0},{11,8},{16,17},{24,25... | collective-permute-start | bytes 540680 | tf_op jit(solution)/shard_map/ppermute | solution.py:56
  84.0 8.6 %collective-permute-start.16 = (bf16[160,128]{1,0:T(8,128)(2,1)S(1)}, bf16[160,128]{1,0:T(8,128)(2,1)S(1)}, u32[]{:S(2)}, u32[]{:S(2)}) collective-permute-start(bf16[160,128]{1,0:T(8,128)(2,1)S(1)} %get-tuple-element.44.refs_0_), channel_id=1, source_target_pairs={{0,4},{8,12},{1,5},{9,13},{2,6},{10,14},{3,7},{11,15},{16,20},{24,... | collective-permute-start | bytes 122888 | tf_op jit(solution)/shard_map/ppermute | solution.py:56
  86.2 6.9 %collective-permute-start.17 = (bf16[160,128]{1,0:T(8,128)(2,1)S(1)}, bf16[160,128]{1,0:T(8,128)(2,1)S(1)}, u32[]{:S(2)}, u32[]{:S(2)}) collective-permute-start(bf16[160,128]{1,0:T(8,128)(2,1)S(1)} %get-tuple-element.45), channel_id=1, source_target_pairs={{0,20},{8,28},{1,21},{9,29},{2,22},{10,30},{3,23},{11,31},{16,4},{... | collective-permute-start | bytes 122888 | tf_op jit(solution)/shard_map/ppermute | solution.py:56
  87.7 5.3 %collective-permute-start.15 = (bf16[160,128]{1,0:T(8,128)(2,1)S(1)}, bf16[160,128]{1,0:T(8,128)(2,1)S(1)}, u32[]{:S(2)}, u32[]{:S(2)}) collective-permute-start(bf16[160,128]{1,0:T(8,128)(2,1)S(1)} %get-tuple-element.45), channel_id=1, source_target_pairs={{0,16},{8,24},{1,17},{9,25},{2,18},{10,26},{3,19},{11,27},{16,0},{... | collective-permute-start | bytes 122888 | tf_op jit(solution)/shard_map/ppermute | solution.py:56
  94.3 2.0 %collective-permute-start.19 = (bf16[4,480,128]{2,1,0:T(8,128)(2,1)S(1)}, bf16[4,480,128]{2,1,0:T(8,128)(2,1)S(1)}, u32[]{:S(2)}, u32[]{:S(2)}) collective-permute-start(bf16[4,480,128]{2,1,0:T(8,128)(2,1)S(1)} %get-tuple-element.48), channel_id=1, source_target_pairs={{0,8},{8,0},{1,9},{9,1},{2,10},{10,2},{3,11},{11,3},{16,24},{24,16... | collective-permute-start | bytes 1474568 | tf_op jit(solution)/shard_map/ppermute | solution.py:56
  96.4 7.5 %collective-permute-start.20 = (bf16[480,128]{1,0:T(8,128)(2,1)S(1)}, bf16[480,128]{1,0:T(8,128)(2,1)S(1)}, u32[]{:S(2)}, u32[]{:S(2)}) collective-permute-start(bf16[480,128]{1,0:T(8,128)(2,1)S(1)} %get-tuple-element.50), channel_id=1, source_target_pairs={{0,1},{8,9},{1,2},{9,10},{2,3},{10,11},{3,0},{11,8},{16,17},{24,25... | collective-permute-start | bytes 368648 | tf_op jit(solution)/shard_map/ppermute | solution.py:56
  98.4 7.7 %collective-permute-start.21 = (bf16[480,128]{1,0:T(8,128)(2,1)S(1)}, bf16[480,128]{1,0:T(8,128)(2,1)S(1)}, u32[]{:S(2)}, u32[]{:S(2)}) collective-permute-start(bf16[480,128]{1,0:T(8,128)(2,1)S(1)} %get-tuple-element.51), channel_id=1, source_target_pairs={{0,2},{8,10},{1,3},{9,11},{2,0},{10,8},{3,1},{11,9},{16,18},{24,26... | collective-permute-start | bytes 368648 | tf_op jit(solution)/shard_map/ppermute | solution.py:56
  99.4 8.2 %collective-permute-start.22 = (bf16[480,128]{1,0:T(8,128)(2,1)S(1)}, bf16[480,128]{1,0:T(8,128)(2,1)S(1)}, u32[]{:S(2)}, u32[]{:S(2)}) collective-permute-start(bf16[480,128]{1,0:T(8,128)(2,1)S(1)} %get-tuple-element.52), channel_id=1, source_target_pairs={{0,3},{8,11},{1,0},{9,8},{2,1},{10,9},{3,2},{11,10},{16,19},{24,27... | collective-permute-start | bytes 368648 | tf_op jit(solution)/shard_map/ppermute | solution.py:56
